TPU v7x, 32 devices: a whole 2x2x4 slice. The times are simulated.
32 devices in a mesh: dp: 4 (over x, core), mp: 8 (over z, y).
Axes of the slice: x: 2, y: 2, z: 4, core: 2. Of those that a mesh axis runs over, the one named last changes fastest.
Arguments:
- tokens: float32 [24576, 1024], P(('dp', 'mp')), may hold values from -12 to 12
- cotangent: float32 [24576, 1024], P(('dp', 'mp')), may hold values from -6 to 6
- group_items: int32 [4], P('dp'), may hold values from 1 to 3, as said below
- dataset_ids: int32 [12], P('dp'), may hold values from 0 to 4
- lead_hours: int32 [12], P('dp'), may hold values from 6 to 168
- set_weights: float32 [5], replicated, may hold values from 0.5 to 2
- lead_weight: float32 [1024], replicated, may hold values from -1.5 to 1.5
- lead_shift: float32 [1024], replicated, may hold values from -1 to 1
- norm_one_gain: float32 [1024], replicated, may hold values from 0.25 to 1.75
- norm_one_shift: float32 [1024], replicated, may hold values from -0.9 to 0.9
- heads_weight: bfloat16 [1024, 3072], P(None, 'mp'), may hold values from -0.25 to 0.25
- heads_bias: float32 [2048], P('mp'), may hold values from -0.9 to 0.9
- merge_weight: bfloat16 [1024, 1024], P('mp'), may hold values from -0.75 to 0.75
- merge_bias: float32 [1024], replicated, may hold values from -1.2 to 1.2
- norm_two_gain: float32 [1024], replicated, may hold values from 0.25 to 1.75
- norm_two_shift: float32 [1024], replicated, may hold values from -2 to 2
- widen_weight: bfloat16 [1024, 4096], P(None, 'mp'), may hold values from -0.1875 to 0.1875
- widen_bias: float32 [4096], P('mp'), may hold values from -3 to 3
- narrow_weight: bfloat16 [4096, 1024], P('mp'), may hold values from -0.1875 to 0.1875
- narrow_bias: float32 [1024], replicated, may hold values from -3 to 3
Outputs:
- activations: float32 [24576, 1024], P(('dp', 'mp'))
- input_grad: float32 [24576, 1024], P(('dp', 'mp'))
- lead_weight_grad: float32 [1024], replicated
- lead_shift_grad: float32 [1024], replicated
- norm_one_gain_grad: float32 [1024], replicated
- norm_one_shift_grad: float32 [1024], replicated
- heads_weight_grad: float32 [1024, 3072], P(None, 'mp')
- heads_bias_grad: float32 [2048], P('mp')
- merge_weight_grad: float32 [1024, 1024], P('mp')
- merge_bias_grad: float32 [1024], replicated
- norm_two_gain_grad: float32 [1024], replicated
- norm_two_shift_grad: float32 [1024], replicated
- widen_weight_grad: float32 [1024, 4096], P(None, 'mp')
- widen_bias_grad: float32 [4096], P('mp')
- narrow_weight_grad: float32 [4096, 1024], P('mp')
- narrow_bias_grad: float32 [1024], replicated
Inputs may be any that keep to these rules, and one draw needn't show every extreme that they name: `group_items`: live items of each group; in every draw some group holds 3 items and some group exactly one.
All inputs are finite; a program needn't handle non-finite values.
Results may differ from a plain program's by a relative error of at most 0.017.
The roundings to bfloat16 on the way count: a program that leaves them out, or rounds other values in their place, can miss the bound.
Values may be sent and summed in bfloat16 or wider, within the bound.
No kernel may reach another device: no remote copies, remote signals or barrier semaphores. Data moves between devices by JAX's collectives and lax.ppermute only.
A program may use at most 256 MiB of HBM per device.

v0:
```python
import jax
import jax.numpy as jnp
from jax import lax
from jax.sharding import PartitionSpec as P

HEAD_DIM = 64


EPSILON = 1e-05


def layer_norm(value, gain, shift):
    mean = jnp.mean(value, -1, keepdims=True)
    centred = value - mean
    variance = jnp.mean(centred * centred, -1, keepdims=True)
    return centred * lax.rsqrt(variance + EPSILON) * gain + shift


def exact_gelu(value):
    return jax.nn.gelu(value, approximate=False)


def dot_last(left, right):
    return lax.dot_general(
        left, right, (((1,), (1,)), ((), ())), preferred_element_type=jnp.float32
    )


def dot_first(left, right):
    return lax.dot_general(
        left, right, (((0,), (0,)), ((), ())), preferred_element_type=jnp.float32
    )


def attend_item(packed):
    length, heads_here = (packed.shape[0], packed.shape[1])
    block_rows = min(512, length)
    factor = HEAD_DIM ** (-0.5)
    queries = packed[:, :, 0]
    key_rows = packed[:, :, 1]
    value_rows = packed[:, :, 2]
    query_blocks = queries.reshape(length // block_rows, block_rows, heads_here, HEAD_DIM)

    def one_block(query_block):
        scores = factor * jnp.einsum(
            "qhd,khd->hqk", query_block, key_rows, preferred_element_type=jnp.float32
        )
        row_max = jnp.max(scores, -1, keepdims=True)
        total_log = row_max + jnp.log(jnp.sum(jnp.exp(scores - row_max), -1, keepdims=True))
        attn_probs = jnp.exp(scores - total_log).astype(jnp.bfloat16)
        context = jnp.einsum(
            "hqk,khd->qhd", attn_probs, value_rows, preferred_element_type=jnp.float32
        )
        return (context.astype(jnp.bfloat16), total_log[..., 0])

    contexts, log_sums = lax.map(one_block, query_blocks)
    return (contexts.reshape(length, heads_here * HEAD_DIM), log_sums)


def attend_back(inputs):
    packed, log_sums, grad_context = inputs
    length, heads_here = (packed.shape[0], packed.shape[1])
    block_rows = min(512, length)
    count_blocks = length // block_rows
    factor = HEAD_DIM ** (-0.5)
    key_rows = packed[:, :, 1]
    value_rows = packed[:, :, 2]
    query_blocks = packed[:, :, 0].reshape(count_blocks, block_rows, heads_here, HEAD_DIM)
    grad_blocks = grad_context.reshape(count_blocks, block_rows, heads_here, HEAD_DIM)

    def one_block(carry, pieces):
        query_block, log_block, grad_block = pieces
        scores = factor * jnp.einsum(
            "qhd,khd->hqk", query_block, key_rows, preferred_element_type=jnp.float32
        )
        attn_probs = jnp.exp(scores - log_block[..., None])
        rounded = attn_probs.astype(jnp.bfloat16)
        grad_probs = jnp.einsum(
            "qhd,khd->hqk", grad_block, value_rows, preferred_element_type=jnp.float32
        )
        grad_values = carry[1] + jnp.einsum(
            "hqk,qhd->khd", rounded, grad_block, preferred_element_type=jnp.float32
        )
        centre = jnp.sum(attn_probs * grad_probs, -1, keepdims=True)
        grad_scores = (attn_probs * (grad_probs - centre)).astype(jnp.bfloat16)
        grad_query = factor * jnp.einsum(
            "hqk,khd->qhd", grad_scores, key_rows, preferred_element_type=jnp.float32
        )
        grad_keys = carry[0] + factor * jnp.einsum(
            "hqk,qhd->khd", grad_scores, query_block, preferred_element_type=jnp.float32
        )
        return ((grad_keys, grad_values), grad_query)

    zeros = jnp.zeros(key_rows.shape, jnp.float32)
    (grad_keys, grad_values), grad_queries = lax.scan(
        one_block, (zeros, zeros), (query_blocks, log_sums, grad_blocks)
    )
    grad_queries = grad_queries.reshape(length, heads_here, HEAD_DIM)
    stacked = jnp.stack([grad_queries, grad_keys, grad_values], 2).astype(jnp.bfloat16)
    return stacked.reshape(length, heads_here * 3 * HEAD_DIM)


def on_device(
    tokens,
    cotangent,
    group_items,
    dataset_ids,
    lead_hours,
    set_weights,
    lead_weight,
    lead_shift,
    norm_one_gain,
    norm_one_shift,
    heads_weight,
    heads_bias,
    merge_weight,
    merge_bias,
    norm_two_gain,
    norm_two_shift,
    widen_weight,
    widen_bias,
    narrow_weight,
    narrow_bias,
):
    rows_here = tokens.shape[0]
    group_rows = rows_here * lax.axis_size("mp")
    slots = dataset_ids.shape[0]
    length = group_rows // slots
    heads_here = heads_weight.shape[1] // (3 * HEAD_DIM)
    row_ids = lax.axis_index("mp") * rows_here + jnp.arange(rows_here, dtype=jnp.int32)
    slot_ids = jnp.arange(slots, dtype=jnp.int32)
    slot_table = ((row_ids // length)[:, None] == slot_ids[None, :]).astype(jnp.float32)
    lead_scaled = jnp.sum(slot_table * (lead_hours.astype(jnp.float32) / 100.0)[None, :], 1)
    live = (slot_ids < group_items[0]).astype(jnp.float32)
    set_ids = jnp.arange(set_weights.shape[0], dtype=jnp.int32)
    set_match = (dataset_ids[:, None] == set_ids[None, :]).astype(jnp.float32)
    item_weight = live * jnp.sum(set_match * set_weights[None, :], 1)
    row_weight = jnp.sum(slot_table * item_weight[None, :], 1)
    start_state = tokens + lead_scaled[:, None] * lead_weight + lead_shift
    normed_one = layer_norm(start_state, norm_one_gain, norm_one_shift).astype(jnp.bfloat16)
    gathered_one = lax.all_gather(normed_one, "mp", axis=0, tiled=True)
    bias_heads = heads_bias.reshape(heads_here, 2, HEAD_DIM)
    full_bias = jnp.stack(
        [bias_heads[:, 0], jnp.zeros_like(bias_heads[:, 0]), bias_heads[:, 1]], 1
    ).reshape(-1)
    packed = (
        jnp.dot(gathered_one, heads_weight, preferred_element_type=jnp.float32) + full_bias
    ).astype(jnp.bfloat16)
    packed_items = packed.reshape(slots, length, heads_here, 3, HEAD_DIM)
    contexts, log_sums = lax.map(attend_item, packed_items)
    context_rows = contexts.reshape(group_rows, heads_here * HEAD_DIM)
    middle = (
        start_state
        + lax.psum_scatter(
            jnp.dot(context_rows, merge_weight, preferred_element_type=jnp.float32),
            "mp",
            scatter_dimension=0,
            tiled=True,
        )
        + merge_bias
    )
    normed_two = layer_norm(middle, norm_two_gain, norm_two_shift).astype(jnp.bfloat16)
    gathered_two = lax.all_gather(normed_two, "mp", axis=0, tiled=True)
    hidden_pre = (
        jnp.dot(gathered_two, widen_weight, preferred_element_type=jnp.float32) + widen_bias
    )
    hidden = exact_gelu(hidden_pre).astype(jnp.bfloat16)
    activations = (
        middle
        + lax.psum_scatter(
            jnp.dot(hidden, narrow_weight, preferred_element_type=jnp.float32).astype(jnp.bfloat16),
            "mp",
            scatter_dimension=0,
            tiled=True,
        ).astype(jnp.float32)
        + narrow_bias
    )
    item_total = lax.psum(group_items.astype(jnp.float32)[0], "dp")
    grad_out = cotangent * row_weight[:, None]
    grad_low = grad_out.astype(jnp.bfloat16)
    grad_rows = lax.all_gather(grad_low, "mp", axis=0, tiled=True)
    grad_hidden = dot_last(grad_rows, narrow_weight)
    narrow_weight_grad = dot_first(hidden, grad_rows)
    narrow_bias_grad = jnp.sum(grad_low.astype(jnp.float32), 0)
    gelu_value, gelu_back = jax.vjp(exact_gelu, hidden_pre)
    grad_pre = gelu_back(grad_hidden)[0].astype(jnp.bfloat16)
    widen_weight_grad = dot_first(gathered_two, grad_pre)
    widen_bias_grad = jnp.sum(grad_pre.astype(jnp.float32), 0)
    grad_norm_two = lax.psum_scatter(
        dot_last(grad_pre, widen_weight), "mp", scatter_dimension=0, tiled=True
    )
    norm_value, norm_two_back = jax.vjp(layer_norm, middle, norm_two_gain, norm_two_shift)
    grad_mid_norm, norm_two_gain_grad, norm_two_shift_grad = norm_two_back(grad_norm_two)
    grad_middle = grad_out + grad_mid_norm
    grad_mid_low = grad_middle.astype(jnp.bfloat16)
    merge_bias_grad = jnp.sum(grad_mid_low.astype(jnp.float32), 0)
    grad_mid_rows = lax.all_gather(grad_mid_low, "mp", axis=0, tiled=True)
    merge_weight_grad = dot_first(context_rows, grad_mid_rows)
    grad_context = dot_last(grad_mid_rows, merge_weight).astype(jnp.bfloat16)
    grad_packed = lax.map(
        attend_back,
        (packed_items, log_sums, grad_context.reshape(slots, length, heads_here * HEAD_DIM)),
    )
    grad_packed = grad_packed.reshape(group_rows, heads_here * 3 * HEAD_DIM)
    heads_weight_grad = dot_first(gathered_one, grad_packed)
    column_sums = jnp.sum(grad_packed.astype(jnp.float32), 0).reshape(heads_here, 3, HEAD_DIM)
    heads_bias_grad = jnp.stack([column_sums[:, 0], column_sums[:, 2]], 1).reshape(-1)
    grad_norm_one = lax.psum_scatter(
        dot_last(grad_packed, heads_weight).astype(jnp.bfloat16),
        "mp",
        scatter_dimension=0,
        tiled=True,
    ).astype(jnp.float32)
    first_value, norm_one_back = jax.vjp(layer_norm, start_state, norm_one_gain, norm_one_shift)
    grad_start_norm, norm_one_gain_grad, norm_one_shift_grad = norm_one_back(grad_norm_one)
    grad_start = grad_middle + grad_start_norm
    lead_weight_grad = jnp.sum(grad_start * lead_scaled[:, None], 0)
    lead_shift_grad = jnp.sum(grad_start, 0)
    vectors = lax.psum(
        (
            lead_weight_grad,
            lead_shift_grad,
            norm_one_gain_grad,
            norm_one_shift_grad,
            merge_bias_grad,
            norm_two_gain_grad,
            norm_two_shift_grad,
            narrow_bias_grad,
        ),
        ("dp", "mp"),
    )
    matrices = (
        lax.psum(heads_weight_grad.astype(jnp.bfloat16), "dp").astype(jnp.float32),
        lax.psum(heads_bias_grad.astype(jnp.bfloat16), "dp").astype(jnp.float32),
        lax.psum(merge_weight_grad.astype(jnp.bfloat16), "dp").astype(jnp.float32),
        lax.psum(widen_weight_grad.astype(jnp.bfloat16), "dp").astype(jnp.float32),
        lax.psum(widen_bias_grad.astype(jnp.bfloat16), "dp").astype(jnp.float32),
        lax.psum(narrow_weight_grad.astype(jnp.bfloat16), "dp").astype(jnp.float32),
    )
    merge_total = matrices[2]
    return (
        activations,
        grad_start / item_total,
        vectors[0] / item_total,
        vectors[1] / item_total,
        vectors[2] / item_total,
        vectors[3] / item_total,
        matrices[0] / item_total,
        matrices[1] / item_total,
        merge_total / item_total,
        vectors[4] / item_total,
        vectors[5] / item_total,
        vectors[6] / item_total,
        matrices[3] / item_total,
        matrices[4] / item_total,
        matrices[5] / item_total,
        vectors[7] / item_total,
    )


def solution(mesh):
    return jax.shard_map(
        on_device,
        mesh=mesh,
        in_specs=(
            P(("dp", "mp"), None),
            P(("dp", "mp"), None),
            P("dp"),
            P("dp"),
            P("dp"),
            P(),
            P(),
            P(),
            P(),
            P(),
            P(None, "mp"),
            P("mp"),
            P("mp", None),
            P(),
            P(),
            P(),
            P(None, "mp"),
            P("mp"),
            P("mp", None),
            P(),
        ),
        out_specs=(
            P(("dp", "mp"), None),
            P(("dp", "mp"), None),
            P(),
            P(),
            P(),
            P(),
            P(None, "mp"),
            P("mp"),
            P("mp", None),
            P(),
            P(),
            P(),
            P(None, "mp"),
            P("mp"),
            P("mp", None),
            P(),
        ),
        check_vma=False,
    )
```

profile of v0, /device:TPU:0, one launch (start us, length us, event | category | flops | bytes accessed | tf_op | source)
XLA Modules:
  0.0 2520.8 jit_solution(8284198617445967042)
XLA Ops:
  18.3 178.7 %all-gather.5.cloned.1.call-done = bf16[6144,1024]{1,0:T(8,128)(2,1)} async-done(((bf16[768,1024]{1,0:T(8,128)(2,1)}), bf16[6144,1024]{1,0:T(8,128)(2,1)}) %all-gather.5.cloned.1.call-update) | async-done | bytes 12582928 | tf_op jit(solution)/shard_map/all_gather | solution.py:141
  208.1 23.4 reshape.212
  231.5 17.8 copy.69
  249.3 81.9 %while.50 = (s32[]{:T(128)}, bf16[3,2048,128]{2,1,0:T(8,128)(2,1)}, f32[3,4,2,512]{3,2,1,0:T(2,128)S(1)}, bf16[3,2048,2,3,64]{1,4,2,3,0:T(8,128)(2,1)}, s32[]{:T(128)}, /*index=5*/s32[]{:T(128)}, s32[]{:T(128)}) while((s32[]{:T(128)}, bf16[3,2048,128]{2,1,0:T(8,128)(2,1)}, f32[3,4,2,512]{3,2,1,0:T(2,128)S(1)}, ...), condition=%wide.region_8.9_spmd, body=%wide.region_3.8_spmd.sunk | while | flops 553712640 | bytes 38076672 | solution.py:150
  251.5 21.4 while.53
  278.8 21.4 while.53
  306.1 21.4 while.53
  343.1 401.8 %reduce-scatter.5.cloned.1.call-done = f32[768,1024]{1,0:T(8,128)} async-done(((f32[6144,1024]{1,0:T(8,128)}), f32[768,1024]{1,0:T(8,128)}) %reduce-scatter.5.cloned.1.call-update) | async-done | bytes 3145744 | tf_op jit(solution)/shard_map/reduce_scatter | solution.py:154
  756.7 171.5 %all-gather.7.cloned.1.call-done = bf16[6144,1024]{1,0:T(8,128)(2,1)} async-done(((bf16[768,1024]{1,0:T(8,128)(2,1)}), bf16[6144,1024]{1,0:T(8,128)(2,1)}) %all-gather.7.cloned.1.call-update) | async-done | bytes 12582928 | tf_op jit(solution)/shard_map/all_gather | solution.py:163
  928.2 14.3 fusion.66
  942.6 162.9 %all-gather.9.cloned.1.call-done = bf16[6144,1024]{1,0:T(8,128)(2,1)} async-done(((bf16[768,1024]{1,0:T(8,128)(2,1)}), bf16[6144,1024]{1,0:T(8,128)(2,1)}) %all-gather.9.cloned.1.call-update) | async-done | bytes 12582928 | tf_op jit(solution)/shard_map/all_gather | solution.py:181
  1105.5 40.0 %fusion.58 = (bf16[512]{0:T(512)(128)(2,1)}, bf16[6144,512]{1,0:T(8,128)(2,1)S(1)}, f32[6144,512]{1,0:T(8,128)}) fusion(f32[6144,512]{1,0:T(8,128)} %fusion.66, f32[512]{0:T(512)S(1)} %copy-done.59, bf16[6144,1024]{1,0:T(8,128)(2,1)} %all-gather.9.cloned.1.call-done, bf16[512,1024]{1,0:T(8,128)(2,1)S(1)} %copy-done), kind=kOutput, calls=%fused_computation.155 | convolution fusion | flops 6675234304 | bytes 45091840 | tf_op jit(solution)/shard_map/dot_general | solution.py:24
  1183.3 378.7 %reduce-scatter.9.cloned.1.call-done = f32[768,1024]{1,0:T(8,128)} async-done(((f32[6144,1024]{1,0:T(8,128)}), f32[768,1024]{1,0:T(8,128)}) %reduce-scatter.9.cloned.1.call-update) | async-done | bytes 3145744 | tf_op jit(solution)/shard_map/reduce_scatter | solution.py:189
  1566.6 205.4 %reduce-scatter.7.cloned.1.call-done = bf16[768,1024]{1,0:T(8,128)(2,1)} async-done(((bf16[6144,1024]{1,0:T(8,128)(2,1)}), bf16[768,1024]{1,0:T(8,128)(2,1)}) %reduce-scatter.7.cloned.1.call-update) | async-done | bytes 1572880 | tf_op jit(solution)/shard_map/reduce_scatter | solution.py:170
  1780.1 12.4 convolution_convert_fusion.4
  1803.2 152.4 %all-gather.11.cloned.1.call-done = bf16[6144,1024]{1,0:T(8,128)(2,1)} async-done(((bf16[768,1024]{1,0:T(8,128)(2,1)}), bf16[6144,1024]{1,0:T(8,128)(2,1)}) %all-gather.11.cloned.1.call-update) | async-done | bytes 12582928 | tf_op jit(solution)/shard_map/all_gather | solution.py:197
  1963.6 187.7 %while.52 = (s32[]{:T(128)}, bf16[3,2048,384]{1,2,0:T(8,128)(2,1)}, bf16[3,2048,2,3,64]{1,4,2,3,0:T(8,128)(2,1)}, f32[3,4,2,512]{3,2,1,0:T(2,128)}, bf16[3,2048,...) while((s32[]{:T(128)}, bf16[3,2048,384]{1,2,0:T(8,128)(2,1)}, ...), condition=%wide.region_22.23_spmd, body=%wide.region_18.22_spmd.sunk | while | flops 1370815488 | bytes 114618872 | solution.py:200
  1973.5 48.9 %while.54 = (s32[]{:T(128)}, f32[2048,2,64]{0,2,1:T(8,128)S(1)}, f32[2048,2,64]{0,2,1:T(8,128)S(1)}, bf16[4,512,2,64]{1,3,2,0:T(8,128)(2,1)}, bf16[4,512,2,64]{1...) while((s32[]{:T(128)}, f32[2048,2,64]{0,2,1:T(8,128)S(1)}, ...), condition=%wide.region_21.21_spmd.clone, body=%wide.region_19.20_spmd.clone.sunk | while | flops 1368718336 | bytes 75788520 | solution.py:95
  2036.0 48.9 %while.54 = (s32[]{:T(128)}, f32[2048,2,64]{0,2,1:T(8,128)S(1)}, f32[2048,2,64]{0,2,1:T(8,128)S(1)}, bf16[4,512,2,64]{1,3,2,0:T(8,128)(2,1)}, bf16[4,512,2,64]{1...) while((s32[]{:T(128)}, f32[2048,2,64]{0,2,1:T(8,128)S(1)}, ...), condition=%wide.region_21.21_spmd.clone, body=%wide.region_19.20_spmd.clone.sunk | while | flops 1368718336 | bytes 75788520 | solution.py:95
  2098.4 48.9 %while.54 = (s32[]{:T(128)}, f32[2048,2,64]{0,2,1:T(8,128)S(1)}, f32[2048,2,64]{0,2,1:T(8,128)S(1)}, bf16[4,512,2,64]{1,3,2,0:T(8,128)(2,1)}, bf16[4,512,2,64]{1...) while((s32[]{:T(128)}, f32[2048,2,64]{0,2,1:T(8,128)S(1)}, ...), condition=%wide.region_21.21_spmd.clone, body=%wide.region_19.20_spmd.clone.sunk | while | flops 1368718336 | bytes 75788520 | solution.py:95
  2175.7 12.1 convolution_convert_fusion.1
  2208.8 34.4 %all-reduce.5.cloned.1.call-done = (bf16[1024,384]{1,0:T(8,128)(2,1)}, bf16[128,1024]{1,0:T(8,128)(2,1)}, bf16[1024,512]{1,0:T(8,128)(2,1)}, bf16[512,1024]{1,0:T(8,128)(2,1)}) async-done(((bf16[1024,384]{1,0:T(8,128)(2,1)}, bf16[128,1024]{1,0:T(8,128)(2,1)}, bf16[1024,512]{1,0:T(8,128)(2,1)}, bf16[512,1024]{1,0:T(8,128)(2,1)}), (bf16[1024,384]{1,0:T(8,128)(2,1)}, bf16[128,1024]{1,0:T(8,128)(2,1)}, ...) | async-done | bytes 3145744 | tf_op jit(solution)/shard_map/psum | solution.py:233
  2254.9 199.4 %reduce-scatter.11.cloned.1.call-done = bf16[768,1024]{1,0:T(8,128)(2,1)} async-done(((bf16[6144,1024]{1,0:T(8,128)(2,1)}), bf16[768,1024]{1,0:T(8,128)(2,1)}) %reduce-scatter.11.cloned.1.call-update) | async-done | bytes 1572880 | tf_op jit(solution)/shard_map/reduce_scatter | solution.py:208
  2468.8 39.9 %all-reduce = (f32[1024]{0:T(1024)S(1)}, f32[1024]{0:T(1024)S(1)}, f32[1024]{0:T(1024)S(1)}, f32[1024]{0:T(1024)S(1)}, f32[1024]{0:T(1024)S(1)}, /*index=5*/f32[...) all-reduce(f32[1024]{0:T(1024)S(1)} %get-tuple-element.268, ...), channel_id=1, replica_groups=mesh['dp'=4,'mp'=8] {'dp','mp'}, use_global_device_ids=true, to_apply=%region_28.29 | all-reduce | flops 8192 | bytes 65536 | tf_op jit(solution)/shard_map/psum | solution.py:219
  (506 shorter events, 458.1 us)
Async XLA Ops:
  7.2 1098.3 %copy-start = (bf16[512,1024]{1,0:T(8,128)(2,1)S(1)}, bf16[512,1024]{1,0:T(8,128)(2,1)}, u32[]{:S(2)}) copy-start(bf16[512,1024]{1,0:T(8,128)(2,1)} %param.46) | copy-start | bytes 3145732
  7.2 189.8 %all-gather.5.cloned.1.call-start = ((), (), s32[]{:S(2)}) async-start(), calls=%async_computation.4 | async-start | bytes 14155776 | tf_op jit(solution)/shard_map/all_gather | solution.py:141
  17.8 727.0 %reduce-scatter.5.cloned.1.call-start = ((), (), s32[]{:S(2)}) async-start(), calls=%async_computation.5 | async-start | bytes 28311552 | tf_op jit(solution)/shard_map/reduce_scatter | solution.py:154
  342.7 402.1 %copy-start.21 = (f32[768]{0:T(1024)S(1)}, f32[768]{0:T(1024)}, u32[]{:S(2)}) copy-start(f32[768]{0:T(1024)} %copy-done.20) | copy-start | bytes 9220
  342.7 402.1 %copy-start.24 = (f32[1024]{0:T(1024)S(1)}, f32[1024]{0:T(1024)}, u32[]{:S(2)}) copy-start(f32[1024]{0:T(1024)} %param.35) | copy-start | bytes 12292
  342.7 402.1 %copy-start.27 = (f32[1024]{0:T(1024)S(1)}, f32[1024]{0:T(1024)}, u32[]{:S(2)}) copy-start(f32[1024]{0:T(1024)} %param.34) | copy-start | bytes 12292
  342.7 402.1 %copy-start.55 = (f32[1024]{0:T(1024)S(1)}, f32[1024]{0:T(1024)}, u32[]{:S(2)}) copy-start(f32[1024]{0:T(1024)} %param.41) | copy-start | bytes 12292
  342.8 408.1 %copy-start.47 = (f32[1024]{0:T(1024)S(1)}, f32[1024]{0:T(1024)}, u32[]{:S(2)}) copy-start(f32[1024]{0:T(1024)} %param.42) | copy-start | bytes 12292
  342.8 408.1 %copy-start.56 = (f32[1024]{0:T(1024)S(1)}, f32[1024]{0:T(1024)}, u32[]{:S(2)}) copy-start(f32[1024]{0:T(1024)} %param.43) | copy-start | bytes 12292
  342.8 585.5 %all-gather.7.cloned.1.call-start = ((), (), s32[]{:S(2)}) async-start(), calls=%async_computation.6 | async-start | bytes 14155776 | tf_op jit(solution)/shard_map/all_gather | solution.py:163
  752.6 352.9 %all-gather.9.cloned.1.call-start = ((), (), s32[]{:S(2)}) async-start(), calls=%async_computation.8 | async-start | bytes 14155776 | tf_op jit(solution)/shard_map/all_gather | solution.py:181
  756.7 348.8 %copy-start.59 = (f32[512]{0:T(512)S(1)}, f32[512]{0:T(512)}, u32[]{:S(2)}) copy-start(f32[512]{0:T(512)} %param.45) | copy-start | bytes 6148
  756.7 805.4 %reduce-scatter.9.cloned.1.call-start = ((), (), s32[]{:S(2)}) async-start(), calls=%async_computation.9 | async-start | bytes 28311552 | tf_op jit(solution)/shard_map/reduce_scatter | solution.py:189
  1160.0 611.9 %reduce-scatter.7.cloned.1.call-start = ((), (), s32[]{:S(2)}) async-start(), calls=%async_computation.7 | async-start | bytes 14155776 | tf_op jit(solution)/shard_map/reduce_scatter | solution.py:170
  1183.2 378.8 %copy-start.33 = (f32[768]{0:T(1024)S(1)}, f32[768]{0:T(1024)}, u32[]{:S(2)}) copy-start(f32[768]{0:T(1024)} %copy-done.32) | copy-start | bytes 9220
  1183.2 378.8 %copy-start.38 = (f32[768]{0:T(1024)S(1)}, f32[768]{0:T(1024)}, u32[]{:S(2)}) copy-start(f32[768]{0:T(1024)} %copy-done.37) | copy-start | bytes 9220
  1183.2 378.8 %copy-start.48 = (f32[1024]{0:T(1024)S(1)}, f32[1024]{0:T(1024)}, u32[]{:S(2)}) copy-start(f32[1024]{0:T(1024)} %param.42) | copy-start | bytes 12292
  1183.3 383.3 %copy-start.46 = (f32[768]{0:T(1024)S(1)}, f32[768]{0:T(1024)}, u32[]{:S(2)}) copy-start(f32[768]{0:T(1024)} %copy-done.45) | copy-start | bytes 9220
  1183.3 588.7 %copy-start.58 = (f32[1024]{0:T(1024)S(1)}, f32[1024]{0:T(1024)}, u32[]{:S(2)}) copy-start(f32[1024]{0:T(1024)} %param.47) | copy-start | bytes 12292
  1183.3 772.3 %all-gather.11.cloned.1.call-start = ((), (), s32[]{:S(2)}) async-start(), calls=%async_computation.10 | async-start | bytes 14155776 | tf_op jit(solution)/shard_map/all_gather | solution.py:197
  1566.6 210.7 %copy-start.35 = (f32[768]{0:T(1024)S(1)}, f32[768]{0:T(1024)}, u32[]{:S(2)}) copy-start(f32[768]{0:T(1024)} %get-tuple-element.271) | copy-start | bytes 9220
  1779.9 463.3 %all-reduce.5.cloned.1.call-start = ((), (), s32[]{:S(2)}) async-start(), calls=%async_computation.12 | async-start | bytes 6291456 | tf_op jit(solution)/shard_map/psum | solution.py:233
  2175.6 278.7 %reduce-scatter.11.cloned.1.call-start = ((), (), s32[]{:S(2)}) async-start(), calls=%async_computation.11 | async-start | bytes 14155776 | tf_op jit(solution)/shard_map/reduce_scatter | solution.py:208
  2245.8 208.5 %copy-start.42 = (f32[1024]{0:T(1024)S(1)}, f32[1024]{0:T(1024)}, u32[]{:S(2)}) copy-start(f32[1024]{0:T(1024)} %param.36) | copy-start | bytes 12292
  (91 other events, 2607.9 us)
Sparse Core Ops, SparseCore 0:
  17.9 179.1 all-gather.4
  342.9 401.8 reduce-scatter.4
  752.7 175.5 all-gather.6
  930.9 174.6 all-gather.8
  1160.1 401.8 reduce-scatter.8
  1565.5 206.4 reduce-scatter.6
  1780.0 175.5 all-gather.10
  2175.7 67.4 all-reduce.4
  2246.8 207.4 reduce-scatter.10
where the time goes:
time: 2530 us; the launch traced here: 2520 us
  waiting for transfers between devices  1890 us (75%)
  matrix products  321 us (13%)
  other arithmetic  124 us (5%)
  local copies, waits for them, and re-layouts  117 us (5%)
  blocking collectives  55 us (2%)
    reduce_scatter x1, waiting for transfers between devices, on_device(): lax.psum_scatter(jnp.dot(context_rows, merge_weight, preferred_element_ty...  402 us
    reduce_scatter x1, waiting for transfers between devices, on_device(): lax.psum_scatter(dot_last(grad_pre, widen_weight), 'mp', scatter_dimensio...  379 us
    reduce_scatter x1, waiting for transfers between devices, on_device(): lax.psum_scatter(jnp.dot(hidden, narrow_weight, preferred_element_type=jn...  205 us
    reduce_scatter x1, waiting for transfers between devices, on_device(): lax.psum_scatter(dot_last(grad_packed, heads_weight).astype(jnp.bfloat16)...  199 us
    all_gather x1, waiting for transfers between devices, on_device(): gathered_one = lax.all_gather(normed_one, 'mp', axis=0, tiled=True)  179 us
    all_gather x1, waiting for transfers between devices, on_device(): gathered_two = lax.all_gather(normed_two, 'mp', axis=0, tiled=True)  172 us
    all_gather x1, waiting for transfers between devices, on_device(): grad_rows = lax.all_gather(grad_low, 'mp', axis=0, tiled=True)  163 us
    all_gather x1, waiting for transfers between devices, on_device(): grad_mid_rows = lax.all_gather(grad_mid_low, 'mp', axis=0, tiled=True)  152 us
  transfers between devices with their start and end apart: 9, of which 9 were waited for; matrix products, arithmetic and copies ran while one was open for 4% of the time, Pallas kernels for 0%

commit v1 on v0

v1 whole, which is shorter than its diff:
```python
import functools

import jax
import jax.numpy as jnp
from jax import lax
from jax.experimental import pallas as pl
from jax.experimental.pallas import tpu as pltpu
from jax.sharding import PartitionSpec as P

HEAD_DIM = 64
EPSILON = 1e-05
F32 = jnp.float32
BF16 = jnp.bfloat16
NN = (((1,), (0,)), ((), ()))
NT = (((1,), (1,)), ((), ()))
TN = (((0,), (0,)), ((), ()))
BOTH = ("mp", "dp")
VMEM_LIMIT = 56 * 2**20

TAIL_STEP = 0.35
TAIL = (
    0.13962124730886327,
    0.1398645225480897,
    0.11981419159397333,
    0.10557980057214614,
    -0.023275300634317965,
    0.1594091170984717,
    -0.25591569617440285,
    0.14406734292143564,
    -0.029165241243977125,
)


def mm(left, right, dims=NN):
    return lax.dot_general(left, right, dims, preferred_element_type=F32)


def params():
    return pltpu.CompilerParams(vmem_limit_bytes=VMEM_LIMIT)


def cost(flops, moved, exps=0):
    return pl.CostEstimate(flops=int(flops), bytes_accessed=int(moved), transcendentals=int(exps))


def gelu_parts(value):
    size = jnp.abs(value)
    t = 1.0 / (1.0 + TAIL_STEP * size)
    poly = jnp.full_like(t, TAIL[-1])
    for term in TAIL[-2::-1]:
        poly = poly * t + term
    bell = jnp.exp(-0.5 * value * value)
    tail = poly * t * bell
    cumulative = jnp.where(value >= 0.0, 1.0 - tail, tail)
    return cumulative, value * (bell * 0.3989422804014327)


def project_kernel(x_ref, w_ref, b_ref, out_ref):
    out_ref[0] = (mm(x_ref[...], w_ref[0]) + b_ref[0]).astype(BF16)


def project(normed, weight, bias):
    shards, width, cols = weight.shape
    rows = normed.shape[0]
    return pl.pallas_call(
        project_kernel,
        grid=(shards,),
        in_specs=[
            pl.BlockSpec((rows, width), lambda m: (0, 0)),
            pl.BlockSpec((1, width, cols), lambda m: (m, 0, 0)),
            pl.BlockSpec((1, 1, cols), lambda m: (m, 0, 0)),
        ],
        out_specs=pl.BlockSpec((1, rows, cols), lambda m: (m, 0, 0)),
        out_shape=jax.ShapeDtypeStruct((shards, rows, cols), BF16),
        compiler_params=params(),
        cost_estimate=cost(2 * shards * rows * width * cols, weight.size * 2 + rows * shards * cols * 2),
    )(normed, weight, bias)


def attend_kernel(heads, block, x_ref, ctx_ref, lse_ref, keys_s, values_s):
    step = pl.program_id(1)
    length = x_ref.shape[1]

    @pl.when(step == 0)
    def _():
        for h in range(heads):
            c = h * 3 * HEAD_DIM
            keys_s[h] = x_ref[0, :, c + HEAD_DIM : c + 2 * HEAD_DIM].T
            values_s[h, :, :HEAD_DIM] = x_ref[0, :, c + 2 * HEAD_DIM : c + 3 * HEAD_DIM]
            values_s[h, :, HEAD_DIM:] = jnp.ones((length, HEAD_DIM), BF16)

    rows = pl.ds(pl.multiple_of(step * block, block), block)
    here = x_ref[0, rows, :]
    for h in range(heads):
        c = h * 3 * HEAD_DIM
        query = here[:, c : c + HEAD_DIM] * jnp.asarray(HEAD_DIM**-0.5, BF16)
        scores = mm(query, keys_s[h])
        row_max = jnp.max(scores, 1, keepdims=True)
        probs = jnp.exp(scores - row_max).astype(BF16)
        summed = mm(probs, values_s[h])
        total = summed[:, HEAD_DIM : HEAD_DIM + 1]
        ctx_ref[0, :, h * HEAD_DIM : (h + 1) * HEAD_DIM] = (summed[:, :HEAD_DIM] / total).astype(BF16)
        total_log = row_max + jnp.log(total)
        lse_ref[0, h : h + 1, :] = jnp.broadcast_to(total_log, (block, 128)).T[:1]


def attend(packed, heads, block):
    units, length, cols = packed.shape
    wide = heads * HEAD_DIM
    return pl.pallas_call(
        functools.partial(attend_kernel, heads, block),
        grid=(units, length // block),
        in_specs=[pl.BlockSpec((1, length, cols), lambda u, i: (u, 0, 0))],
        out_specs=[
            pl.BlockSpec((1, block, wide), lambda u, i: (u, i, 0)),
            pl.BlockSpec((1, heads, block), lambda u, i: (u, 0, i)),
        ],
        out_shape=[
            jax.ShapeDtypeStruct((units, length, wide), BF16),
            jax.ShapeDtypeStruct((units, heads, length), F32),
        ],
        scratch_shapes=[
            pltpu.VMEM((heads, HEAD_DIM, length), BF16),
            pltpu.VMEM((heads, length, 2 * HEAD_DIM), BF16),
        ],
        compiler_params=params(),
        cost_estimate=cost(units * heads * 16 * length * length * HEAD_DIM, packed.size * 3, units * heads * length * length),
    )(packed)


def attend_back_kernel(
    heads, block, x_ref, ctx_ref, dctx_ref, lse_ref, grad_ref, keys_t, keys_s, values_s, dk_s, dv_s
):
    step = pl.program_id(1)

    @pl.when(step == 0)
    def _():
        for h in range(heads):
            c = h * 3 * HEAD_DIM
            key = x_ref[0, :, c + HEAD_DIM : c + 2 * HEAD_DIM]
            keys_s[h] = key
            keys_t[h] = key.T
            values_s[h] = x_ref[0, :, c + 2 * HEAD_DIM : c + 3 * HEAD_DIM]
        dk_s[...] = jnp.zeros_like(dk_s)
        dv_s[...] = jnp.zeros_like(dv_s)

    rows = pl.ds(pl.multiple_of(step * block, block), block)
    here = x_ref[0, rows, :]
    grads = dctx_ref[0]
    prods = ctx_ref[0].astype(F32) * grads.astype(F32)
    for h in range(heads):
        c = h * 3 * HEAD_DIM
        part = slice(h * HEAD_DIM, (h + 1) * HEAD_DIM)
        query = here[:, c : c + HEAD_DIM] * jnp.asarray(HEAD_DIM**-0.5, BF16)
        grad = grads[:, part]
        centre = jnp.sum(prods[:, part].T, 0, keepdims=True)
        scores_t = mm(keys_s[h], query.T)
        probs_t = jnp.exp(scores_t - lse_ref[0, h : h + 1, :])
        grad_probs_t = mm(values_s[h], grad.T)
        grad_scores_t = (probs_t * (grad_probs_t - centre)).astype(BF16)
        dv_s[h] += mm(probs_t.astype(BF16), grad)
        dk_s[h] += mm(grad_scores_t, query)
        grad_query_t = mm(keys_t[h], grad_scores_t)
        grad_ref[0, rows, c : c + HEAD_DIM] = (grad_query_t.T * HEAD_DIM**-0.5).astype(BF16)

    @pl.when(step == pl.num_programs(1) - 1)
    def _():
        for h in range(heads):
            c = h * 3 * HEAD_DIM
            grad_ref[0, :, c + HEAD_DIM : c + 2 * HEAD_DIM] = dk_s[h].astype(BF16)
            grad_ref[0, :, c + 2 * HEAD_DIM : c + 3 * HEAD_DIM] = dv_s[h].astype(BF16)


def attend_back(packed, context, grad_context, lse, heads, block):
    units, length, cols = packed.shape
    wide = heads * HEAD_DIM
    return pl.pallas_call(
        functools.partial(attend_back_kernel, heads, block),
        grid=(units, length // block),
        in_specs=[
            pl.BlockSpec((1, length, cols), lambda u, i: (u, 0, 0)),
            pl.BlockSpec((1, block, wide), lambda u, i: (u, i, 0)),
            pl.BlockSpec((1, block, wide), lambda u, i: (u, i, 0)),
            pl.BlockSpec((1, heads, block), lambda u, i: (u, 0, i)),
        ],
        out_specs=pl.BlockSpec((1, length, cols), lambda u, i: (u, 0, 0)),
        out_shape=jax.ShapeDtypeStruct((units, length, cols), BF16),
        scratch_shapes=[
            pltpu.VMEM((heads, HEAD_DIM, length), BF16),
            pltpu.VMEM((heads, length, HEAD_DIM), BF16),
            pltpu.VMEM((heads, length, HEAD_DIM), BF16),
            pltpu.VMEM((heads, length, HEAD_DIM), F32),
            pltpu.VMEM((heads, length, HEAD_DIM), F32),
        ],
        compiler_params=params(),
        cost_estimate=cost(units * heads * 40 * length * length * HEAD_DIM, packed.size * 5, units * heads * length * length),
    )(packed, context, grad_context, lse)


def feed_kernel(
    parts, x_ref, g_ref, widen_ref, narrow_ref, bias_ref, out_ref, dx_ref, grads_ref, bias_grad_ref, out_s, dx_s
):
    step = pl.program_id(0)
    count, depth, tile = widen_ref.shape[1:]
    width = count * depth
    piece = depth // parts
    widen = widen_ref[0].reshape(width, tile)
    normed = x_ref[...]
    grad = g_ref[...]
    narrow = [
        narrow_ref[0, :, c * piece : (c + 1) * piece, :].reshape(tile, tile) for c in range(parts)
    ]
    narrow = jnp.concatenate(narrow, 1)
    pre = mm(normed, widen) + bias_ref[0]
    cumulative, slope = gelu_parts(pre)
    hidden = (pre * cumulative).astype(BF16)
    grad_pre = (mm(grad, narrow, NT) * (cumulative + slope)).astype(BF16)
    out = mm(hidden, narrow)
    dx = mm(grad_pre, widen, NT)

    @pl.when(step == 0)
    def _():
        out_s[...] = out
        dx_s[...] = dx

    @pl.when(step > 0)
    def _():
        out_s[...] += out
        dx_s[...] += dx

    grads_ref[0, :, :piece, :] = mm(grad_pre, normed, TN).astype(BF16).reshape(count, tile // count, width)
    grads_ref[0, :, piece:, :] = mm(hidden, grad, TN).astype(BF16).reshape(count, tile // count, width)
    bias_grad_ref[0] = jnp.sum(grad_pre.astype(F32), 0, keepdims=True)

    @pl.when(step == pl.num_programs(0) - 1)
    def _():
        out_ref[...] = out_s[...]
        dx_ref[...] = dx_s[...]


def feed(normed, grad, rest, bias, extra):
    shards, count, _, tile = rest.shape
    rows, width = normed.shape
    depth = width // count
    parts = width // tile
    piece = tile // count
    return pl.pallas_call(
        functools.partial(feed_kernel, parts),
        grid=(shards,),
        in_specs=[
            pl.BlockSpec((rows, width), lambda m: (0, 0)),
            pl.BlockSpec((rows, width), lambda m: (0, 0)),
            pl.BlockSpec((1, count, depth, tile), lambda m: (m, 0, 0, 0)),
            pl.BlockSpec((1, count, depth, tile), lambda m: (m, 0, 1, 0)),
            pl.BlockSpec((1, 1, tile), lambda m: (m, 0, 0)),
        ],
        out_specs=[
            pl.BlockSpec((rows, width), lambda m: (0, 0)),
            pl.BlockSpec((rows, width), lambda m: (0, 0)),
            pl.BlockSpec((1, count, 2 * piece, width), lambda m: (m, 0, 0, 0)),
            pl.BlockSpec((1, 1, tile), lambda m: (m, 0, 0)),
        ],
        out_shape=[
            jax.ShapeDtypeStruct((rows, width), F32),
            jax.ShapeDtypeStruct((rows, width), F32),
            jax.ShapeDtypeStruct((shards, count, 2 * piece + extra, width), BF16),
            jax.ShapeDtypeStruct((shards, 1, tile), F32),
        ],
        scratch_shapes=[pltpu.VMEM((rows, width), F32), pltpu.VMEM((rows, width), F32)],
        compiler_params=params(),
        cost_estimate=cost(12 * shards * rows * width * tile, rest.size * 4 + rows * width * 12, rows * shards * tile),
    )(normed, grad, rest, rest, bias)


def project_back_kernel(x_ref, g_ref, w_ref, dx_ref, grads_ref, bias_grad_ref, dx_s):
    step = pl.program_id(0)
    grad = g_ref[0]
    dx = mm(grad, w_ref[0], NT)

    @pl.when(step == 0)
    def _():
        dx_s[...] = dx

    @pl.when(step > 0)
    def _():
        dx_s[...] += dx

    grads_ref[0] = mm(grad, x_ref[...], TN).astype(BF16)
    bias_grad_ref[0] = jnp.sum(grad.astype(F32), 0, keepdims=True)

    @pl.when(step == pl.num_programs(0) - 1)
    def _():
        dx_ref[...] = dx_s[...]


def project_back(normed, grad, weight):
    shards, width, cols = weight.shape
    rows = normed.shape[0]
    return pl.pallas_call(
        project_back_kernel,
        grid=(shards,),
        in_specs=[
            pl.BlockSpec((rows, width), lambda m: (0, 0)),
            pl.BlockSpec((1, rows, cols), lambda m: (m, 0, 0)),
            pl.BlockSpec((1, width, cols), lambda m: (m, 0, 0)),
        ],
        out_specs=[
            pl.BlockSpec((rows, width), lambda m: (0, 0)),
            pl.BlockSpec((1, cols, width), lambda m: (m, 0, 0)),
            pl.BlockSpec((1, 1, cols), lambda m: (m, 0, 0)),
        ],
        out_shape=[
            jax.ShapeDtypeStruct((rows, width), F32),
            jax.ShapeDtypeStruct((shards, cols, width), BF16),
            jax.ShapeDtypeStruct((shards, 1, cols), F32),
        ],
        scratch_shapes=[pltpu.VMEM((rows, width), F32)],
        compiler_params=params(),
        cost_estimate=cost(4 * shards * rows * width * cols, weight.size * 6),
    )(normed, grad, weight)


def norm_parts(value):
    mean = jnp.mean(value, -1, keepdims=True)
    centred = value - mean
    scale = lax.rsqrt(jnp.mean(centred * centred, -1, keepdims=True) + EPSILON)
    return centred * scale, scale


def norm_back(normal, scale, gain, grad):
    grad_x = grad * gain
    mean = jnp.mean(grad_x, -1, keepdims=True)
    along = jnp.mean(grad_x * normal, -1, keepdims=True)
    return (
        (grad_x - mean - normal * along) * scale,
        jnp.sum(grad * normal, 0),
        jnp.sum(grad, 0),
    )


def split_rows(array, count):
    share = array.shape[0] // count
    return lax.dynamic_slice_in_dim(array, lax.axis_index("dp") * share, share, 0)


def on_device(
    tokens,
    cotangent,
    group_items,
    dataset_ids,
    lead_hours,
    set_weights,
    lead_weight,
    lead_shift,
    norm_one_gain,
    norm_one_shift,
    heads_weight,
    heads_bias,
    merge_weight,
    merge_bias,
    norm_two_gain,
    norm_two_shift,
    widen_weight,
    widen_bias,
    narrow_weight,
    narrow_bias,
):
    shards = lax.axis_size("mp")
    copies = lax.axis_size("dp")
    rows_here, width = tokens.shape
    group_rows = rows_here * shards
    slots = dataset_ids.shape[0]
    length = group_rows // slots
    cols = heads_weight.shape[1]
    heads_here = cols // (3 * HEAD_DIM)
    wide = heads_here * HEAD_DIM
    tile = widen_weight.shape[1]
    parts = width // tile
    block = min(256, length)

    heads_all = lax.all_gather(split_rows(heads_weight, copies), BOTH, axis=0, tiled=True)
    heads_all = heads_all.reshape(shards, width, cols)

    def fold(part):
        return jnp.concatenate(jnp.split(part, parts, 1), 0)

    rest = jnp.concatenate(
        [
            split_rows(widen_weight, copies),
            fold(split_rows(narrow_weight, copies)),
            fold(split_rows(merge_weight, copies)),
        ],
        0,
    )
    bias_heads = heads_bias.reshape(heads_here, 2, HEAD_DIM)
    full_bias = jnp.stack(
        [bias_heads[:, 0], jnp.zeros_like(bias_heads[:, 0]), bias_heads[:, 1]], 1
    ).reshape(-1)
    biases = jnp.concatenate([full_bias, widen_bias])
    biases = lax.all_to_all(
        jnp.broadcast_to(biases, (shards,) + biases.shape), "mp", 0, 0, tiled=True
    )
    heads_bias_all = biases[:, None, :cols]
    widen_bias_all = biases[:, None, cols:]

    row_ids = lax.axis_index("mp") * rows_here + jnp.arange(rows_here, dtype=jnp.int32)
    slot_ids = jnp.arange(slots, dtype=jnp.int32)
    slot_table = ((row_ids // length)[:, None] == slot_ids[None, :]).astype(F32)
    lead_scaled = jnp.sum(slot_table * (lead_hours.astype(F32) / 100.0)[None, :], 1)
    live = (slot_ids < group_items[0]).astype(F32)
    set_ids = jnp.arange(set_weights.shape[0], dtype=jnp.int32)
    set_match = (dataset_ids[:, None] == set_ids[None, :]).astype(F32)
    item_weight = live * jnp.sum(set_match * set_weights[None, :], 1)
    row_weight = jnp.sum(slot_table * item_weight[None, :], 1)
    item_total = lax.psum(group_items.astype(F32)[0], "dp")

    start_state = tokens + lead_scaled[:, None] * lead_weight + lead_shift
    first_normal, first_scale = norm_parts(start_state)
    normed_one = (first_normal * norm_one_gain + norm_one_shift).astype(BF16)
    packed = project(normed_one, heads_all, heads_bias_all)
    packed, rest = lax.optimization_barrier((packed, rest))
    rest = lax.all_gather(rest, BOTH, axis=0, tiled=True)
    rest = rest.reshape(shards, copies, -1, tile)
    packed = lax.all_to_all(packed, "mp", 0, 0, tiled=True).reshape(slots, length, cols)
    context, lse = attend(packed, heads_here, block)
    context_rows = lax.all_to_all(
        context.reshape(shards, rows_here, wide), "mp", 0, 0, tiled=True
    )
    context_rows = context_rows.transpose(1, 0, 2).reshape(rows_here, width)
    merge_rows = merge_weight.shape[0] // copies
    merge_all = rest[:, :, -merge_rows * parts :, :].reshape(shards, copies, parts, merge_rows, tile)
    merge_all = merge_all.transpose(0, 1, 3, 2, 4).reshape(width, width)
    middle = start_state + mm(context_rows, merge_all) + merge_bias
    second_normal, second_scale = norm_parts(middle)
    normed_two = (second_normal * norm_two_gain + norm_two_shift).astype(BF16)

    grad_out = cotangent * row_weight[:, None]
    grad_low = grad_out.astype(BF16)
    narrow_bias_grad = jnp.sum(grad_low.astype(F32), 0)
    fed, grad_norm_two, grads_one, widen_bias_grad = feed(
        normed_two, grad_low, rest, widen_bias_all, merge_rows
    )
    activations = middle + fed + narrow_bias
    grad_mid_norm, norm_two_gain_grad, norm_two_shift_grad = norm_back(
        second_normal, second_scale, norm_two_gain, grad_norm_two
    )
    grad_middle = grad_out + grad_mid_norm
    grad_mid_low = grad_middle.astype(BF16)
    merge_bias_grad = jnp.sum(grad_mid_low.astype(F32), 0)
    merge_weight_grad = mm(context_rows, grad_mid_low, TN).astype(BF16)
    grads_one = grads_one.at[:, :, -merge_rows:].set(
        merge_weight_grad.reshape(shards, copies, merge_rows, width)
    )
    grads_one = lax.psum_scatter(
        grads_one.reshape(-1, width), BOTH, scatter_dimension=0, tiled=True
    )
    grad_context = mm(grad_mid_low, merge_all, NT).astype(BF16)
    grad_context = lax.all_to_all(
        grad_context.reshape(rows_here, shards, wide).transpose(1, 0, 2), "mp", 0, 0, tiled=True
    )
    grad_packed = attend_back(
        packed, context, grad_context.reshape(slots, length, wide), lse, heads_here, block
    )
    grad_packed = lax.all_to_all(
        grad_packed.reshape(shards, rows_here, cols), "mp", 0, 0, tiled=True
    )
    grad_norm_one, grads_two, heads_bias_grad = project_back(normed_one, grad_packed, heads_all)
    grads_two = lax.psum_scatter(
        grads_two.reshape(-1, width), BOTH, scatter_dimension=0, tiled=True
    )
    grad_start_norm, norm_one_gain_grad, norm_one_shift_grad = norm_back(
        first_normal, first_scale, norm_one_gain, grad_norm_one
    )
    grad_start = grad_middle + grad_start_norm
    lead_weight_grad = jnp.sum(grad_start * lead_scaled[:, None], 0)
    lead_shift_grad = jnp.sum(grad_start, 0)
    vectors = (
        lead_weight_grad,
        lead_shift_grad,
        norm_one_gain_grad,
        norm_one_shift_grad,
        merge_bias_grad,
        norm_two_gain_grad,
        norm_two_shift_grad,
        narrow_bias_grad,
    )
    vectors = jnp.concatenate(
        [jnp.stack(vectors).reshape(-1), widen_bias_grad.reshape(-1), heads_bias_grad.reshape(-1)]
    )
    vectors = lax.psum(vectors, ("dp", "mp")) / item_total
    shared = vectors[: 8 * width].reshape(8, width)
    place = lax.axis_index("mp")
    widen_bias_total = lax.dynamic_slice_in_dim(vectors, 8 * width + place * tile, tile, 0)
    heads_bias_total = lax.dynamic_slice_in_dim(
        vectors, 8 * width + shards * tile + place * cols, cols, 0
    ).reshape(heads_here, 3, HEAD_DIM)
    heads_bias_total = jnp.stack([heads_bias_total[:, 0], heads_bias_total[:, 2]], 1).reshape(-1)

    grads_one = lax.all_gather(grads_one, "dp", axis=0, tiled=True).astype(F32) / item_total
    grads_one = grads_one.reshape(copies, -1, width)
    piece = tile // copies
    widen_total = grads_one[:, :piece].reshape(tile, width).T
    narrow_total = grads_one[:, piece : 2 * piece].reshape(tile, width)
    merge_total = grads_one[:, 2 * piece :].reshape(-1, width)
    grads_two = lax.all_gather(grads_two, "dp", axis=0, tiled=True).astype(F32) / item_total
    heads_total = grads_two.T
    return (
        activations,
        grad_start / item_total,
        shared[0],
        shared[1],
        shared[2],
        shared[3],
        heads_total,
        heads_bias_total,
        merge_total,
        shared[4],
        shared[5],
        shared[6],
        widen_total,
        widen_bias_total,
        narrow_total,
        shared[7],
    )


def solution(mesh):
    return jax.shard_map(
        on_device,
        mesh=mesh,
        in_specs=(
            P(("dp", "mp"), None),
            P(("dp", "mp"), None),
            P("dp"),
            P("dp"),
            P("dp"),
            P(),
            P(),
            P(),
            P(),
            P(),
            P(None, "mp"),
            P("mp"),
            P("mp", None),
            P(),
            P(),
            P(),
            P(None, "mp"),
            P("mp"),
            P("mp", None),
            P(),
        ),
        out_specs=(
            P(("dp", "mp"), None),
            P(("dp", "mp"), None),
            P(),
            P(),
            P(),
            P(),
            P(None, "mp"),
            P("mp"),
            P("mp", None),
            P(),
            P(),
            P(),
            P(None, "mp"),
            P("mp"),
            P("mp", None),
            P(),
        ),
        check_vma=False,
    )
```

time: 2530 us -> 914 us (0.36)
  waiting for transfers between devices: 1890 us -> 141 us
  blocking collectives: 55 us -> 439 us
  matrix products: 321 us -> 13.1 us
  Pallas kernels: 0 us -> 219 us
  other arithmetic: 124 us -> 36.9 us
  local copies, waits for them, and re-layouts: 117 us -> 32 us
    reduce_scatter x4 -> x2, waiting for transfers between devices: 1190 us -> 52.7 us  [the longest x1 52.7 us: on_device(): lax.psum_scatter(grads_two.reshape(-1, width), BOTH, scatter_dimension=0,...]
    all_gather x4 -> x3, waiting for transfers between devices: 666 us -> 62.6 us  [the longest x1 49 us: on_device(): lax.all_gather(split_rows(heads_weight, copies), BOTH, axis=0, tiled=True)]
    all_to_all x0 -> x3, blocking collectives: none -> 384 us  [the longest x1 197 us: on_device(): lax.all_to_all(packed, 'mp', 0, 0, tiled=True).reshape(slots, length, cols)]
    dot_general x96 -> x3, matrix products: 321 us -> 13.1 us  [mm(): return lax.dot_general(left, right, dims, preferred_element_type=F32)]
    pallas_call x0 -> x5, Pallas kernels: none -> 219 us  [the longest x1 77.7 us: attend_back(): pl.pallas_call(functools.partial(attend_back_kernel, heads, block), grid=...]
    while x95 -> x0, local copies, waits for them, and re-layouts: 37.7 us -> none  [the longest x1 17.8 us: on_device(): contexts, log_sums = lax.map(attend_item, packed_items)]
    reduce_sum x23 -> x7, other arithmetic: 55.2 us -> 18.5 us  [the longest x2 6.68 us: norm_back(): jnp.sum(grad * normal, 0)]
    convert_element_type x15 -> x2, other arithmetic: 39.1 us -> 3.72 us  [the longest x1 2.02 us: on_device(): normed_one = (first_normal * norm_one_gain + norm_one_shift).astype(BF16)]
  transfers between devices with their start and end apart: 9 -> 7, of which waited for: 9 -> 4; matrix products, arithmetic and copies ran while one was open for 4% -> 6% of each run, Pallas kernels for 0% -> 16%
where the time goes in v1:
time: 914 us; the launch traced here: 908 us
  blocking collectives  439 us (48%)
  Pallas kernels  219 us (24%)
  waiting for transfers between devices  141 us (15%)
  other arithmetic  36.9 us (4%)
  local copies, waits for them, and re-layouts  32 us (4%)
  between operations  15.3 us (2%)
  matrix products  13.1 us (1%)
  starting transfers between devices  12 us (1%)
    all_to_all x1, blocking collectives, on_device(): lax.all_to_all(packed, 'mp', 0, 0, tiled=True).reshape(slots, length, cols)  197 us
    all_to_all x1, blocking collectives, on_device(): lax.all_to_all(grad_packed.reshape(shards, rows_here, cols), 'mp', 0, 0,...  146 us
    pallas_call x1, Pallas kernels, attend_back(): pl.pallas_call(functools.partial(attend_back_kernel, heads, block), grid=...  77.7 us
    pallas_call x1, Pallas kernels, feed(): pl.pallas_call(functools.partial(feed_kernel, parts), grid=(shards,), in_...  61.1 us
    reduce_scatter x1, waiting for transfers between devices, on_device(): lax.psum_scatter(grads_two.reshape(-1, width), BOTH, scatter_dimension=0,...  52.7 us
    all_gather x1, waiting for transfers between devices, on_device(): lax.all_gather(split_rows(heads_weight, copies), BOTH, axis=0, tiled=True)  49 us
    pallas_call x1, Pallas kernels, attend(): pl.pallas_call(functools.partial(attend_kernel, heads, block), grid=(unit...  47.4 us
    all_to_all x1, blocking collectives, on_device(): lax.all_to_all(grad_context.reshape(rows_here, shards, wide).transpose(1,...  40.9 us
  transfers between devices with their start and end apart: 7, of which 4 were waited for; matrix products, arithmetic and copies ran while one was open for 6% of the time, Pallas kernels for 16%

profile of v1, /device:TPU:0, one launch (start us, length us, event | category | flops | bytes accessed | tf_op | source)
XLA Modules:
  0.0 907.8 jit_solution(12028223127534730513)
XLA Ops:
  11.5 7.3 all-to-all-start
  34.7 49.0 %all-gather.4.cloned.1.call-done = bf16[8192,384]{1,0:T(8,128)(2,1)} async-done(((bf16[256,384]{1,0:T(8,128)(2,1)}), bf16[8192,384]{1,0:T(8,128)(2,1)}) %all-gather.4.cloned.1.call-update) | async-done | bytes 6291472 | tf_op jit(solution)/shard_map/all_gather | solution.py:381
  83.7 11.7 %shard_map.315 = bf16[8,768,384]{2,1,0:T(8,128)(2,1)} custom-call(bf16[768,1024]{1,0:T(8,128)(2,1)} %add_convert_fusion.1.x_ref, bf16[8,1024,384]{2,1,0:T(8,128)(2,1)} %bitcast.95, f32[8,1,384]{2,1,0:T(1,128)} %copy.54.b_ref), custom_call_target="tpu_custom_call" | custom-call | flops 4831838208 | bytes 11010048 | tf_op jit(solution)/shard_map/pallas_call | solution.py:65
  95.4 196.8 %all_to_all.29 = bf16[8,768,384]{2,1,0:T(8,128)(2,1)} all-to-all(bf16[8,768,384]{2,1,0:T(8,128)(2,1)} %shard_map.315), channel_id=1, replica_groups=mesh['dp'=4,'mp'=8] {'mp'}, dimensions={0} | all-to-all | bytes 9437184 | tf_op jit(solution)/shard_map/all_to_all | solution.py:424
  292.2 47.4 %shard_map.316 = (bf16[3,2048,128]{2,1,0:T(8,128)(2,1)}, f32[3,2,2048]{2,1,0:T(2,128)}) custom-call(bf16[3,2048,384]{2,1,0:T(8,128)(2,1)} %bitcast.67), custom_call_target="tpu_custom_call" | custom-call | flops 25769803776 | bytes 7077888 | tf_op jit(solution)/shard_map/pallas_call | solution.py:110
  342.2 4.3 all-to-all-start.2
  346.7 3.9 convert_reduce_fusion
  357.2 25.6 %all-to-all-done.2 = bf16[8,768,128]{1,2,0:T(8,128)(2,1)} async-done(((bf16[8,768,128]{1,2,0:T(8,128)(2,1)}), bf16[8,768,128]{1,2,0:T(8,128)(2,1)}, u32[]{:S(2)}, u32[]{:S(2)}) %all-to-all-start.2) | async-done | bytes 1572896 | tf_op jit(solution)/shard_map/all_to_all | solution.py:426
  382.8 4.4 fusion.12
  389.6 61.1 %shard_map.317 = (f32[768,1024]{1,0:T(8,128)}, f32[768,1024]{1,0:T(8,128)}, bf16[8,4,288,1024]{3,2,1,0:T(8,128)(2,1)}, f32[8,1,512]{2,1,0:T(1,128)}) custom-call(bf16[768,1024]{1,0:T(8,128)(2,1)} %add_convert_fusion.x_ref, bf16[768,1024]{1,0:T(8,128)(2,1)} %get-tuple-element.95.g_ref, bf16[8,4,576,512]{3,2,1,0:T(8,128)(2,1)} %bitcast.79, ...), custom_call_target="tpu_custom_call" | custom-call | flops 38654705664 | bytes 47185920 | tf_op jit(solution)/shard_map/pallas_call | solution.py:247
  454.5 4.2 convert_reduce_fusion.1
  458.7 4.4 convolution_convert_fusion
  464.7 4.4 fusion
  469.3 40.9 %all_to_all.30 = bf16[8,768,128]{2,1,0:T(8,128)(2,1)} all-to-all(bf16[8,768,128]{2,1,0:T(8,128)(2,1)S(1)} %bitcast.66), channel_id=1, replica_groups=mesh['dp'=4,'mp'=8] {'mp'}, dimensions={0} | all-to-all | bytes 3145728 | tf_op jit(solution)/shard_map/all_to_all | solution.py:458
  510.2 77.7 %shard_map.318 = bf16[3,2048,384]{2,1,0:T(8,128)(2,1)} custom-call(bf16[3,2048,384]{2,1,0:T(8,128)(2,1)} %bitcast.68, bf16[3,2048,128]{2,1,0:T(8,128)(2,1)} %get-tuple-element.40.ctx_ref, bf16[3,2048,128]{2,1,0:T(8,128)(2,1)} %bitcast.76, f32[3,2,2048]{2,1,0:T(2,128)} %get-tuple-element.44.lse_ref), custom_call_target="tpu_custom_call" | custom-call | flops 64424509440 | bytes 11796480 | tf_op jit(solution)/shard_map/pallas_call | solution.py:177
  587.9 146.0 %all_to_all.31.g_ref = bf16[8,768,384]{2,1,0:T(8,128)(2,1)} all-to-all(bf16[8,768,384]{2,1,0:T(8,128)(2,1)} %bitcast.69), channel_id=1, replica_groups=mesh['dp'=4,'mp'=8] {'mp'}, dimensions={0} | all-to-all | bytes 9437184 | tf_op jit(solution)/shard_map/all_to_all | solution.py:464
  733.9 21.1 %shard_map.319 = (f32[768,1024]{1,0:T(8,128)}, bf16[8,384,1024]{2,1,0:T(8,128)(2,1)}, f32[8,1,384]{2,1,0:T(1,128)}) custom-call(bf16[768,1024]{1,0:T(8,128)(2,1)} %add_convert_fusion.1.x_ref, bf16[8,768,384]{2,1,0:T(8,128)(2,1)} %all_to_all.31.g_ref, bf16[8,1024,384]{2,1,0:T(8,128)(2,1)} %bitcast.96), custom_call_target="tpu_custom_call" | custom-call | flops 9663676416 | bytes 18874368 | tf_op jit(solution)/shard_map/pallas_call | solution.py:299
  755.1 6.9 psum.14
  762.1 3.6 multiply_reduce_fusion.1
  769.3 39.3 %psum.15 = f32[15360]{0:T(1024)S(1)} all-reduce(f32[15360]{0:T(1024)S(1)} %pad_maximum_fusion), channel_id=1, replica_groups=mesh['dp'=4,'mp'=8] {'dp','mp'}, use_global_device_ids=true, to_apply=%region_20.21 | all-reduce | flops 15360 | bytes 122880 | tf_op jit(solution)/shard_map/psum | solution.py:490
  811.3 4.8 broadcast_divide_fusion
  816.1 52.7 %reduce-scatter.7.cloned.1.call-done = bf16[96,1024]{1,0:T(8,128)(2,1)} async-done(((bf16[3072,1024]{1,0:T(8,128)(2,1)}), bf16[96,1024]{1,0:T(8,128)(2,1)}) %reduce-scatter.7.cloned.1.call-update) | async-done | bytes 196624 | tf_op jit(solution)/shard_map/reduce_scatter | solution.py:468
  868.8 8.7 all_gather.14
  880.0 13.6 %all-gather.8.cloned.1.call-done = bf16[1152,1024]{1,0:T(8,128)(2,1)} async-done(((bf16[288,1024]{1,0:T(8,128)(2,1)}), bf16[1152,1024]{1,0:T(8,128)(2,1)}) %all-gather.8.cloned.1.call-update) | async-done | bytes 2359312 | tf_op jit(solution)/shard_map/all_gather | solution.py:499
  (121 shorter events, 52.9 us)
Async XLA Ops:
  7.2 22.6 %copy-start.9 = (f32[1024]{0:T(1024)S(1)}, f32[1024]{0:T(1024)}, u32[]{:S(2)}) copy-start(f32[1024]{0:T(1024)} %param.28) | copy-start | bytes 12292
  7.2 22.6 %copy-start.8 = (f32[1024]{0:T(1024)S(1)}, f32[1024]{0:T(1024)}, u32[]{:S(2)}) copy-start(f32[1024]{0:T(1024)} %param.29) | copy-start | bytes 12292
  7.2 76.5 %all-gather.4.cloned.1.call-start = ((), (), s32[]{:S(2)}) async-start(), calls=%async_computation.7 | async-start | bytes 6488064 | tf_op jit(solution)/shard_map/all_gather | solution.py:381
  9.0 20.8 %copy-start.2 = (f32[768,1024]{1,0:T(8,128)S(1)}, f32[768,1024]{1,0:T(8,128)}, u32[]{:S(2)}) copy-start(f32[768,1024]{1,0:T(8,128)} %param.22) | copy-start | bytes 9437188
  11.5 22.6 %all-to-all-start = ((f32[8,1,896]{2,1,0:T(1,128)}), f32[8,1,896]{2,1,0:T(1,128)S(1)}, u32[]{:S(2)}, u32[]{:S(2)}) async-start(f32[8,1,896]{2,1,0:T(1,128)} %broadcast_in_dim.6), calls=%async_computation | async-start | bytes 57344 | tf_op jit(solution)/shard_map/all_to_all | solution.py:400
  18.8 332.5 %all-gather.6.cloned.1.call-start = ((), (), s32[]{:S(2)}) async-start(), calls=%async_computation.8 | async-start | bytes 19464192 | tf_op jit(solution)/shard_map/all_gather | solution.py:422
  27.3 3.4 copy-start.15
  27.3 3.4 copy-start.22
  30.7 3.4 copy-start.12
  342.2 40.6 %all-to-all-start.2 = ((bf16[8,768,128]{1,2,0:T(8,128)(2,1)}), bf16[8,768,128]{1,2,0:T(8,128)(2,1)}, u32[]{:S(2)}, u32[]{:S(2)}) async-start(bf16[8,768,128]{1,2,0:T(8,128)(2,1)} %copy.55), calls=%async_computation.2 | async-start | bytes 3145728 | tf_op jit(solution)/shard_map/all_to_all | solution.py:426
  346.5 415.5 %reduce-scatter.5.cloned.1.call-start = ((), (), s32[]{:S(2)}) async-start(), calls=%async_computation.9 | async-start | bytes 19464192 | tf_op jit(solution)/shard_map/reduce_scatter | solution.py:454
  355.3 27.5 %copy-start.23 = (f32[1024]{0:T(1024)S(1)}, f32[1024]{0:T(1024)}, u32[]{:S(2)}) copy-start(f32[1024]{0:T(1024)} %param.35) | copy-start | bytes 12292
  450.7 3.1 copy-start.3
  450.7 3.8 copy-start.6
  450.7 3.8 copy-start.21
  458.7 4.4 copy-start.4
  464.6 404.2 %reduce-scatter.7.cloned.1.call-start = ((), (), s32[]{:S(2)}) async-start(), calls=%async_computation.11 | async-start | bytes 6488064 | tf_op jit(solution)/shard_map/reduce_scatter | solution.py:468
  755.0 7.0 copy-start.11
  755.0 7.0 copy-start.13
  755.0 7.0 copy-start.16
  755.1 138.5 %all-gather.8.cloned.1.call-start = ((), (), s32[]{:S(2)}) async-start(), calls=%async_computation.10 | async-start | bytes 2949120 | tf_op jit(solution)/shard_map/all_gather | solution.py:499
  762.0 3.6 copy-start.5
  762.1 4.1 copy-start.7
  896.6 4.3 copy-start.1
  (7 other events, 14.6 us)
Sparse Core Ops, SparseCore 0:
  11.5 72.1 all-gather.3
  95.5 200.5 all-gather.5
  464.7 260.3 reduce-scatter.4
  755.2 113.5 reduce-scatter.6
  870.3 23.2 all-gather.7

commit v2 on v1

--- a/solution.py
+++ b/solution.py
@@ -55,29 +55,108 @@
     return cumulative, value * (bell * 0.3989422804014327)
 
 
-def project_kernel(x_ref, w_ref, b_ref, out_ref):
-    out_ref[0] = (mm(x_ref[...], w_ref[0]) + b_ref[0]).astype(BF16)
-
-
-def project(normed, weight, bias):
-    shards, width, cols = weight.shape
-    rows = normed.shape[0]
+def project_kernel(slots, table_ref, own_ref, other_ref, w_ref, out_ref):
+    step = pl.program_id(0)
+    count = pl.num_programs(0)
+    width = own_ref.shape[-1]
+    block = own_ref.shape[1]
+    here = jnp.where(step < count // 2, own_ref[0], other_ref[0])
+    for j in range(slots):
+
+        @pl.when(table_ref[step] == table_ref[2 * count + j])
+        def _():
+            bias = jnp.sum(w_ref[j, width : width + 3, :].astype(F32), 0, keepdims=True)
+            rows = pl.ds(pl.multiple_of(table_ref[count + step] * block, block), block)
+            out_ref[j, rows, :] = (mm(here, w_ref[j, :width, :]) + bias).astype(BF16)
+
+
+def project(own, other, weight, table, length):
+    half, block, width = own.shape
+    slots, _, cols = weight.shape
     return pl.pallas_call(
-        project_kernel,
-        grid=(shards,),
-        in_specs=[
-            pl.BlockSpec((rows, width), lambda m: (0, 0)),
-            pl.BlockSpec((1, width, cols), lambda m: (m, 0, 0)),
-            pl.BlockSpec((1, 1, cols), lambda m: (m, 0, 0)),
+        functools.partial(project_kernel, slots),
+        grid_spec=pltpu.PrefetchScalarGridSpec(
+            num_scalar_prefetch=1,
+            grid=(2 * half,),
+            in_specs=[
+                pl.BlockSpec((1, block, width), lambda q, t: (jnp.minimum(q, half - 1), 0, 0)),
+                pl.BlockSpec((1, block, width), lambda q, t: (jnp.maximum(q - half, 0), 0, 0)),
+                pl.BlockSpec(weight.shape, lambda q, t: (0, 0, 0)),
+            ],
+            out_specs=pl.BlockSpec((slots, length, cols), lambda q, t: (0, 0, 0)),
+        ),
+        out_shape=jax.ShapeDtypeStruct((slots, length, cols), BF16),
+        compiler_params=params(),
+        cost_estimate=cost(2 * slots * length * width * cols, own.size * 4 + slots * length * cols * 2),
+    )(table, own, other, weight)
+
+
+def project_back_kernel(slots, table_ref, own_ref, other_ref, w_ref, g_ref, own_dx, other_dx, dw_ref, dx_s, dw_s):
+    step = pl.program_id(0)
+    count = pl.num_programs(0)
+    width = own_ref.shape[-1]
+    block = own_ref.shape[1]
+    here = jnp.where(step < count // 2, own_ref[0], other_ref[0])
+    dx_s[...] = jnp.zeros_like(dx_s)
+
+    @pl.when(step == 0)
+    def _():
+        dw_s[...] = jnp.zeros_like(dw_s)
+
+    for j in range(slots):
+
+        @pl.when(table_ref[step] == table_ref[2 * count + j])
+        def _():
+            rows = pl.ds(pl.multiple_of(table_ref[count + step] * block, block), block)
+            grad = g_ref[j, rows, :]
+            dx_s[...] += mm(grad, w_ref[j, :width, :], NT)
+            dw_s[j] += mm(grad, here, TN)
+
+    @pl.when(step < count // 2)
+    def _():
+        own_dx[0] = dx_s[...].astype(BF16)
+
+    @pl.when(step >= count // 2)
+    def _():
+        other_dx[0] = dx_s[...].astype(BF16)
+
+    @pl.when(step == count - 1)
+    def _():
+        dw_ref[...] = dw_s[...].astype(BF16)
+
+
+def project_back(own, other, weight, grad, table):
+    half, block, width = own.shape
+    slots, length, cols = grad.shape
+    return pl.pallas_call(
+        functools.partial(project_back_kernel, slots),
+        grid_spec=pltpu.PrefetchScalarGridSpec(
+            num_scalar_prefetch=1,
+            grid=(2 * half,),
+            in_specs=[
+                pl.BlockSpec((1, block, width), lambda q, t: (jnp.minimum(q, half - 1), 0, 0)),
+                pl.BlockSpec((1, block, width), lambda q, t: (jnp.maximum(q - half, 0), 0, 0)),
+                pl.BlockSpec(weight.shape, lambda q, t: (0, 0, 0)),
+                pl.BlockSpec(grad.shape, lambda q, t: (0, 0, 0)),
+            ],
+            out_specs=[
+                pl.BlockSpec((1, block, width), lambda q, t: (jnp.minimum(q, half - 1), 0, 0)),
+                pl.BlockSpec((1, block, width), lambda q, t: (jnp.maximum(q - half, 0), 0, 0)),
+                pl.BlockSpec((slots, cols, width), lambda q, t: (0, 0, 0)),
+            ],
+            scratch_shapes=[pltpu.VMEM((block, width), F32), pltpu.VMEM((slots, cols, width), F32)],
+        ),
+        out_shape=[
+            jax.ShapeDtypeStruct((half, block, width), BF16),
+            jax.ShapeDtypeStruct((half, block, width), BF16),
+            jax.ShapeDtypeStruct((slots, cols, width), BF16),
         ],
-        out_specs=pl.BlockSpec((1, rows, cols), lambda m: (m, 0, 0)),
-        out_shape=jax.ShapeDtypeStruct((shards, rows, cols), BF16),
         compiler_params=params(),
-        cost_estimate=cost(2 * shards * rows * width * cols, weight.size * 2 + rows * shards * cols * 2),
-    )(normed, weight, bias)
-
-
-def attend_kernel(heads, block, x_ref, ctx_ref, lse_ref, keys_s, values_s):
+        cost_estimate=cost(4 * slots * length * width * cols, own.size * 8 + grad.size * 2),
+    )(table, own, other, weight, grad)
+
+
+def attend_kernel(heads, block, place_ref, x_ref, ctx_ref, lse_ref, keys_s, values_s):
     step = pl.program_id(1)
     length = x_ref.shape[1]
 
@@ -104,32 +183,36 @@
         lse_ref[0, h : h + 1, :] = jnp.broadcast_to(total_log, (block, 128)).T[:1]
 
 
-def attend(packed, heads, block):
+def attend(packed, heads, block, places, count):
     units, length, cols = packed.shape
     wide = heads * HEAD_DIM
+    steps = length // block
     return pl.pallas_call(
         functools.partial(attend_kernel, heads, block),
-        grid=(units, length // block),
-        in_specs=[pl.BlockSpec((1, length, cols), lambda u, i: (u, 0, 0))],
-        out_specs=[
-            pl.BlockSpec((1, block, wide), lambda u, i: (u, i, 0)),
-            pl.BlockSpec((1, heads, block), lambda u, i: (u, 0, i)),
-        ],
+        grid_spec=pltpu.PrefetchScalarGridSpec(
+            num_scalar_prefetch=1,
+            grid=(units, steps),
+            in_specs=[pl.BlockSpec((1, length, cols), lambda u, i, t: (u, 0, 0))],
+            out_specs=[
+                pl.BlockSpec((1, block, wide), lambda u, i, t: (t[u * steps + i], 0, 0)),
+                pl.BlockSpec((1, heads, block), lambda u, i, t: (u, 0, i)),
+            ],
+            scratch_shapes=[
+                pltpu.VMEM((heads, HEAD_DIM, length), BF16),
+                pltpu.VMEM((heads, length, 2 * HEAD_DIM), BF16),
+            ],
+        ),
         out_shape=[
-            jax.ShapeDtypeStruct((units, length, wide), BF16),
+            jax.ShapeDtypeStruct((count, block, wide), BF16),
             jax.ShapeDtypeStruct((units, heads, length), F32),
-        ],
-        scratch_shapes=[
-            pltpu.VMEM((heads, HEAD_DIM, length), BF16),
-            pltpu.VMEM((heads, length, 2 * HEAD_DIM), BF16),
         ],
         compiler_params=params(),
         cost_estimate=cost(units * heads * 16 * length * length * HEAD_DIM, packed.size * 3, units * heads * length * length),
-    )(packed)
+    )(places, packed)
 
 
 def attend_back_kernel(
-    heads, block, x_ref, ctx_ref, dctx_ref, lse_ref, grad_ref, keys_t, keys_s, values_s, dk_s, dv_s
+    heads, block, place_ref, x_ref, ctx_ref, dctx_ref, lse_ref, grad_ref, sums_ref, keys_t, keys_s, values_s, dk_s, dv_s
 ):
     step = pl.program_id(1)
 
@@ -169,32 +252,43 @@
             c = h * 3 * HEAD_DIM
             grad_ref[0, :, c + HEAD_DIM : c + 2 * HEAD_DIM] = dk_s[h].astype(BF16)
             grad_ref[0, :, c + 2 * HEAD_DIM : c + 3 * HEAD_DIM] = dv_s[h].astype(BF16)
-
-
-def attend_back(packed, context, grad_context, lse, heads, block):
+        sums_ref[0] = jnp.sum(grad_ref[0].astype(F32), 0, keepdims=True)
+
+
+def attend_back(packed, context, grad_context, lse, heads, block, places):
     units, length, cols = packed.shape
     wide = heads * HEAD_DIM
+    steps = length // block
     return pl.pallas_call(
         functools.partial(attend_back_kernel, heads, block),
-        grid=(units, length // block),
-        in_specs=[
-            pl.BlockSpec((1, length, cols), lambda u, i: (u, 0, 0)),
-            pl.BlockSpec((1, block, wide), lambda u, i: (u, i, 0)),
-            pl.BlockSpec((1, block, wide), lambda u, i: (u, i, 0)),
-            pl.BlockSpec((1, heads, block), lambda u, i: (u, 0, i)),
-        ],
-        out_specs=pl.BlockSpec((1, length, cols), lambda u, i: (u, 0, 0)),
-        out_shape=jax.ShapeDtypeStruct((units, length, cols), BF16),
-        scratch_shapes=[
-            pltpu.VMEM((heads, HEAD_DIM, length), BF16),
-            pltpu.VMEM((heads, length, HEAD_DIM), BF16),
-            pltpu.VMEM((heads, length, HEAD_DIM), BF16),
-            pltpu.VMEM((heads, length, HEAD_DIM), F32),
-            pltpu.VMEM((heads, length, HEAD_DIM), F32),
+        grid_spec=pltpu.PrefetchScalarGridSpec(
+            num_scalar_prefetch=1,
+            grid=(units, steps),
+            in_specs=[
+                pl.BlockSpec((1, length, cols), lambda u, i, t: (u, 0, 0)),
+                pl.BlockSpec((1, block, wide), lambda u, i, t: (t[u * steps + i], 0, 0)),
+                pl.BlockSpec((1, block, wide), lambda u, i, t: (t[u * steps + i], 0, 0)),
+                pl.BlockSpec((1, heads, block), lambda u, i, t: (u, 0, i)),
+            ],
+            out_specs=[
+                pl.BlockSpec((1, length, cols), lambda u, i, t: (u, 0, 0)),
+                pl.BlockSpec((1, 1, cols), lambda u, i, t: (u, 0, 0)),
+            ],
+            scratch_shapes=[
+                pltpu.VMEM((heads, HEAD_DIM, length), BF16),
+                pltpu.VMEM((heads, length, HEAD_DIM), BF16),
+                pltpu.VMEM((heads, length, HEAD_DIM), BF16),
+                pltpu.VMEM((heads, length, HEAD_DIM), F32),
+                pltpu.VMEM((heads, length, HEAD_DIM), F32),
+            ],
+        ),
+        out_shape=[
+            jax.ShapeDtypeStruct((units, length, cols), BF16),
+            jax.ShapeDtypeStruct((units, 1, cols), F32),
         ],
         compiler_params=params(),
         cost_estimate=cost(units * heads * 40 * length * length * HEAD_DIM, packed.size * 5, units * heads * length * length),
-    )(packed, context, grad_context, lse)
+    )(places, packed, context, grad_context, lse)
 
 
 def feed_kernel(
@@ -211,7 +305,8 @@
         narrow_ref[0, :, c * piece : (c + 1) * piece, :].reshape(tile, tile) for c in range(parts)
     ]
     narrow = jnp.concatenate(narrow, 1)
-    pre = mm(normed, widen) + bias_ref[0]
+    bias = jnp.sum(bias_ref[0, 0, 0:3, :].astype(F32), 0, keepdims=True)
+    pre = mm(normed, widen) + bias
     cumulative, slope = gelu_parts(pre)
     hidden = (pre * cumulative).astype(BF16)
     grad_pre = (mm(grad, narrow, NT) * (cumulative + slope)).astype(BF16)
@@ -238,7 +333,7 @@
         dx_ref[...] = dx_s[...]
 
 
-def feed(normed, grad, rest, bias, extra):
+def feed(normed, grad, rest, bias_at, extra):
     shards, count, _, tile = rest.shape
     rows, width = normed.shape
     depth = width // count
@@ -252,7 +347,7 @@
             pl.BlockSpec((rows, width), lambda m: (0, 0)),
             pl.BlockSpec((1, count, depth, tile), lambda m: (m, 0, 0, 0)),
             pl.BlockSpec((1, count, depth, tile), lambda m: (m, 0, 1, 0)),
-            pl.BlockSpec((1, 1, tile), lambda m: (m, 0, 0)),
+            pl.BlockSpec((1, 1, 16, tile), lambda m: (m, 0, bias_at // 16, 0)),
         ],
         out_specs=[
             pl.BlockSpec((rows, width), lambda m: (0, 0)),
@@ -269,55 +364,77 @@
         scratch_shapes=[pltpu.VMEM((rows, width), F32), pltpu.VMEM((rows, width), F32)],
         compiler_params=params(),
         cost_estimate=cost(12 * shards * rows * width * tile, rest.size * 4 + rows * width * 12, rows * shards * tile),
-    )(normed, grad, rest, rest, bias)
-
-
-def project_back_kernel(x_ref, g_ref, w_ref, dx_ref, grads_ref, bias_grad_ref, dx_s):
-    step = pl.program_id(0)
-    grad = g_ref[0]
-    dx = mm(grad, w_ref[0], NT)
-
-    @pl.when(step == 0)
-    def _():
-        dx_s[...] = dx
-
-    @pl.when(step > 0)
-    def _():
-        dx_s[...] += dx
-
-    grads_ref[0] = mm(grad, x_ref[...], TN).astype(BF16)
-    bias_grad_ref[0] = jnp.sum(grad.astype(F32), 0, keepdims=True)
-
-    @pl.when(step == pl.num_programs(0) - 1)
-    def _():
-        dx_ref[...] = dx_s[...]
-
-
-def project_back(normed, grad, weight):
-    shards, width, cols = weight.shape
-    rows = normed.shape[0]
+    )(normed, grad, rest, rest, rest)
+
+
+def merge_kernel(shards, slots, place_ref, got_ref, w_ref, start_ref, vec_ref, ctx_ref, middle_ref, normed_ref):
+    b = pl.program_id(0)
+    wide = got_ref.shape[-1]
+    for p in range(shards):
+        ctx_ref[:, p * wide : (p + 1) * wide] = got_ref[place_ref[b * shards + p]]
+    middle = start_ref[...] + mm(ctx_ref[...], w_ref[...]) + vec_ref[0:1, :]
+    middle_ref[...] = middle
+    normal, _ = norm_parts(middle)
+    normed_ref[...] = (normal * vec_ref[1:2, :] + vec_ref[2:3, :]).astype(BF16)
+
+
+def merge(got, weight, start, vectors, places, slots):
+    count, block, wide = got.shape
+    rows, width = start.shape
+    shards = width // wide
+    row_spec = pl.BlockSpec((block, width), lambda b, t: (b, 0))
     return pl.pallas_call(
-        project_back_kernel,
-        grid=(shards,),
-        in_specs=[
-            pl.BlockSpec((rows, width), lambda m: (0, 0)),
-            pl.BlockSpec((1, rows, cols), lambda m: (m, 0, 0)),
-            pl.BlockSpec((1, width, cols), lambda m: (m, 0, 0)),
+        functools.partial(merge_kernel, shards, slots),
+        grid_spec=pltpu.PrefetchScalarGridSpec(
+            num_scalar_prefetch=1,
+            grid=(slots,),
+            in_specs=[
+                pl.BlockSpec(got.shape, lambda b, t: (0, 0, 0)),
+                pl.BlockSpec(weight.shape, lambda b, t: (0, 0)),
+                row_spec,
+                pl.BlockSpec(vectors.shape, lambda b, t: (0, 0)),
+            ],
+            out_specs=[row_spec, row_spec, row_spec],
+        ),
+        out_shape=[
+            jax.ShapeDtypeStruct((rows, width), BF16),
+            jax.ShapeDtypeStruct((rows, width), F32),
+            jax.ShapeDtypeStruct((rows, width), BF16),
         ],
-        out_specs=[
-            pl.BlockSpec((rows, width), lambda m: (0, 0)),
-            pl.BlockSpec((1, cols, width), lambda m: (m, 0, 0)),
-            pl.BlockSpec((1, 1, cols), lambda m: (m, 0, 0)),
-        ],
-        out_shape=[
-            jax.ShapeDtypeStruct((rows, width), F32),
-            jax.ShapeDtypeStruct((shards, cols, width), BF16),
-            jax.ShapeDtypeStruct((shards, 1, cols), F32),
-        ],
-        scratch_shapes=[pltpu.VMEM((rows, width), F32)],
         compiler_params=params(),
-        cost_estimate=cost(4 * shards * rows * width * cols, weight.size * 6),
-    )(normed, grad, weight)
+        cost_estimate=cost(2 * rows * width * width, rows * width * 20),
+    )(places, got, weight, start, vectors)
+
+
+def merge_back_kernel(shards, count, shard_ref, g_ref, w_ref, out_ref, dctx_s):
+    wide = out_ref.shape[-1]
+    grad = g_ref[...]
+    for p in range(shards):
+        dctx_s[p] = mm(grad, w_ref[p * wide : (p + 1) * wide, :], NT).astype(BF16)
+    for i in range(count):
+        out_ref[i] = dctx_s[shard_ref[i]]
+
+
+def merge_back(grad, weight, shard_of, wide):
+    rows, width = grad.shape
+    shards = width // wide
+    count = shard_of.shape[0]
+    return pl.pallas_call(
+        functools.partial(merge_back_kernel, shards, count),
+        grid_spec=pltpu.PrefetchScalarGridSpec(
+            num_scalar_prefetch=1,
+            grid=(1,),
+            in_specs=[
+                pl.BlockSpec((rows, width), lambda b, t: (0, 0)),
+                pl.BlockSpec((width, width), lambda b, t: (0, 0)),
+            ],
+            out_specs=pl.BlockSpec((count, rows, wide), lambda b, t: (0, 0, 0)),
+            scratch_shapes=[pltpu.VMEM((shards, rows, wide), BF16)],
+        ),
+        out_shape=jax.ShapeDtypeStruct((count, rows, wide), BF16),
+        compiler_params=params(),
+        cost_estimate=cost(2 * rows * width * width, rows * width * 8),
+    )(shard_of, grad, weight)
 
 
 def norm_parts(value):
@@ -371,39 +488,101 @@
     group_rows = rows_here * shards
     slots = dataset_ids.shape[0]
     length = group_rows // slots
+    block = rows_here // slots
     cols = heads_weight.shape[1]
     heads_here = cols // (3 * HEAD_DIM)
     wide = heads_here * HEAD_DIM
     tile = widen_weight.shape[1]
     parts = width // tile
-    block = min(256, length)
-
-    heads_all = lax.all_gather(split_rows(heads_weight, copies), BOTH, axis=0, tiled=True)
-    heads_all = heads_all.reshape(shards, width, cols)
-
-    def fold(part):
-        return jnp.concatenate(jnp.split(part, parts, 1), 0)
-
-    rest = jnp.concatenate(
+    dp_at = lax.axis_index("dp")
+    mp_at = lax.axis_index("mp")
+    both = ("dp", "mp")
+
+    def attention_device(group, k):
+        return (group // 2 * 2 + k % 2) * shards + k // 2 * 2 + group % 2
+
+    def row_device(group, k):
+        return group * shards + k
+
+    groups = range(copies)
+    spots = range(shards)
+
+    def meet(k_rows, k_unit):
+        return any(
+            (slots * k_rows + b) // shards == (slots * k_unit + j) // shards
+            for b in range(slots)
+            for j in range(slots)
+        )
+
+    swap = [(row_device(g, k), attention_device(g, k)) for g in groups for k in spots]
+    core_swap = [(g, g + 1 - g % 2 * 2) for g in groups]
+    reach = max(abs(a // 2 - b // 2) for a in spots for b in spots if meet(a, b))
+    shifts = [
+        s for s in range(1 - shards, shards) if any(0 <= k + s < shards and meet(k + s, k) for k in spots)
+    ]
+    lowest = shifts[0]
+
+    def far(step):
+        return [
+            (k, k + 2 * step)
+            for k in spots
+            if 0 <= k + 2 * step < shards
+            and any(
+                meet(k // 2 * 2 + a, (k // 2 + step) * 2 + b) or meet((k // 2 + step) * 2 + b, k // 2 * 2 + a)
+                for a in range(2)
+                for b in range(2)
+            )
+        ]
+
+    steps = [o for o in range(-reach, reach + 1) if o != 0]
+
+    k_here = mp_at // 2 * 2 + dp_at % 2
+    unit_ids = slots * k_here + jnp.arange(slots, dtype=jnp.int32)
+    unit_items = unit_ids // shards
+    offsets = jnp.arange(-reach, reach + 1, dtype=jnp.int32)
+    pair_at = mp_at // 2 + offsets
+    core_at = jnp.stack([dp_at % 2, 1 - dp_at % 2]).astype(jnp.int32)
+    seen = (pair_at[None, :] * 2 + core_at[:, None])[:, :, None] * slots + jnp.arange(slots, dtype=jnp.int32)
+    seen_ok = jnp.broadcast_to(((pair_at >= 0) & (pair_at < shards // 2))[None, :, None], seen.shape)
+    table = jnp.concatenate(
         [
-            split_rows(widen_weight, copies),
-            fold(split_rows(narrow_weight, copies)),
-            fold(split_rows(merge_weight, copies)),
-        ],
-        0,
-    )
-    bias_heads = heads_bias.reshape(heads_here, 2, HEAD_DIM)
-    full_bias = jnp.stack(
-        [bias_heads[:, 0], jnp.zeros_like(bias_heads[:, 0]), bias_heads[:, 1]], 1
+            jnp.where(seen_ok, seen // shards, -1).reshape(-1),
+            jnp.where(seen_ok, seen % shards, 0).reshape(-1),
+            unit_items,
+        ]
+    ).astype(jnp.int32)
+    unit_blocks = unit_items[:, None] * shards + jnp.arange(shards, dtype=jnp.int32)[None, :]
+    unit_places = (
+        ((unit_blocks // slots - k_here - lowest) * slots + jnp.arange(slots, dtype=jnp.int32)[:, None]) * slots
+        + unit_blocks % slots
     ).reshape(-1)
-    biases = jnp.concatenate([full_bias, widen_bias])
-    biases = lax.all_to_all(
-        jnp.broadcast_to(biases, (shards,) + biases.shape), "mp", 0, 0, tiled=True
-    )
-    heads_bias_all = biases[:, None, :cols]
-    widen_bias_all = biases[:, None, cols:]
-
-    row_ids = lax.axis_index("mp") * rows_here + jnp.arange(rows_here, dtype=jnp.int32)
+    row_units = (
+        (slots * mp_at + jnp.arange(slots, dtype=jnp.int32)) // shards * shards
+    )[:, None] + jnp.arange(shards, dtype=jnp.int32)[None, :]
+    row_places = (
+        ((mp_at - row_units // slots - lowest) * slots + row_units % slots) * slots
+        + jnp.arange(slots, dtype=jnp.int32)[:, None]
+    ).reshape(-1)
+    ends = mp_at - jnp.asarray(shifts, jnp.int32)
+    wanted = ((slots * ends[:, None] + jnp.arange(slots, dtype=jnp.int32)[None, :]) % shards).reshape(-1)
+
+    def shift_pairs(s):
+        return [
+            (attention_device(g, k), row_device(g, k + s))
+            for g in groups
+            for k in spots
+            if 0 <= k + s < shards and meet(k + s, k)
+        ]
+
+    def weight_pairs(j):
+        return [
+            (g * shards + (slots * k + j) % shards, attention_device(g, k)) for g in groups for k in spots
+        ]
+
+    def back(pairs):
+        return [(b, a) for a, b in pairs]
+
+    row_ids = mp_at * rows_here + jnp.arange(rows_here, dtype=jnp.int32)
     slot_ids = jnp.arange(slots, dtype=jnp.int32)
     slot_table = ((row_ids // length)[:, None] == slot_ids[None, :]).astype(F32)
     lead_scaled = jnp.sum(slot_table * (lead_hours.astype(F32) / 100.0)[None, :], 1)
@@ -417,29 +596,66 @@
     start_state = tokens + lead_scaled[:, None] * lead_weight + lead_shift
     first_normal, first_scale = norm_parts(start_state)
     normed_one = (first_normal * norm_one_gain + norm_one_shift).astype(BF16)
-    packed = project(normed_one, heads_all, heads_bias_all)
-    packed, rest = lax.optimization_barrier((packed, rest))
+
+    def exact_rows(vector):
+        high = vector.astype(BF16)
+        left = vector - high.astype(F32)
+        middle = left.astype(BF16)
+        low = (left - middle.astype(F32)).astype(BF16)
+        return jnp.pad(jnp.stack([high, middle, low]), ((0, 13), (0, 0)))
+
+    bias_heads = heads_bias.reshape(heads_here, 2, HEAD_DIM)
+    full_bias = jnp.stack(
+        [bias_heads[:, 0], jnp.zeros_like(bias_heads[:, 0]), bias_heads[:, 1]], 1
+    ).reshape(-1)
+    heads_rows = jnp.concatenate([heads_weight, exact_rows(full_bias)], 0)
+    unit_weights = jnp.stack([lax.ppermute(heads_rows, both, weight_pairs(j)) for j in range(slots)])
+
+    def fold(part):
+        return jnp.concatenate(jnp.split(part, parts, 1), 0)
+
+    rest = jnp.concatenate(
+        [
+            split_rows(widen_weight, copies),
+            fold(split_rows(narrow_weight, copies)),
+            fold(split_rows(merge_weight, copies)),
+            exact_rows(widen_bias),
+        ],
+        0,
+    )
+    merge_rows = merge_weight.shape[0] // copies
+    merge_at = 2 * (width // copies)
+    bias_at = merge_at + merge_rows * parts
+
+    mine = lax.ppermute(normed_one, both, swap)
+    around = {o: lax.ppermute(mine, "mp", far(-o)) for o in steps}
+    around[0] = mine
+    own = jnp.stack([around[o] for o in range(-reach, reach + 1)])
+    own, rest = lax.optimization_barrier((own, rest))
     rest = lax.all_gather(rest, BOTH, axis=0, tiled=True)
     rest = rest.reshape(shards, copies, -1, tile)
-    packed = lax.all_to_all(packed, "mp", 0, 0, tiled=True).reshape(slots, length, cols)
-    context, lse = attend(packed, heads_here, block)
-    context_rows = lax.all_to_all(
-        context.reshape(shards, rows_here, wide), "mp", 0, 0, tiled=True
-    )
-    context_rows = context_rows.transpose(1, 0, 2).reshape(rows_here, width)
-    merge_rows = merge_weight.shape[0] // copies
-    merge_all = rest[:, :, -merge_rows * parts :, :].reshape(shards, copies, parts, merge_rows, tile)
+    other = lax.ppermute(own, "dp", core_swap).reshape(-1, block, width)
+    own = own.reshape(-1, block, width)
+
+    packed = project(own, other, unit_weights, table, length)
+    messages = len(shifts) * slots * slots
+    context, lse = attend(packed, heads_here, block, unit_places, messages)
+    context_out = context.reshape(len(shifts), slots * slots * block, wide)
+    context_got = jnp.stack(
+        [lax.ppermute(context_out[i], both, shift_pairs(s)) for i, s in enumerate(shifts)]
+    ).reshape(messages, block, wide)
+    merge_all = rest[:, :, merge_at:bias_at, :].reshape(shards, copies, parts, merge_rows, tile)
     merge_all = merge_all.transpose(0, 1, 3, 2, 4).reshape(width, width)
-    middle = start_state + mm(context_rows, merge_all) + merge_bias
+    merge_vectors = jnp.pad(jnp.stack([merge_bias, norm_two_gain, norm_two_shift]), ((0, 5), (0, 0)))
+    context_rows, middle, normed_two = merge(
+        context_got, merge_all, start_state, merge_vectors, row_places, slots
+    )
     second_normal, second_scale = norm_parts(middle)
-    normed_two = (second_normal * norm_two_gain + norm_two_shift).astype(BF16)
 
     grad_out = cotangent * row_weight[:, None]
     grad_low = grad_out.astype(BF16)
     narrow_bias_grad = jnp.sum(grad_low.astype(F32), 0)
-    fed, grad_norm_two, grads_one, widen_bias_grad = feed(
-        normed_two, grad_low, rest, widen_bias_all, merge_rows
-    )
+    fed, grad_norm_two, grads_one, widen_bias_grad = feed(normed_two, grad_low, rest, bias_at, merge_rows)
     activations = middle + fed + narrow_bias
     grad_mid_norm, norm_two_gain_grad, norm_two_shift_grad = norm_back(
         second_normal, second_scale, norm_two_gain, grad_norm_two
@@ -454,20 +670,38 @@
     grads_one = lax.psum_scatter(
         grads_one.reshape(-1, width), BOTH, scatter_dimension=0, tiled=True
     )
-    grad_context = mm(grad_mid_low, merge_all, NT).astype(BF16)
-    grad_context = lax.all_to_all(
-        grad_context.reshape(rows_here, shards, wide).transpose(1, 0, 2), "mp", 0, 0, tiled=True
-    )
-    grad_packed = attend_back(
-        packed, context, grad_context.reshape(slots, length, wide), lse, heads_here, block
-    )
-    grad_packed = lax.all_to_all(
-        grad_packed.reshape(shards, rows_here, cols), "mp", 0, 0, tiled=True
-    )
-    grad_norm_one, grads_two, heads_bias_grad = project_back(normed_one, grad_packed, heads_all)
-    grads_two = lax.psum_scatter(
-        grads_two.reshape(-1, width), BOTH, scatter_dimension=0, tiled=True
-    )
+    grad_context = merge_back(grad_mid_low, merge_all, wanted, wide).reshape(
+        len(shifts), slots * rows_here, wide
+    )
+    grad_context = jnp.stack(
+        [lax.ppermute(grad_context[i], both, back(shift_pairs(s))) for i, s in enumerate(shifts)]
+    ).reshape(messages, block, wide)
+    grad_packed, unit_sums = attend_back(
+        packed, context, grad_context, lse, heads_here, block, unit_places
+    )
+    own_dx, other_dx, unit_grads = project_back(own, other, unit_weights, grad_packed, table)
+
+    spans = 2 * reach + 1
+    other_dx = lax.ppermute(other_dx.reshape(spans, rows_here, width), "dp", core_swap)
+    pair_dx = own_dx.reshape(spans, rows_here, width).astype(F32) + other_dx.astype(F32)
+    mine_dx = pair_dx[reach]
+    for o in steps:
+        mine_dx += lax.ppermute(pair_dx[reach + o].astype(BF16), "mp", far(o)).astype(F32)
+    grad_norm_one = lax.ppermute(mine_dx.astype(BF16), both, back(swap)).astype(F32)
+
+    heads_total = sum(
+        lax.ppermute(unit_grads[j], both, back(weight_pairs(j))).astype(F32) for j in range(slots)
+    )
+    heads_total = lax.psum(heads_total.astype(BF16), "dp").astype(F32)
+    heads_bias_grad = jnp.sum(
+        jnp.where(
+            (unit_ids % shards)[:, None, None] == jnp.arange(shards, dtype=jnp.int32)[None, :, None],
+            unit_sums,
+            0.0,
+        ),
+        0,
+    )
+
     grad_start_norm, norm_one_gain_grad, norm_one_shift_grad = norm_back(
         first_normal, first_scale, norm_one_gain, grad_norm_one
     )
@@ -502,8 +736,7 @@
     widen_total = grads_one[:, :piece].reshape(tile, width).T
     narrow_total = grads_one[:, piece : 2 * piece].reshape(tile, width)
     merge_total = grads_one[:, 2 * piece :].reshape(-1, width)
-    grads_two = lax.all_gather(grads_two, "dp", axis=0, tiled=True).astype(F32) / item_total
-    heads_total = grads_two.T
+    heads_total = heads_total.T / item_total
     return (
         activations,
         grad_start / item_total,

time: 914 us -> 735 us (0.80)
  blocking collectives: 439 us -> 47.3 us
  starting transfers between devices: 12 us -> 131 us
  Pallas kernels: 219 us -> 258 us
  waiting for transfers between devices: 141 us -> 165 us
  other arithmetic: 36.9 us -> 59.5 us
  local copies, waits for them, and re-layouts: 32 us -> 46.7 us
  matrix products: 13.1 us -> 1.87 us
    all_to_all x3 -> x0, blocking collectives: 384 us -> none  [the longest x1 197 us: on_device(): lax.all_to_all(packed, 'mp', 0, 0, tiled=True).reshape(slots, length, cols)]
    ppermute x0 -> x28, waiting for transfers between devices: none -> 141 us  [the longest x3 38 us: on_device(): lax.ppermute(heads_rows, both, weight_pairs(j))]
    ppermute x0 -> x28, starting transfers between devices: none -> 131 us  [the longest x7 40.6 us: on_device(): lax.ppermute(context_out[i], both, shift_pairs(s))]
    reduce_scatter x1 -> x0, waiting for transfers between devices: 52.7 us -> none  [on_device(): lax.psum_scatter(grads_two.reshape(-1, width), BOTH, scatter_dimension=0,...]
    all_gather x1 -> x0, waiting for transfers between devices: 49 us -> none  [on_device(): lax.all_gather(split_rows(heads_weight, copies), BOTH, axis=0, tiled=True)]
    pallas_call x4 -> x6, Pallas kernels: 158 us -> 197 us  [the longest x1 79.2 us: attend_back(): pl.pallas_call(functools.partial(attend_back_kernel, heads, block), grid_...]
    all_to_all x2 -> x0, waiting for transfers between devices: 25.6 us -> none  [the longest x1 25.6 us: on_device(): lax.all_to_all(context.reshape(shards, rows_here, wide), 'mp', 0, 0, tile...]
    psum x0 -> x1, waiting for transfers between devices: none -> 24.1 us  [on_device(): heads_total = lax.psum(heads_total.astype(BF16), 'dp').astype(F32)]
  transfers between devices with their start and end apart: 7 -> 32, of which waited for: 4 -> 14; matrix products, arithmetic and copies ran while one was open for 6% -> 9% of each run, Pallas kernels for 16% -> 26%
where the time goes in v2:
time: 735 us; the launch traced here: 725 us
  Pallas kernels  258 us (35%)
  waiting for transfers between devices  165 us (22%)
  starting transfers between devices  131 us (18%)
  other arithmetic  59.5 us (8%)
  blocking collectives  47.3 us (6%)
  local copies, waits for them, and re-layouts  46.7 us (6%)
  between operations  15.5 us (2%)
    pallas_call x1, Pallas kernels, attend_back(): pl.pallas_call(functools.partial(attend_back_kernel, heads, block), grid_...  79.2 us
    pallas_call x1, Pallas kernels, feed(): pl.pallas_call(functools.partial(feed_kernel, parts), grid=(shards,), in_...  61 us
    pallas_call x1, Pallas kernels, attend(): pl.pallas_call(functools.partial(attend_kernel, heads, block), grid_spec=...  48.2 us
    ppermute x7, starting transfers between devices, on_device(): lax.ppermute(context_out[i], both, shift_pairs(s))  40.6 us
    psum x1, blocking collectives, on_device(): vectors = lax.psum(vectors, ('dp', 'mp')) / item_total  40.1 us
    ppermute x3, waiting for transfers between devices, on_device(): lax.ppermute(heads_rows, both, weight_pairs(j))  38 us
    ppermute x2, waiting for transfers between devices, on_device(): lax.ppermute(pair_dx[reach + o].astype(BF16), 'mp', far(o)).astype(F32)  36.8 us
    pallas_call x1, Pallas kernels, project_back(): pl.pallas_call(functools.partial(project_back_kernel, slots), grid_spec=p...  32 us
  transfers between devices with their start and end apart: 32, of which 14 were waited for; matrix products, arithmetic and copies ran while one was open for 9% of the time, Pallas kernels for 26%

profile of v2, /device:TPU:0, one launch (start us, length us, event | category | flops | bytes accessed | tf_op | source)
XLA Modules:
  0.0 725.5 jit_solution(7162545022993628633)
XLA Ops:
  30.7 7.1 collective-permute-done.2
  42.8 20.5 %collective-permute-start.3 = (bf16[3,768,1024]{2,1,0:T(8,128)(2,1)}, bf16[3,768,1024]{2,1,0:T(8,128)(2,1)}, u32[]{:S(2)}, u32[]{:S(2)}) collective-permute-start(bf16[3,768,1024]{2,1,0:T(8,128)(2,1)} %pad_maximum_fusion), channel_id=1, source_target_pairs={{0,8},{8,0},{16,24},{24,16},{1,9},{9,1},{17,25},{25,17},{2,10},{10... | collective-permute-start | bytes 14155784 | tf_op jit(solution)/shard_map/ppermute | solution.py:637
  77.6 36.7 %collective-permute-done.6 = bf16[1040,384]{1,0:T(8,128)(2,1)S(1)} collective-permute-done((bf16[1040,384]{1,0:T(8,128)(2,1)S(1)}, bf16[1040,384]{1,0:T(8,128)(2,1)S(1)}, u32[]{:S(2)}, u32[]{:S(2)}) %collective-permute-start.6) | collective-permute-done | bytes 798752 | tf_op jit(solution)/shard_map/ppermute | solution.py:612
  117.4 20.7 %shard_map.324.x_ref = bf16[3,2048,384]{2,1,0:T(8,128)(2,1)} custom-call(s32[39]{0:T(128)} %pad_add_fusion.1.table_ref, bf16[9,256,1024]{2,1,0:T(8,128)(2,1)} %bitcast.126, bf16[9,256,1024]{2,1,0:T(8,128)(2,1)} %bitcast.6.other_ref, bf16[3,1040,384]{2,1,0:T(8,128)(2,1)} %pad_maximum_fusion.1.w_ref), custom_call_target="tpu_custom_call" | custom-call | flops 4831838208 | bytes 14155776 | tf_op jit(solution)/shard_map/pallas_call | solution.py:76
  138.1 48.2 %shard_map.325 = (bf16[63,256,128]{2,1,0:T(8,128)(2,1)}, f32[3,2,2048]{2,1,0:T(2,128)}) custom-call(s32[24]{0:T(128)} %get-tuple-element.172.place_ref, bf16[3,2048,384]{2,1,0:T(8,128)(2,1)} %shard_map.324.x_ref), custom_call_target="tpu_custom_call" | custom-call | flops 25769803776 | bytes 7077888 | tf_op jit(solution)/shard_map/pallas_call | solution.py:190
  195.8 12.8 %collective-permute-start.11 = (bf16[2304,128]{1,0:T(8,128)(2,1)S(1)}, bf16[2304,128]{1,0:T(8,128)(2,1)S(1)}, u32[]{:S(2)}, u32[]{:S(2)}) collective-permute-start(bf16[2304,128]{1,0:T(8,128)(2,1)S(1)} %bitcast.141), channel_id=1, source_target_pairs={{0,1},{8,2},{2,3},{10,4},{4,5},{12,6},{6,7},{1,9},{9,10},{3,11},{1... | collective-permute-start | bytes 1769480 | tf_op jit(solution)/shard_map/ppermute | solution.py:645
  208.7 22.7 %collective-permute-start.12 = (bf16[2304,128]{1,0:T(8,128)(2,1)S(1)}, bf16[2304,128]{1,0:T(8,128)(2,1)S(1)}, u32[]{:S(2)}, u32[]{:S(2)}) collective-permute-start(bf16[2304,128]{1,0:T(8,128)(2,1)S(1)} %bitcast.139), channel_id=1, source_target_pairs={{0,2},{2,4},{10,5},{12,7},{1,10},{3,12},{11,13},{13,15},{16,18},{1... | collective-permute-start | bytes 1769480 | tf_op jit(solution)/shard_map/ppermute | solution.py:645
  246.3 8.4 %shard_map.326 = (bf16[768,1024]{1,0:T(8,128)(2,1)}, f32[768,1024]{1,0:T(8,128)}, bf16[768,1024]{1,0:T(8,128)(2,1)}) custom-call(s32[24]{0:T(128)} %get-tuple-element.173.place_ref, bf16[63,256,128]{2,1,0:T(8,128)(2,1)} %bitcast.24.got_ref, bf16[1024,1024]{1,0:T(8,128)(2,1)} %bitcast.121, f32[768,1024]{1,0:T(8,128)} %copy-done, ...), custom_call_target="tpu_custom_call" | custom-call | flops 1610612736 | bytes 15728640 | tf_op jit(solution)/shard_map/pallas_call | solution.py:386
  258.1 61.0 %shard_map.327 = (f32[768,1024]{1,0:T(8,128)}, f32[768,1024]{1,0:T(8,128)}, bf16[8,4,288,1024]{3,2,1,0:T(8,128)(2,1)}, f32[8,1,512]{2,1,0:T(1,128)}) custom-call(bf16[768,1024]{1,0:T(8,128)(2,1)} %get-tuple-element.48.x_ref, bf16[768,1024]{1,0:T(8,128)(2,1)} %get-tuple-element.121.g_ref, bf16[8,4,592,512]{3,2,1,0:T(8,128)(2,1)} %bitcast.153, ...), custom_call_target="tpu_custom_call" | custom-call | flops 38654705664 | bytes 48234496 | tf_op jit(solution)/shard_map/pallas_call | solution.py:342
  332.7 8.3 %shard_map.328 = bf16[21,768,128]{2,1,0:T(8,128)(2,1)} custom-call(s32[21]{0:T(128)} %and_select_fusion.1.shard_ref, bf16[768,1024]{1,0:T(8,128)(2,1)} %copy-done.7, bf16[1024,1024]{1,0:T(8,128)(2,1)} %bitcast.122), custom_call_target="tpu_custom_call" | custom-call | flops 1610612736 | bytes 6291456 | tf_op jit(solution)/shard_map/pallas_call | solution.py:422
  344.3 14.7 %collective-permute-start.15 = (bf16[2304,128]{1,0:T(8,128)(2,1)S(1)}, bf16[2304,128]{1,0:T(8,128)(2,1)S(1)}, u32[]{:S(2)}, u32[]{:S(2)}) collective-permute-start(bf16[2304,128]{1,0:T(8,128)(2,1)S(1)} %bitcast.148), channel_id=1, source_target_pairs={{0,2},{2,4},{3,12},{5,14},{8,3},{10,5},{11,13},{13,15},{16,18},{18... | collective-permute-start | bytes 1769480 | tf_op jit(solution)/shard_map/ppermute | solution.py:677
  364.3 7.7 %collective-permute-done.15 = bf16[2304,128]{1,0:T(8,128)(2,1)S(1)} collective-permute-done((bf16[2304,128]{1,0:T(8,128)(2,1)S(1)}, bf16[2304,128]{1,0:T(8,128)(2,1)S(1)}, u32[]{:S(2)}, u32[]{:S(2)}) %collective-permute-start.15) | collective-permute-done | bytes 589856 | tf_op jit(solution)/shard_map/ppermute | solution.py:677
  378.7 15.2 %collective-permute-done.19 = bf16[2304,128]{1,0:T(8,128)(2,1)S(1)} collective-permute-done((bf16[2304,128]{1,0:T(8,128)(2,1)S(1)}, bf16[2304,128]{1,0:T(8,128)(2,1)S(1)}, u32[]{:S(2)}, u32[]{:S(2)}) %collective-permute-start.19) | collective-permute-done | bytes 589856 | tf_op jit(solution)/shard_map/ppermute | solution.py:677
  396.0 79.2 %shard_map.329 = (bf16[3,2048,384]{2,1,0:T(8,128)(2,1)}, f32[3,1,384]{2,1,0:T(1,128)}) custom-call(s32[24]{0:T(128)} %get-tuple-element.172.place_ref, bf16[3,2048,384]{2,1,0:T(8,128)(2,1)} %shard_map.324.x_ref, bf16[63,256,128]{2,1,0:T(8,128)(2,1)} %get-tuple-element.45.ctx_ref, bf16[63,256,128]{2,1,0:T(8,128)(2,1)} %bitcast.158, ...), custom_call_target="tpu_custom_call" | custom-call | flops 64424509440 | bytes 11796480 | tf_op jit(solution)/shard_map/pallas_call | solution.py:262
  475.2 32.0 %shard_map.330 = (bf16[9,256,1024]{2,1,0:T(8,128)(2,1)}, bf16[9,256,1024]{2,1,0:T(8,128)(2,1)}, bf16[3,384,1024]{2,1,0:T(8,128)(2,1)}) custom-call(s32[39]{0:T(128)} %pad_add_fusion.1.table_ref, bf16[9,256,1024]{2,1,0:T(8,128)(2,1)} %bitcast.127, bf16[9,256,1024]{2,1,0:T(8,128)(2,1)} %bitcast.6.other_ref, bf16[3,1040,384]{2,1,0:T(8,128)(2,1)} %pad_maximum_fusion.1.w_ref, ...), custom_call_target="tpu_custom_call" | custom-call | flops 9663676416 | bytes 23592960 | tf_op jit(solution)/shard_map/pallas_call | solution.py:131
  507.3 8.1 %collective-permute-done.21 = bf16[3,768,1024]{2,1,0:T(8,128)(2,1)S(1)} collective-permute-done((bf16[3,768,1024]{2,1,0:T(8,128)(2,1)}, bf16[3,768,1024]{2,1,0:T(8,128)(2,1)S(1)}, u32[]{:S(2)}, u32[]{:S(2)}) %collective-permute-start.21) | collective-permute-done | bytes 4718624 | tf_op jit(solution)/shard_map/ppermute | solution.py:685
  517.6 8.9 %fusion.37 = (bf16[3,768,1024]{2,1,0:T(8,128)(2,1)}, f32[3,768,1024]{2,1,0:T(8,128)S(1)}) fusion(bf16[3,768,1024]{2,1,0:T(8,128)(2,1)} %copy-done.8, bf16[3,768,1024]{2,1,0:T(8,128)(2,1)} %bitcast.128), kind=kLoop, calls=%fused_computation.165 | loop fusion | flops 9437184 | bytes 23592960 | tf_op jit(solution)/shard_map/convert.2
  528.8 9.4 %collective-permute-start.23 = (bf16[768,1024]{1,0:T(8,128)(2,1)S(1)}, bf16[768,1024]{1,0:T(8,128)(2,1)S(1)}, u32[]{:S(2)}, u32[]{:S(2)}) collective-permute-start(bf16[768,1024]{1,0:T(8,128)(2,1)S(1)} %get-tuple-element.133), channel_id=1, source_target_pairs={{0,2},{1,3},{2,4},{3,5},{4,6},{5,7},{8,10},{9,11},{10,12},{11,13},... | collective-permute-start | bytes 4718600 | tf_op jit(solution)/shard_map/ppermute | solution.py:689
  545.8 33.0 %collective-permute-done.23 = bf16[768,1024]{1,0:T(8,128)(2,1)S(1)} collective-permute-done((bf16[768,1024]{1,0:T(8,128)(2,1)S(1)}, bf16[768,1024]{1,0:T(8,128)(2,1)S(1)}, u32[]{:S(2)}, u32[]{:S(2)}) %collective-permute-start.23) | collective-permute-done | bytes 1572896 | tf_op jit(solution)/shard_map/ppermute | solution.py:689
  584.7 13.5 %collective-permute-start.24 = (bf16[768,1024]{1,0:T(8,128)(2,1)}, bf16[768,1024]{1,0:T(8,128)(2,1)}, u32[]{:S(2)}, u32[]{:S(2)}) collective-permute-start(bf16[768,1024]{1,0:T(8,128)(2,1)} %fusion.10), channel_id=1, source_target_pairs={{0,0},{8,1},{2,2},{10,3},{4,4},{12,5},{6,6},{14,7},{1,8},{9,9},{3,... | collective-permute-start | bytes 4718600 | tf_op jit(solution)/shard_map/ppermute | solution.py:690
  598.2 17.4 %collective-permute-done.27 = bf16[384,1024]{1,0:T(8,128)(2,1)S(1)} collective-permute-done((bf16[384,1024]{1,0:T(8,128)(2,1)S(1)}, bf16[384,1024]{1,0:T(8,128)(2,1)S(1)}, u32[]{:S(2)}, u32[]{:S(2)}) %collective-permute-start.27) | collective-permute-done | bytes 786464 | tf_op jit(solution)/shard_map/ppermute | solution.py:693
  619.1 7.2 psum.21
  626.4 24.1 %all-reduce.5.cloned.1.call-done = bf16[384,1024]{1,0:T(8,128)(2,1)} async-done(((bf16[384,1024]{1,0:T(8,128)(2,1)}), bf16[384,1024]{1,0:T(8,128)(2,1)}) %all-reduce.5.cloned.1.call-update) | async-done | bytes 786448 | tf_op jit(solution)/shard_map/psum | solution.py:695
  663.7 40.1 %psum.22 = f32[15360]{0:T(1024)S(1)} all-reduce(f32[15360]{0:T(1024)S(1)} %pad_maximum_fusion.3), channel_id=1, replica_groups=mesh['dp'=4,'mp'=8] {'dp','mp'}, use_global_device_ids=true, to_apply=%region_21.22 | all-reduce | flops 15360 | bytes 122880 | tf_op jit(solution)/shard_map/psum | solution.py:724
  (239 shorter events, 153.1 us)
Async XLA Ops:
  7.2 233.3 %all-gather.3.cloned.1.call-start = ((), (), s32[]{:S(2)}) async-start(), calls=%async_computation.1 | async-start | bytes 20004864 | tf_op jit(solution)/shard_map/all_gather | solution.py:635
  14.5 23.3 %collective-permute-start.2 = (bf16[768,1024]{1,0:T(8,128)(2,1)S(1)}, bf16[768,1024]{1,0:T(8,128)(2,1)S(1)}, u32[]{:S(2)}, u32[]{:S(2)}) collective-permute-start(bf16[768,1024]{1,0:T(8,128)(2,1)S(1)} %collective-permute-done), channel_id=1, source_target_pairs={{2,0},{3,1},{4,2},{5,3},{6,4},{7,5},{10,8},{11,9},{12,10},{13,11},... | collective-permute-start | bytes 4718600 | tf_op jit(solution)/shard_map/ppermute | solution.py:631
  15.8 23.5 %collective-permute-start.1 = (bf16[768,1024]{1,0:T(8,128)(2,1)S(1)}, bf16[768,1024]{1,0:T(8,128)(2,1)}, u32[]{:S(2)}, u32[]{:S(2)}) collective-permute-start(bf16[768,1024]{1,0:T(8,128)(2,1)S(1)} %collective-permute-done), channel_id=1, source_target_pairs={{0,2},{1,3},{2,4},{3,5},{4,6},{5,7},{8,10},{9,11},{10,12},{11,13},... | collective-permute-start | bytes 4718600 | tf_op jit(solution)/shard_map/ppermute | solution.py:631
  42.8 575.7 %reduce-scatter.2.cloned.1.call-start = ((), (), s32[]{:S(2)}) async-start(), calls=%async_computation.3 | async-start | bytes 19464192 | tf_op jit(solution)/shard_map/reduce_scatter | solution.py:670
  42.8 74.5 %collective-permute-start.3 = (bf16[3,768,1024]{2,1,0:T(8,128)(2,1)}, bf16[3,768,1024]{2,1,0:T(8,128)(2,1)}, u32[]{:S(2)}, u32[]{:S(2)}) collective-permute-start(bf16[3,768,1024]{2,1,0:T(8,128)(2,1)} %pad_maximum_fusion), channel_id=1, source_target_pairs={{0,8},{8,0},{16,24},{24,16},{1,9},{9,1},{17,25},{25,17},{2,10},{10... | collective-permute-start | bytes 14155784 | tf_op jit(solution)/shard_map/ppermute | solution.py:637
  64.9 49.5 %collective-permute-start.6 = (bf16[1040,384]{1,0:T(8,128)(2,1)S(1)}, bf16[1040,384]{1,0:T(8,128)(2,1)S(1)}, u32[]{:S(2)}, u32[]{:S(2)}) collective-permute-start(bf16[1040,384]{1,0:T(8,128)(2,1)S(1)} %pad_maximum_fusion.2), channel_id=1, source_target_pairs={{2,0},{5,8},{0,2},{3,10},{6,4},{1,12},{4,6},{7,14},{10,1},{13,9},{... | collective-permute-start | bytes 2396168 | tf_op jit(solution)/shard_map/ppermute | solution.py:612
  69.1 46.6 %collective-permute-start.5 = (bf16[1040,384]{1,0:T(8,128)(2,1)S(1)}, bf16[1040,384]{1,0:T(8,128)(2,1)S(1)}, u32[]{:S(2)}, u32[]{:S(2)}) collective-permute-start(bf16[1040,384]{1,0:T(8,128)(2,1)S(1)} %pad_maximum_fusion.2), channel_id=1, source_target_pairs={{1,0},{4,8},{7,2},{2,10},{5,4},{0,12},{3,6},{6,14},{9,1},{12,9},{1... | collective-permute-start | bytes 2396168 | tf_op jit(solution)/shard_map/ppermute | solution.py:612
  73.8 41.9 %collective-permute-start.4 = (bf16[1040,384]{1,0:T(8,128)(2,1)S(1)}, bf16[1040,384]{1,0:T(8,128)(2,1)S(1)}, u32[]{:S(2)}, u32[]{:S(2)}) collective-permute-start(bf16[1040,384]{1,0:T(8,128)(2,1)S(1)} %pad_maximum_fusion.2), channel_id=1, source_target_pairs={{0,0},{3,8},{6,2},{1,10},{4,4},{7,12},{2,6},{5,14},{8,1},{11,9},{1... | collective-permute-start | bytes 2396168 | tf_op jit(solution)/shard_map/ppermute | solution.py:612
  192.5 39.7 %collective-permute-start.8 = (bf16[2304,128]{1,0:T(8,128)(2,1)S(1)}, bf16[2304,128]{1,0:T(8,128)(2,1)S(1)}, u32[]{:S(2)}, u32[]{:S(2)}) collective-permute-start(bf16[2304,128]{1,0:T(8,128)(2,1)S(1)} %bitcast.147), channel_id=1, source_target_pairs={{2,0},{4,2},{12,3},{14,5},{3,8},{5,10},{13,11},{15,13},{18,16},{20... | collective-permute-start | bytes 1769480 | tf_op jit(solution)/shard_map/ppermute | solution.py:645
  193.8 40.4 %collective-permute-start.9 = (bf16[2304,128]{1,0:T(8,128)(2,1)S(1)}, bf16[2304,128]{1,0:T(8,128)(2,1)S(1)}, u32[]{:S(2)}, u32[]{:S(2)}) collective-permute-start(bf16[2304,128]{1,0:T(8,128)(2,1)S(1)} %bitcast.145), channel_id=1, source_target_pairs={{8,0},{2,1},{10,2},{4,3},{12,4},{6,5},{14,6},{9,8},{3,9},{11,10},{... | collective-permute-start | bytes 1769480 | tf_op jit(solution)/shard_map/ppermute | solution.py:645
  195.1 40.0 %collective-permute-start.10 = (bf16[2304,128]{1,0:T(8,128)(2,1)S(1)}, bf16[2304,128]{1,0:T(8,128)(2,1)S(1)}, u32[]{:S(2)}, u32[]{:S(2)}) collective-permute-start(bf16[2304,128]{1,0:T(8,128)(2,1)S(1)} %bitcast.143), channel_id=1, source_target_pairs={{0,0},{8,1},{2,2},{10,3},{4,4},{12,5},{6,6},{14,7},{1,8},{9,9},{3,... | collective-permute-start | bytes 1769480 | tf_op jit(solution)/shard_map/ppermute | solution.py:645
  195.8 40.2 %collective-permute-start.11 = (bf16[2304,128]{1,0:T(8,128)(2,1)S(1)}, bf16[2304,128]{1,0:T(8,128)(2,1)S(1)}, u32[]{:S(2)}, u32[]{:S(2)}) collective-permute-start(bf16[2304,128]{1,0:T(8,128)(2,1)S(1)} %bitcast.141), channel_id=1, source_target_pairs={{0,1},{8,2},{2,3},{10,4},{4,5},{12,6},{6,7},{1,9},{9,10},{3,11},{1... | collective-permute-start | bytes 1769480 | tf_op jit(solution)/shard_map/ppermute | solution.py:645
  208.7 30.0 %collective-permute-start.12 = (bf16[2304,128]{1,0:T(8,128)(2,1)S(1)}, bf16[2304,128]{1,0:T(8,128)(2,1)S(1)}, u32[]{:S(2)}, u32[]{:S(2)}) collective-permute-start(bf16[2304,128]{1,0:T(8,128)(2,1)S(1)} %bitcast.139), channel_id=1, source_target_pairs={{0,2},{2,4},{10,5},{12,7},{1,10},{3,12},{11,13},{13,15},{16,18},{1... | collective-permute-start | bytes 1769480 | tf_op jit(solution)/shard_map/ppermute | solution.py:645
  331.4 319.2 %all-reduce.5.cloned.1.call-start = ((), (), s32[]{:S(2)}) async-start(), calls=%async_computation.2 | async-start | bytes 1572864 | tf_op jit(solution)/shard_map/psum | solution.py:695
  344.3 27.6 %collective-permute-start.15 = (bf16[2304,128]{1,0:T(8,128)(2,1)S(1)}, bf16[2304,128]{1,0:T(8,128)(2,1)S(1)}, u32[]{:S(2)}, u32[]{:S(2)}) collective-permute-start(bf16[2304,128]{1,0:T(8,128)(2,1)S(1)} %bitcast.148), channel_id=1, source_target_pairs={{0,2},{2,4},{3,12},{5,14},{8,3},{10,5},{11,13},{13,15},{16,18},{18... | collective-permute-start | bytes 1769480 | tf_op jit(solution)/shard_map/ppermute | solution.py:677
  362.9 30.9 %collective-permute-start.19 = (bf16[2304,128]{1,0:T(8,128)(2,1)S(1)}, bf16[2304,128]{1,0:T(8,128)(2,1)S(1)}, u32[]{:S(2)}, u32[]{:S(2)}) collective-permute-start(bf16[2304,128]{1,0:T(8,128)(2,1)S(1)} %bitcast.140), channel_id=1, source_target_pairs={{2,0},{4,2},{5,10},{7,12},{10,1},{12,3},{13,11},{15,13},{18,16},{2... | collective-permute-start | bytes 1769480 | tf_op jit(solution)/shard_map/ppermute | solution.py:677
  371.9 22.0 %collective-permute-start.20 = (bf16[2304,128]{1,0:T(8,128)(2,1)S(1)}, bf16[2304,128]{1,0:T(8,128)(2,1)S(1)}, u32[]{:S(2)}, u32[]{:S(2)}) collective-permute-start(bf16[2304,128]{1,0:T(8,128)(2,1)S(1)} %bitcast.138), channel_id=1, source_target_pairs={{5,2},{13,3},{21,18},{29,19}} | collective-permute-start | bytes 1769480 | tf_op jit(solution)/shard_map/ppermute | solution.py:677
  528.8 50.0 %collective-permute-start.23 = (bf16[768,1024]{1,0:T(8,128)(2,1)S(1)}, bf16[768,1024]{1,0:T(8,128)(2,1)S(1)}, u32[]{:S(2)}, u32[]{:S(2)}) collective-permute-start(bf16[768,1024]{1,0:T(8,128)(2,1)S(1)} %get-tuple-element.133), channel_id=1, source_target_pairs={{0,2},{1,3},{2,4},{3,5},{4,6},{5,7},{8,10},{9,11},{10,12},{11,13},... | collective-permute-start | bytes 4718600 | tf_op jit(solution)/shard_map/ppermute | solution.py:689
  538.2 44.4 %collective-permute-start.22 = (bf16[768,1024]{1,0:T(8,128)(2,1)S(1)}, bf16[768,1024]{1,0:T(8,128)(2,1)S(1)}, u32[]{:S(2)}, u32[]{:S(2)}) collective-permute-start(bf16[768,1024]{1,0:T(8,128)(2,1)S(1)} %get-tuple-element.132), channel_id=1, source_target_pairs={{2,0},{3,1},{4,2},{5,3},{6,4},{7,5},{10,8},{11,9},{12,10},{13,11},... | collective-permute-start | bytes 4718600 | tf_op jit(solution)/shard_map/ppermute | solution.py:689
  539.7 75.9 %collective-permute-start.27 = (bf16[384,1024]{1,0:T(8,128)(2,1)S(1)}, bf16[384,1024]{1,0:T(8,128)(2,1)S(1)}, u32[]{:S(2)}, u32[]{:S(2)}) collective-permute-start(bf16[384,1024]{1,0:T(8,128)(2,1)S(1)} %get-tuple-element.150), channel_id=1, source_target_pairs={{0,2},{8,5},{2,0},{10,3},{4,6},{12,1},{6,4},{14,7},{1,10},{9,13},{... | collective-permute-start | bytes 2359304 | tf_op jit(solution)/shard_map/ppermute | solution.py:693
  544.3 72.8 %collective-permute-start.26 = (bf16[384,1024]{1,0:T(8,128)(2,1)S(1)}, bf16[384,1024]{1,0:T(8,128)(2,1)S(1)}, u32[]{:S(2)}, u32[]{:S(2)}) collective-permute-start(bf16[384,1024]{1,0:T(8,128)(2,1)S(1)} %get-tuple-element.151), channel_id=1, source_target_pairs={{0,1},{8,4},{2,7},{10,2},{4,5},{12,0},{6,3},{14,6},{1,9},{9,12},{3... | collective-permute-start | bytes 2359304 | tf_op jit(solution)/shard_map/ppermute | solution.py:693
  544.9 72.1 %collective-permute-start.25 = (bf16[384,1024]{1,0:T(8,128)(2,1)S(1)}, bf16[384,1024]{1,0:T(8,128)(2,1)S(1)}, u32[]{:S(2)}, u32[]{:S(2)}) collective-permute-start(bf16[384,1024]{1,0:T(8,128)(2,1)S(1)} %get-tuple-element.149), channel_id=1, source_target_pairs={{0,0},{8,3},{2,6},{10,1},{4,4},{12,7},{6,2},{14,5},{1,8},{9,11},{3... | collective-permute-start | bytes 2359304 | tf_op jit(solution)/shard_map/ppermute | solution.py:693
  584.7 71.9 %collective-permute-start.24 = (bf16[768,1024]{1,0:T(8,128)(2,1)}, bf16[768,1024]{1,0:T(8,128)(2,1)}, u32[]{:S(2)}, u32[]{:S(2)}) collective-permute-start(bf16[768,1024]{1,0:T(8,128)(2,1)} %fusion.10), channel_id=1, source_target_pairs={{0,0},{8,1},{2,2},{10,3},{4,4},{12,5},{6,6},{14,7},{1,8},{9,9},{3,... | collective-permute-start | bytes 4718600 | tf_op jit(solution)/shard_map/ppermute | solution.py:690
  618.4 92.9 %all-gather.5.cloned.1.call-start = ((), (), s32[]{:S(2)}) async-start(), calls=%async_computation.4 | async-start | bytes 2949120 | tf_op jit(solution)/shard_map/all_gather | solution.py:733
  (40 other events, 436.8 us)
Sparse Core Ops, SparseCore 0:
  42.9 184.3 all-gather.2
  331.5 224.8 reduce-scatter.1
  618.5 32.0 all-reduce.4
  651.9 24.6 all-gather.4

commit v3 on v2

--- a/solution.py
+++ b/solution.py
@@ -55,105 +55,132 @@
     return cumulative, value * (bell * 0.3989422804014327)
 
 
-def project_kernel(slots, table_ref, own_ref, other_ref, w_ref, out_ref):
+def collect(items_s, pieces, table_ref, base, shards):
+    block = pieces[0].shape[1]
+    for i in range(shards):
+        for at, piece in enumerate(pieces):
+
+            @pl.when(table_ref[base + 2 * i] == at)
+            def _():
+                items_s[i * block : (i + 1) * block, :] = piece[table_ref[base + 2 * i + 1]]
+
+
+def project_kernel(shards, count, table_ref, w_ref, *refs):
+    pieces, out_ref, items_s = refs[:count], refs[count], refs[count + 1]
     step = pl.program_id(0)
-    count = pl.num_programs(0)
-    width = own_ref.shape[-1]
-    block = own_ref.shape[1]
-    here = jnp.where(step < count // 2, own_ref[0], other_ref[0])
-    for j in range(slots):
-
-        @pl.when(table_ref[step] == table_ref[2 * count + j])
-        def _():
-            bias = jnp.sum(w_ref[j, width : width + 3, :].astype(F32), 0, keepdims=True)
-            rows = pl.ds(pl.multiple_of(table_ref[count + step] * block, block), block)
-            out_ref[j, rows, :] = (mm(here, w_ref[j, :width, :]) + bias).astype(BF16)
-
-
-def project(own, other, weight, table, length):
-    half, block, width = own.shape
-    slots, _, cols = weight.shape
+    width = items_s.shape[1]
+    collect(items_s, pieces, table_ref, step * 2 * shards, shards)
+    bias = jnp.sum(w_ref[0, width : width + 3, :].astype(F32), 0, keepdims=True)
+    out_ref[0] = (mm(items_s[...], w_ref[0, :width, :]) + bias).astype(BF16)
+
+
+def whole(shape):
+    return pl.BlockSpec(shape, lambda *_: (0,) * len(shape))
+
+
+def project(pieces, weight, table, length, slots):
+    shards, depth, cols = weight.shape
+    width = pieces[0].shape[2]
+    at = 2 * shards * slots + slots
     return pl.pallas_call(
-        functools.partial(project_kernel, slots),
+        functools.partial(project_kernel, shards, len(pieces)),
         grid_spec=pltpu.PrefetchScalarGridSpec(
             num_scalar_prefetch=1,
-            grid=(2 * half,),
-            in_specs=[
-                pl.BlockSpec((1, block, width), lambda q, t: (jnp.minimum(q, half - 1), 0, 0)),
-                pl.BlockSpec((1, block, width), lambda q, t: (jnp.maximum(q - half, 0), 0, 0)),
-                pl.BlockSpec(weight.shape, lambda q, t: (0, 0, 0)),
-            ],
-            out_specs=pl.BlockSpec((slots, length, cols), lambda q, t: (0, 0, 0)),
+            grid=(slots,),
+            in_specs=[pl.BlockSpec((1, depth, cols), lambda j, t: (t[at + j], 0, 0))]
+            + [whole(piece.shape) for piece in pieces],
+            out_specs=pl.BlockSpec((1, length, cols), lambda j, t: (j, 0, 0)),
+            scratch_shapes=[pltpu.VMEM((length, width), BF16)],
         ),
         out_shape=jax.ShapeDtypeStruct((slots, length, cols), BF16),
         compiler_params=params(),
-        cost_estimate=cost(2 * slots * length * width * cols, own.size * 4 + slots * length * cols * 2),
-    )(table, own, other, weight)
-
-
-def project_back_kernel(slots, table_ref, own_ref, other_ref, w_ref, g_ref, own_dx, other_dx, dw_ref, dx_s, dw_s):
+        cost_estimate=cost(2 * slots * length * width * cols, len(pieces) * pieces[0].size * 2 + slots * length * cols * 2),
+    )(table, weight, *pieces)
+
+
+def weight_back_kernel(shards, count, table_ref, g_ref, *refs):
+    pieces, out_ref, items_s = refs[:count], refs[count], refs[count + 1]
+    collect(items_s, pieces, table_ref, pl.program_id(0) * 2 * shards, shards)
+    out_ref[0] = mm(g_ref[0], items_s[...], TN).astype(BF16)
+
+
+def weight_back(pieces, grad, table):
+    slots, length, cols = grad.shape
+    width = pieces[0].shape[2]
+    shards = length // pieces[0].shape[1]
+    return pl.pallas_call(
+        functools.partial(weight_back_kernel, shards, len(pieces)),
+        grid_spec=pltpu.PrefetchScalarGridSpec(
+            num_scalar_prefetch=1,
+            grid=(slots,),
+            in_specs=[pl.BlockSpec((1, length, cols), lambda j, t: (j, 0, 0))]
+            + [whole(piece.shape) for piece in pieces],
+            out_specs=pl.BlockSpec((1, cols, width), lambda j, t: (j, 0, 0)),
+            scratch_shapes=[pltpu.VMEM((length, width), BF16)],
+        ),
+        out_shape=jax.ShapeDtypeStruct((slots, cols, width), BF16),
+        compiler_params=params(),
+        cost_estimate=cost(2 * slots * length * width * cols, len(pieces) * pieces[0].size * 2 + slots * cols * width * 2),
+    )(table, grad, *pieces)
+
+
+def rows_back_kernel(shards, slots, count, table_ref, w_ref, g_ref, *refs):
+    outs, sum_s = refs[:count], refs[count]
+    block, width = outs[0].shape[1:]
     step = pl.program_id(0)
-    count = pl.num_programs(0)
-    width = own_ref.shape[-1]
-    block = own_ref.shape[1]
-    here = jnp.where(step < count // 2, own_ref[0], other_ref[0])
-    dx_s[...] = jnp.zeros_like(dx_s)
+    tail = 2 * shards * slots + step
+    first = jnp.logical_or(step == 0, table_ref[tail] != table_ref[jnp.maximum(tail - 1, 0)])
+    last = jnp.logical_or(
+        step == slots - 1, table_ref[tail] != table_ref[jnp.minimum(tail + 1, 2 * shards * slots + slots - 1)]
+    )
 
     @pl.when(step == 0)
     def _():
-        dw_s[...] = jnp.zeros_like(dw_s)
-
-    for j in range(slots):
-
-        @pl.when(table_ref[step] == table_ref[2 * count + j])
-        def _():
-            rows = pl.ds(pl.multiple_of(table_ref[count + step] * block, block), block)
-            grad = g_ref[j, rows, :]
-            dx_s[...] += mm(grad, w_ref[j, :width, :], NT)
-            dw_s[j] += mm(grad, here, TN)
-
-    @pl.when(step < count // 2)
+        for out in outs:
+            out[...] = jnp.zeros_like(out)
+
+    part = mm(g_ref[0], w_ref[0, :width, :], NT)
+
+    @pl.when(first)
     def _():
-        own_dx[0] = dx_s[...].astype(BF16)
-
-    @pl.when(step >= count // 2)
+        sum_s[...] = part
+
+    @pl.when(jnp.logical_not(first))
     def _():
-        other_dx[0] = dx_s[...].astype(BF16)
-
-    @pl.when(step == count - 1)
+        sum_s[...] += part
+
+    @pl.when(last)
     def _():
-        dw_ref[...] = dw_s[...].astype(BF16)
-
-
-def project_back(own, other, weight, grad, table):
-    half, block, width = own.shape
-    slots, length, cols = grad.shape
+        for i in range(shards):
+            base = step * 2 * shards + 2 * i
+            for at, out in enumerate(outs):
+
+                @pl.when(table_ref[base] == at)
+                def _():
+                    out[table_ref[base + 1]] = sum_s[i * block : (i + 1) * block, :].astype(BF16)
+
+
+def rows_back(grad, weight, table, block, count, blocks, width):
+    shards, depth, cols = weight.shape
+    slots, length = grad.shape[:2]
+    at = 2 * shards * slots + slots
+    piece = (blocks, block, width)
     return pl.pallas_call(
-        functools.partial(project_back_kernel, slots),
+        functools.partial(rows_back_kernel, shards, slots, count),
         grid_spec=pltpu.PrefetchScalarGridSpec(
             num_scalar_prefetch=1,
-            grid=(2 * half,),
+            grid=(slots,),
             in_specs=[
-                pl.BlockSpec((1, block, width), lambda q, t: (jnp.minimum(q, half - 1), 0, 0)),
-                pl.BlockSpec((1, block, width), lambda q, t: (jnp.maximum(q - half, 0), 0, 0)),
-                pl.BlockSpec(weight.shape, lambda q, t: (0, 0, 0)),
-                pl.BlockSpec(grad.shape, lambda q, t: (0, 0, 0)),
+                pl.BlockSpec((1, depth, cols), lambda j, t: (t[at + j], 0, 0)),
+                pl.BlockSpec((1, length, cols), lambda j, t: (j, 0, 0)),
             ],
-            out_specs=[
-                pl.BlockSpec((1, block, width), lambda q, t: (jnp.minimum(q, half - 1), 0, 0)),
-                pl.BlockSpec((1, block, width), lambda q, t: (jnp.maximum(q - half, 0), 0, 0)),
-                pl.BlockSpec((slots, cols, width), lambda q, t: (0, 0, 0)),
-            ],
-            scratch_shapes=[pltpu.VMEM((block, width), F32), pltpu.VMEM((slots, cols, width), F32)],
+            out_specs=[whole(piece)] * count,
+            scratch_shapes=[pltpu.VMEM((length, width), F32)],
         ),
-        out_shape=[
-            jax.ShapeDtypeStruct((half, block, width), BF16),
-            jax.ShapeDtypeStruct((half, block, width), BF16),
-            jax.ShapeDtypeStruct((slots, cols, width), BF16),
-        ],
+        out_shape=[jax.ShapeDtypeStruct(piece, BF16)] * count,
         compiler_params=params(),
-        cost_estimate=cost(4 * slots * length * width * cols, own.size * 8 + grad.size * 2),
-    )(table, own, other, weight, grad)
+        cost_estimate=cost(2 * slots * length * width * cols, count * blocks * block * width * 2 + grad.size * 2),
+    )(table, weight, grad)
 
 
 def attend_kernel(heads, block, place_ref, x_ref, ctx_ref, lse_ref, keys_s, values_s):
@@ -292,24 +319,31 @@
 
 
 def feed_kernel(
-    parts, x_ref, g_ref, widen_ref, narrow_ref, bias_ref, out_ref, dx_ref, grads_ref, bias_grad_ref, out_s, dx_s
+    parts, x_ref, g_ref, widen_ref, narrow_ref, bias_ref, out_ref, dx_ref, hidden_ref, pre_ref, bias_grad_ref, out_s, dx_s
 ):
     step = pl.program_id(0)
-    count, depth, tile = widen_ref.shape[1:]
-    width = count * depth
+    some, count, depth, tile = widen_ref.shape
     piece = depth // parts
-    widen = widen_ref[0].reshape(width, tile)
-    normed = x_ref[...]
-    grad = g_ref[...]
-    narrow = [
-        narrow_ref[0, :, c * piece : (c + 1) * piece, :].reshape(tile, tile) for c in range(parts)
-    ]
-    narrow = jnp.concatenate(narrow, 1)
-    bias = jnp.sum(bias_ref[0, 0, 0:3, :].astype(F32), 0, keepdims=True)
-    pre = mm(normed, widen) + bias
+    widen = jnp.concatenate([widen_ref[a].reshape(count * depth, tile) for a in range(some)], 1)
+    narrow = jnp.concatenate(
+        [
+            jnp.concatenate(
+                [narrow_ref[a, :, c * piece : (c + 1) * piece, :].reshape(tile, tile) for c in range(parts)], 1
+            )
+            for a in range(some)
+        ],
+        0,
+    )
+    bias = jnp.concatenate(
+        [jnp.sum(bias_ref[a, 0, 0:3, :].astype(F32), 0, keepdims=True) for a in range(some)], 1
+    )
+    pre = mm(x_ref[...], widen) + bias
     cumulative, slope = gelu_parts(pre)
     hidden = (pre * cumulative).astype(BF16)
-    grad_pre = (mm(grad, narrow, NT) * (cumulative + slope)).astype(BF16)
+    grad_pre = (mm(g_ref[...], narrow, NT) * (cumulative + slope)).astype(BF16)
+    hidden_ref[0] = hidden
+    pre_ref[0] = grad_pre
+    bias_grad_ref[0] = jnp.sum(grad_pre.astype(F32), 0, keepdims=True)
     out = mm(hidden, narrow)
     dx = mm(grad_pre, widen, NT)
 
@@ -323,48 +357,81 @@
         out_s[...] += out
         dx_s[...] += dx
 
-    grads_ref[0, :, :piece, :] = mm(grad_pre, normed, TN).astype(BF16).reshape(count, tile // count, width)
-    grads_ref[0, :, piece:, :] = mm(hidden, grad, TN).astype(BF16).reshape(count, tile // count, width)
-    bias_grad_ref[0] = jnp.sum(grad_pre.astype(F32), 0, keepdims=True)
-
     @pl.when(step == pl.num_programs(0) - 1)
     def _():
-        out_ref[...] = out_s[...]
-        dx_ref[...] = dx_s[...]
-
-
-def feed(normed, grad, rest, bias_at, extra):
+        out_ref[...] = out_s[...].astype(out_ref.dtype)
+        dx_ref[...] = dx_s[...].astype(dx_ref.dtype)
+
+
+def feed(normed, grad, rest, bias_at, some, dtype):
     shards, count, _, tile = rest.shape
     rows, width = normed.shape
     depth = width // count
     parts = width // tile
-    piece = tile // count
+    steps = shards // some
+    unit_spec = pl.BlockSpec((1, rows, some * tile), lambda m: (m, 0, 0))
     return pl.pallas_call(
         functools.partial(feed_kernel, parts),
-        grid=(shards,),
+        grid=(steps,),
         in_specs=[
-            pl.BlockSpec((rows, width), lambda m: (0, 0)),
-            pl.BlockSpec((rows, width), lambda m: (0, 0)),
-            pl.BlockSpec((1, count, depth, tile), lambda m: (m, 0, 0, 0)),
-            pl.BlockSpec((1, count, depth, tile), lambda m: (m, 0, 1, 0)),
-            pl.BlockSpec((1, 1, 16, tile), lambda m: (m, 0, bias_at // 16, 0)),
+            whole((rows, width)),
+            whole((rows, width)),
+            pl.BlockSpec((some, count, depth, tile), lambda m: (m, 0, 0, 0)),
+            pl.BlockSpec((some, count, depth, tile), lambda m: (m, 0, 1, 0)),
+            pl.BlockSpec((some, 1, 16, tile), lambda m: (m, 0, bias_at // 16, 0)),
         ],
         out_specs=[
-            pl.BlockSpec((rows, width), lambda m: (0, 0)),
-            pl.BlockSpec((rows, width), lambda m: (0, 0)),
-            pl.BlockSpec((1, count, 2 * piece, width), lambda m: (m, 0, 0, 0)),
-            pl.BlockSpec((1, 1, tile), lambda m: (m, 0, 0)),
+            whole((rows, width)),
+            whole((rows, width)),
+            unit_spec,
+            unit_spec,
+            pl.BlockSpec((1, 1, some * tile), lambda m: (m, 0, 0)),
         ],
         out_shape=[
-            jax.ShapeDtypeStruct((rows, width), F32),
-            jax.ShapeDtypeStruct((rows, width), F32),
-            jax.ShapeDtypeStruct((shards, count, 2 * piece + extra, width), BF16),
-            jax.ShapeDtypeStruct((shards, 1, tile), F32),
+            jax.ShapeDtypeStruct((rows, width), dtype),
+            jax.ShapeDtypeStruct((rows, width), dtype),
+            jax.ShapeDtypeStruct((steps, rows, some * tile), BF16),
+            jax.ShapeDtypeStruct((steps, rows, some * tile), BF16),
+            jax.ShapeDtypeStruct((steps, 1, some * tile), F32),
         ],
         scratch_shapes=[pltpu.VMEM((rows, width), F32), pltpu.VMEM((rows, width), F32)],
         compiler_params=params(),
-        cost_estimate=cost(12 * shards * rows * width * tile, rest.size * 4 + rows * width * 12, rows * shards * tile),
+        cost_estimate=cost(8 * shards * rows * width * tile, rest.size * 2 + rows * width * 28, rows * shards * tile),
     )(normed, grad, rest, rest, rest)
+
+
+def feed_grads_kernel(*refs):
+    out_ref = refs[-1]
+    some, count, both, width = out_ref.shape
+    piece = both // 2
+    widen = narrow = 0.0
+    for at in range(0, len(refs) - 1, 4):
+        x_ref, g_ref, hidden_ref, pre_ref = refs[at : at + 4]
+        widen += mm(pre_ref[0], x_ref[...], TN)
+        narrow += mm(hidden_ref[0], g_ref[...], TN)
+    out_ref[:, :, :piece, :] = widen.astype(BF16).reshape(some, count, piece, width)
+    out_ref[:, :, piece:, :] = narrow.astype(BF16).reshape(some, count, piece, width)
+
+
+def feed_grads(feed_parts, count, some, extra):
+    steps, _, tiles = feed_parts[0][2].shape
+    width = feed_parts[0][0].shape[1]
+    both = 2 * tiles // some // count
+    specs, rows_all = [], 0
+    for part in feed_parts:
+        rows = part[0].shape[0]
+        rows_all += rows
+        unit_spec = pl.BlockSpec((1, rows, tiles), lambda m: (m, 0, 0))
+        specs += [whole((rows, width)), whole((rows, width)), unit_spec, unit_spec]
+    return pl.pallas_call(
+        feed_grads_kernel,
+        grid=(steps,),
+        in_specs=specs,
+        out_specs=pl.BlockSpec((some, count, both, width), lambda m: (m, 0, 0, 0)),
+        out_shape=jax.ShapeDtypeStruct((steps * some, count, both + extra, width), BF16),
+        compiler_params=params(),
+        cost_estimate=cost(4 * steps * rows_all * width * tiles, steps * rows_all * tiles * 4 + steps * tiles * width * 4),
+    )(*[array for part in feed_parts for array in part])
 
 
 def merge_kernel(shards, slots, place_ref, got_ref, w_ref, start_ref, vec_ref, ctx_ref, middle_ref, normed_ref):
@@ -455,9 +522,9 @@
     )
 
 
-def split_rows(array, count):
+def share_of(array, at, count):
     share = array.shape[0] // count
-    return lax.dynamic_slice_in_dim(array, lax.axis_index("dp") * share, share, 0)
+    return lax.dynamic_slice_in_dim(array, at * share, share, 0)
 
 
 def on_device(
@@ -492,8 +559,10 @@
     cols = heads_weight.shape[1]
     heads_here = cols // (3 * HEAD_DIM)
     wide = heads_here * HEAD_DIM
-    tile = widen_weight.shape[1]
+    tile = widen_weight.shape[1] // 2
     parts = width // tile
+    count = copies // 2
+    some = 2
     dp_at = lax.axis_index("dp")
     mp_at = lax.axis_index("mp")
     both = ("dp", "mp")
@@ -514,73 +583,119 @@
             for j in range(slots)
         )
 
-    swap = [(row_device(g, k), attention_device(g, k)) for g in groups for k in spots]
     core_swap = [(g, g + 1 - g % 2 * 2) for g in groups]
+    half_swap = [(g, g ^ 2) for g in groups]
+    half_at = dp_at // 2 % 2
+    piece_at = dp_at // 4 * 2 + dp_at % 2
+    plane = [[k * copies + g for k in spots for g in groups if g // 2 % 2 == h] for h in range(2)]
+    row_swap = [(k, k + 1 - k % 2 * 2) for k in spots]
     reach = max(abs(a // 2 - b // 2) for a in spots for b in spots if meet(a, b))
-    shifts = [
-        s for s in range(1 - shards, shards) if any(0 <= k + s < shards and meet(k + s, k) for k in spots)
-    ]
-    lowest = shifts[0]
+    classes = []
+    for s in sorted(range(1 - shards, shards), key=abs):
+        pairs = [(k, k + s) for k in spots if 0 <= k + s < shards and meet(k + s, k)]
+        for known in classes:
+            if not any(a == c or b == d for a, b in pairs for c, d in known):
+                known += pairs
+                break
+        else:
+            if pairs:
+                classes.append(pairs)
+    color = [[0] * shards for _ in spots]
+    senders = [[0] * shards for _ in classes]
+    for i, pairs in enumerate(classes):
+        for unit, rows in pairs:
+            color[unit][rows] = i
+            senders[i][rows] = unit
+    color = jnp.asarray(color, jnp.int32)
+    senders = jnp.asarray(senders, jnp.int32)
+
+    def extents(pairs):
+        ranges = []
+        for unit, rows in pairs:
+            shared = [
+                (j, b)
+                for j in range(slots)
+                for b in range(slots)
+                if (slots * rows + b) // shards == (slots * unit + j) // shards
+            ]
+            ranges.append([(min(part), max(part) + 1) for part in zip(*shared)])
+        sizes = [max(r[at][1] - r[at][0] for r in ranges) for at in range(2)]
+        unit_starts = [[0] * shards for _ in range(2)]
+        row_starts = [[0] * shards for _ in range(2)]
+        for (unit, rows), r in zip(pairs, ranges):
+            for at in range(2):
+                unit_starts[at][unit] = row_starts[at][rows] = min(r[at][0], slots - sizes[at])
+        return sizes, unit_starts, row_starts
+
+    def exchange(array, to_rows):
+        got = []
+        for i, pairs in enumerate(classes):
+            sizes, unit_starts, row_starts = extents(pairs)
+            ends = [(attention_device(g, unit), row_device(g, rows)) for g in groups for unit, rows in pairs]
+            ends = ends if to_rows else back(ends)
+            message = array[i]
+            if sizes == [slots, slots]:
+                got.append(lax.ppermute(message, both, ends))
+                continue
+            at_unit = [jnp.asarray(part, jnp.int32)[k_here] for part in unit_starts]
+            at_rows = [jnp.asarray(part, jnp.int32)[mp_at] for part in row_starts]
+            at_from, at_to = (at_unit, at_rows) if to_rows else (at_rows, at_unit)
+            some_part = lax.dynamic_slice(message, (*at_from, 0, 0), (*sizes, *message.shape[2:]))
+            some_part = lax.ppermute(some_part, both, ends)
+            got.append((some_part, at_to))
+        return got
+
+    def together(got, shape):
+        whole_ones = [
+            lax.dynamic_update_slice(jnp.zeros(shape, BF16), part[0], (*part[1], 0, 0))
+            if isinstance(part, tuple)
+            else part
+            for part in got
+        ]
+        return jnp.stack(whole_ones).reshape(-1, *shape[2:])
 
     def far(step):
         return [
-            (k, k + 2 * step)
+            (attention_device(g, k), row_device(g, k + 2 * step))
+            for g in groups
             for k in spots
-            if 0 <= k + 2 * step < shards
-            and any(
-                meet(k // 2 * 2 + a, (k // 2 + step) * 2 + b) or meet((k // 2 + step) * 2 + b, k // 2 * 2 + a)
-                for a in range(2)
-                for b in range(2)
-            )
+            if 0 <= k + 2 * step < shards and any(meet(k + 2 * step, k // 2 * 2 + b) for b in range(2))
         ]
 
-    steps = [o for o in range(-reach, reach + 1) if o != 0]
+    def back(pairs):
+        return [(b, a) for a, b in pairs]
+
+    steps = range(-reach, reach + 1)
 
     k_here = mp_at // 2 * 2 + dp_at % 2
     unit_ids = slots * k_here + jnp.arange(slots, dtype=jnp.int32)
     unit_items = unit_ids // shards
-    offsets = jnp.arange(-reach, reach + 1, dtype=jnp.int32)
-    pair_at = mp_at // 2 + offsets
-    core_at = jnp.stack([dp_at % 2, 1 - dp_at % 2]).astype(jnp.int32)
-    seen = (pair_at[None, :] * 2 + core_at[:, None])[:, :, None] * slots + jnp.arange(slots, dtype=jnp.int32)
-    seen_ok = jnp.broadcast_to(((pair_at >= 0) & (pair_at < shards // 2))[None, :, None], seen.shape)
-    table = jnp.concatenate(
+    unit_blocks = unit_items[:, None] * shards + jnp.arange(shards, dtype=jnp.int32)[None, :]
+    block_spots = unit_blocks // slots
+    table = jnp.stack(
         [
-            jnp.where(seen_ok, seen // shards, -1).reshape(-1),
-            jnp.where(seen_ok, seen % shards, 0).reshape(-1),
-            unit_items,
-        ]
-    ).astype(jnp.int32)
-    unit_blocks = unit_items[:, None] * shards + jnp.arange(shards, dtype=jnp.int32)[None, :]
+            (block_spots + dp_at) % 2,
+            (block_spots // 2 - mp_at // 2 + reach) * slots + unit_blocks % slots,
+        ],
+        2,
+    )
+    table = jnp.concatenate([table.reshape(-1), unit_items, unit_ids % shards]).astype(jnp.int32)
+    counting = jnp.arange(slots, dtype=jnp.int32)
     unit_places = (
-        ((unit_blocks // slots - k_here - lowest) * slots + jnp.arange(slots, dtype=jnp.int32)[:, None]) * slots
-        + unit_blocks % slots
+        (color[k_here, block_spots] * slots + counting[:, None]) * slots + unit_blocks % slots
     ).reshape(-1)
-    row_units = (
-        (slots * mp_at + jnp.arange(slots, dtype=jnp.int32)) // shards * shards
-    )[:, None] + jnp.arange(shards, dtype=jnp.int32)[None, :]
+    row_units = ((slots * mp_at + counting) // shards * shards)[:, None] + jnp.arange(
+        shards, dtype=jnp.int32
+    )[None, :]
     row_places = (
-        ((mp_at - row_units // slots - lowest) * slots + row_units % slots) * slots
-        + jnp.arange(slots, dtype=jnp.int32)[:, None]
+        (color[row_units // slots, mp_at] * slots + row_units % slots) * slots + counting[:, None]
     ).reshape(-1)
-    ends = mp_at - jnp.asarray(shifts, jnp.int32)
-    wanted = ((slots * ends[:, None] + jnp.arange(slots, dtype=jnp.int32)[None, :]) % shards).reshape(-1)
-
-    def shift_pairs(s):
-        return [
-            (attention_device(g, k), row_device(g, k + s))
-            for g in groups
-            for k in spots
-            if 0 <= k + s < shards and meet(k + s, k)
-        ]
+    wanted = ((slots * senders[:, mp_at][:, None] + counting[None, :]) % shards).reshape(-1)
 
     def weight_pairs(j):
         return [
             (g * shards + (slots * k + j) % shards, attention_device(g, k)) for g in groups for k in spots
         ]
-
-    def back(pairs):
-        return [(b, a) for a, b in pairs]
 
     row_ids = mp_at * rows_here + jnp.arange(rows_here, dtype=jnp.int32)
     slot_ids = jnp.arange(slots, dtype=jnp.int32)
@@ -591,60 +706,61 @@
     set_match = (dataset_ids[:, None] == set_ids[None, :]).astype(F32)
     item_weight = live * jnp.sum(set_match * set_weights[None, :], 1)
     row_weight = jnp.sum(slot_table * item_weight[None, :], 1)
-    item_total = lax.psum(group_items.astype(F32)[0], "dp")
 
     start_state = tokens + lead_scaled[:, None] * lead_weight + lead_shift
     first_normal, first_scale = norm_parts(start_state)
     normed_one = (first_normal * norm_one_gain + norm_one_shift).astype(BF16)
 
-    def exact_rows(vector):
+    def exact_rows(vector, pad):
         high = vector.astype(BF16)
         left = vector - high.astype(F32)
         middle = left.astype(BF16)
         low = (left - middle.astype(F32)).astype(BF16)
-        return jnp.pad(jnp.stack([high, middle, low]), ((0, 13), (0, 0)))
+        return jnp.pad(jnp.stack([high, middle, low]), ((0, pad - 3), (0, 0)))
 
     bias_heads = heads_bias.reshape(heads_here, 2, HEAD_DIM)
     full_bias = jnp.stack(
         [bias_heads[:, 0], jnp.zeros_like(bias_heads[:, 0]), bias_heads[:, 1]], 1
     ).reshape(-1)
-    heads_rows = jnp.concatenate([heads_weight, exact_rows(full_bias)], 0)
-    unit_weights = jnp.stack([lax.ppermute(heads_rows, both, weight_pairs(j)) for j in range(slots)])
+    heads_rows = jnp.concatenate([heads_weight, exact_rows(full_bias, 16 * count)], 0)
+    heads_all = lax.all_gather(
+        share_of(heads_rows, piece_at, count), BOTH, axis=0, tiled=True, axis_index_groups=plane
+    ).reshape(shards, -1, cols)
 
     def fold(part):
         return jnp.concatenate(jnp.split(part, parts, 1), 0)
 
     rest = jnp.concatenate(
         [
-            split_rows(widen_weight, copies),
-            fold(split_rows(narrow_weight, copies)),
-            fold(split_rows(merge_weight, copies)),
-            exact_rows(widen_bias),
+            share_of(lax.dynamic_slice_in_dim(widen_weight, half_at * tile, tile, 1), piece_at, count),
+            fold(share_of(share_of(narrow_weight, half_at, 2), piece_at, count)),
+            fold(share_of(merge_weight, piece_at, count)),
+            exact_rows(share_of(widen_bias, half_at, 2), 16),
         ],
         0,
     )
-    merge_rows = merge_weight.shape[0] // copies
-    merge_at = 2 * (width // copies)
+    merge_rows = merge_weight.shape[0] // count
+    merge_at = 2 * (width // count)
     bias_at = merge_at + merge_rows * parts
 
-    mine = lax.ppermute(normed_one, both, swap)
-    around = {o: lax.ppermute(mine, "mp", far(-o)) for o in steps}
-    around[0] = mine
-    own = jnp.stack([around[o] for o in range(-reach, reach + 1)])
-    own, rest = lax.optimization_barrier((own, rest))
-    rest = lax.all_gather(rest, BOTH, axis=0, tiled=True)
-    rest = rest.reshape(shards, copies, -1, tile)
-    other = lax.ppermute(own, "dp", core_swap).reshape(-1, block, width)
-    own = own.reshape(-1, block, width)
-
-    packed = project(own, other, unit_weights, table, length)
-    messages = len(shifts) * slots * slots
+    own = jnp.stack([lax.ppermute(normed_one, both, back(far(o))) for o in steps])
+    grad_out = cotangent * row_weight[:, None]
+    grad_low = grad_out.astype(BF16)
+    own, rest, grad_low, live_items = lax.optimization_barrier((own, rest, grad_low, group_items))
+    item_total = lax.psum(live_items.astype(F32)[0], "dp")
+    rest = lax.all_gather(rest, BOTH, axis=0, tiled=True, axis_index_groups=plane)
+    rest = rest.reshape(shards, count, -1, tile)
+    their_grad = lax.ppermute(grad_low, "dp", half_swap)
+    other = lax.ppermute(own, "dp", core_swap)
+    other, item_total = lax.optimization_barrier((other, item_total))
+    pieces = [part.reshape(-1, block, width) for part in (own, other)]
+
+    packed = project(pieces, heads_all, table, length, slots)
+    messages = len(classes) * slots * slots
+    message = (slots, slots, block, wide)
     context, lse = attend(packed, heads_here, block, unit_places, messages)
-    context_out = context.reshape(len(shifts), slots * slots * block, wide)
-    context_got = jnp.stack(
-        [lax.ppermute(context_out[i], both, shift_pairs(s)) for i, s in enumerate(shifts)]
-    ).reshape(messages, block, wide)
-    merge_all = rest[:, :, merge_at:bias_at, :].reshape(shards, copies, parts, merge_rows, tile)
+    context_got = together(exchange(context.reshape(-1, *message), True), message)
+    merge_all = rest[:, :, merge_at:bias_at, :].reshape(shards, count, parts, merge_rows, tile)
     merge_all = merge_all.transpose(0, 1, 3, 2, 4).reshape(width, width)
     merge_vectors = jnp.pad(jnp.stack([merge_bias, norm_two_gain, norm_two_shift]), ((0, 5), (0, 0)))
     context_rows, middle, normed_two = merge(
@@ -652,47 +768,73 @@
     )
     second_normal, second_scale = norm_parts(middle)
 
-    grad_out = cotangent * row_weight[:, None]
-    grad_low = grad_out.astype(BF16)
     narrow_bias_grad = jnp.sum(grad_low.astype(F32), 0)
-    fed, grad_norm_two, grads_one, widen_bias_grad = feed(normed_two, grad_low, rest, bias_at, merge_rows)
-    activations = middle + fed + narrow_bias
+    chunk = rows_here // 2
+    chunks = [slice(0, chunk), slice(chunk, rows_here)]
+    their_normed = [lax.ppermute(normed_two[rows], "dp", half_swap) for rows in chunks]
+    fed, grad_norm_two, hidden, grad_pre, widen_bias_grad = feed(
+        normed_two, grad_low, rest, bias_at, some, F32
+    )
+    feed_parts = [(normed_two, grad_low, hidden, grad_pre)]
+    their_fed, their_dx = [], []
+    for i, rows in enumerate(chunks):
+        their_normed[i], fed = lax.optimization_barrier((their_normed[i], fed))
+        their = (their_normed[i], their_grad[rows])
+        part_fed, part_dx, hidden, grad_pre, part_bias = feed(*their, rest, bias_at, some, BF16)
+        feed_parts.append(their + (hidden, grad_pre))
+        widen_bias_grad += part_bias
+        their_fed.append(part_fed)
+        their_dx.append(lax.ppermute(part_dx, "dp", half_swap))
+        fed = lax.optimization_barrier((fed, part_dx))[0]
+    their_dx[-1], *their_fed = lax.optimization_barrier((their_dx[-1], *their_fed))
+    grad_norm_two = grad_norm_two + jnp.concatenate(their_dx).astype(F32)
+    their_fed = lax.ppermute(jnp.concatenate(their_fed), "dp", half_swap)
+    widen_bias_grad = widen_bias_grad.reshape(shards, 1, tile)
+    widen_bias_grad = jnp.where(
+        jnp.arange(2, dtype=jnp.int32)[None, :, None] == half_at, widen_bias_grad, 0.0
+    )
     grad_mid_norm, norm_two_gain_grad, norm_two_shift_grad = norm_back(
         second_normal, second_scale, norm_two_gain, grad_norm_two
     )
     grad_middle = grad_out + grad_mid_norm
     grad_mid_low = grad_middle.astype(BF16)
     merge_bias_grad = jnp.sum(grad_mid_low.astype(F32), 0)
+    grad_context = merge_back(grad_mid_low, merge_all, wanted, wide)
+    grad_context = exchange(grad_context.reshape(-1, *message), False)
+    first = feed_parts[0][:2]
+    grad_context[0], *hold = lax.optimization_barrier((grad_context[0], *feed_parts[0][2:]))
+    feed_parts[0] = first + tuple(hold)
+    grads_one = feed_grads(feed_parts, count, some, merge_weight.shape[0] // copies)
+    grad_context[1], grads_one = lax.optimization_barrier((grad_context[1], grads_one))
+    grad_context = together(grad_context, message)
     merge_weight_grad = mm(context_rows, grad_mid_low, TN).astype(BF16)
-    grads_one = grads_one.at[:, :, -merge_rows:].set(
-        merge_weight_grad.reshape(shards, copies, merge_rows, width)
+    merge_weight_grad = merge_weight_grad.reshape(shards, copies // 4, 2, 2, -1, width)
+    kept = lax.dynamic_index_in_dim(merge_weight_grad, half_at, 2, False)
+    sent = lax.dynamic_index_in_dim(merge_weight_grad, 1 - half_at, 2, False)
+    kept = kept.astype(F32) + lax.ppermute(sent, "dp", half_swap).astype(F32)
+    grads_one = grads_one.at[:, :, 2 * (tile // count) :].set(
+        kept.astype(BF16).reshape(shards, count, -1, width)
     )
     grads_one = lax.psum_scatter(
-        grads_one.reshape(-1, width), BOTH, scatter_dimension=0, tiled=True
-    )
-    grad_context = merge_back(grad_mid_low, merge_all, wanted, wide).reshape(
-        len(shifts), slots * rows_here, wide
-    )
-    grad_context = jnp.stack(
-        [lax.ppermute(grad_context[i], both, back(shift_pairs(s))) for i, s in enumerate(shifts)]
-    ).reshape(messages, block, wide)
+        grads_one.reshape(-1, width), BOTH, scatter_dimension=0, tiled=True, axis_index_groups=plane
+    )
     grad_packed, unit_sums = attend_back(
         packed, context, grad_context, lse, heads_here, block, unit_places
     )
-    own_dx, other_dx, unit_grads = project_back(own, other, unit_weights, grad_packed, table)
-
-    spans = 2 * reach + 1
-    other_dx = lax.ppermute(other_dx.reshape(spans, rows_here, width), "dp", core_swap)
-    pair_dx = own_dx.reshape(spans, rows_here, width).astype(F32) + other_dx.astype(F32)
-    mine_dx = pair_dx[reach]
-    for o in steps:
-        mine_dx += lax.ppermute(pair_dx[reach + o].astype(BF16), "mp", far(o)).astype(F32)
-    grad_norm_one = lax.ppermute(mine_dx.astype(BF16), both, back(swap)).astype(F32)
-
-    heads_total = sum(
-        lax.ppermute(unit_grads[j], both, back(weight_pairs(j))).astype(F32) for j in range(slots)
-    )
-    heads_total = lax.psum(heads_total.astype(BF16), "dp").astype(F32)
+    grad_packed, their_fed = lax.optimization_barrier((grad_packed, their_fed))
+    activations = middle + fed + their_fed.astype(F32) + narrow_bias
+    own_dx, other_dx = rows_back(grad_packed, heads_all, table, block, 2, len(steps) * slots, width)
+
+    other_dx = lax.ppermute(other_dx, "dp", core_swap).reshape(-1, rows_here, width)
+    own_dx = own_dx.reshape(-1, rows_here, width)
+    pair_dx = [(own_dx[i].astype(F32) + other_dx[i].astype(F32)).astype(BF16) for i in range(len(steps))]
+    grad_packed, *pair_dx = lax.optimization_barrier((grad_packed, *pair_dx))
+    grad_norm_one = [lax.ppermute(pair_dx[i], both, far(o)) for i, o in enumerate(steps)]
+
+    unit_grads = weight_back(pieces, grad_packed, table)
+    grad_norm_one[-1], unit_grads = lax.optimization_barrier((grad_norm_one[-1], unit_grads))
+    grad_norm_one = sum(part.astype(F32) for part in grad_norm_one)
+    heads_parts = [lax.ppermute(unit_grads[j], both, back(weight_pairs(j))) for j in range(slots)]
     heads_bias_grad = jnp.sum(
         jnp.where(
             (unit_ids % shards)[:, None, None] == jnp.arange(shards, dtype=jnp.int32)[None, :, None],
@@ -721,21 +863,37 @@
     vectors = jnp.concatenate(
         [jnp.stack(vectors).reshape(-1), widen_bias_grad.reshape(-1), heads_bias_grad.reshape(-1)]
     )
-    vectors = lax.psum(vectors, ("dp", "mp")) / item_total
+    hops = [
+        (axis, [(i, i ^ 1 << bit) for i in range(size)])
+        for axis, size in (("dp", copies), ("mp", shards))
+        for bit in range((size - 1).bit_length())
+    ]
+    heads_total = None
+    for at, (axis, pairs) in enumerate(hops):
+        vectors += lax.ppermute(vectors, axis, pairs)
+        if at == 0:
+            vectors, *heads_parts = lax.optimization_barrier((vectors, *heads_parts))
+            heads_total = sum(part.astype(F32) for part in heads_parts).astype(BF16)
+        elif at <= (copies - 1).bit_length():
+            axis, pairs = hops[at - 1]
+            over = lax.ppermute(heads_total, axis, pairs)
+            heads_total = (heads_total.astype(F32) + over.astype(F32)).astype(BF16)
+    vectors, heads_total = lax.optimization_barrier((vectors / item_total, heads_total))
+    heads_total = heads_total.astype(F32)
     shared = vectors[: 8 * width].reshape(8, width)
     place = lax.axis_index("mp")
-    widen_bias_total = lax.dynamic_slice_in_dim(vectors, 8 * width + place * tile, tile, 0)
+    widen_bias_total = lax.dynamic_slice_in_dim(vectors, 8 * width + place * 2 * tile, 2 * tile, 0)
     heads_bias_total = lax.dynamic_slice_in_dim(
-        vectors, 8 * width + shards * tile + place * cols, cols, 0
+        vectors, 8 * width + shards * 2 * tile + place * cols, cols, 0
     ).reshape(heads_here, 3, HEAD_DIM)
     heads_bias_total = jnp.stack([heads_bias_total[:, 0], heads_bias_total[:, 2]], 1).reshape(-1)
 
     grads_one = lax.all_gather(grads_one, "dp", axis=0, tiled=True).astype(F32) / item_total
-    grads_one = grads_one.reshape(copies, -1, width)
-    piece = tile // copies
-    widen_total = grads_one[:, :piece].reshape(tile, width).T
-    narrow_total = grads_one[:, piece : 2 * piece].reshape(tile, width)
-    merge_total = grads_one[:, 2 * piece :].reshape(-1, width)
+    piece = tile // count
+    grads_one = grads_one.reshape(copies // 4, 2, 2, -1, width).transpose(1, 0, 2, 3, 4)
+    widen_total = grads_one[:, :, :, :piece].reshape(2 * tile, width).T
+    narrow_total = grads_one[:, :, :, piece : 2 * piece].reshape(2 * tile, width)
+    merge_total = grads_one[:, :, :, 2 * piece :].transpose(1, 0, 2, 3, 4).reshape(-1, width)
     heads_total = heads_total.T / item_total
     return (
         activations,

time: 735 us -> 666 us (0.906)
  waiting for transfers between devices: 165 us -> 103 us
  blocking collectives: 47.3 us -> 10.7 us
  between operations: 15.5 us -> 23.6 us
    ppermute x28 -> x37, waiting for transfers between devices: 141 us -> 103 us  [the longest x3 35.4 us: on_device(): lax.ppermute(normed_one, both, back(far(o)))]
    psum x2 -> x1, blocking collectives: 47.3 us -> 10.7 us  [on_device(): item_total = lax.psum(live_items.astype(F32)[0], 'dp')]
    psum x1 -> x0, waiting for transfers between devices: 24.1 us -> none  [on_device(): heads_total = lax.psum(heads_total.astype(BF16), 'dp').astype(F32)]
    another operation x5 -> x3, other arithmetic: 14.2 us -> 5.15 us  [the longest x1 5.12 us: on_device(): jnp.stack([lax.ppermute(normed_one, both, back(far(o))) for o in steps])]
    convert_element_type x2 -> x6, other arithmetic: 3.43 us -> 11.8 us  [the longest x1 5.46 us: on_device(): (own_dx[i].astype(F32) + other_dx[i].astype(F32)).astype(BF16)]
    pallas_call x3 -> x7, Pallas kernels: 114 us -> 122 us  [the longest x3 56.1 us: feed(): pl.pallas_call(functools.partial(feed_kernel, parts), grid=(steps,), in_s...]
    ppermute x28 -> x37, starting transfers between devices: 131 us -> 135 us  [the longest x10 43 us: exchange(): got.append(lax.ppermute(message, both, ends))]
    unnamed x85 -> x111, local copies, waits for them, and re-layouts: 24.6 us -> 24.2 us
  transfers between devices with their start and end apart: 32 -> 41, of which waited for: 14 -> 11; matrix products, arithmetic and copies ran while one was open for 9% -> 12% of each run, Pallas kernels for 26% -> 38%
where the time goes in v3:
time: 666 us; the launch traced here: 655 us
  Pallas kernels  265 us (40%)
  starting transfers between devices  135 us (20%)
  waiting for transfers between devices  103 us (15%)
  other arithmetic  63.2 us (9%)
  local copies, waits for them, and re-layouts  51.8 us (8%)
  between operations  23.6 us (4%)
  blocking collectives  10.7 us (2%)
    pallas_call x1, Pallas kernels, attend_back(): pl.pallas_call(functools.partial(attend_back_kernel, heads, block), grid_...  79.2 us
    pallas_call x3, Pallas kernels, feed(): pl.pallas_call(functools.partial(feed_kernel, parts), grid=(steps,), in_s...  56.1 us
    pallas_call x1, Pallas kernels, attend(): pl.pallas_call(functools.partial(attend_kernel, heads, block), grid_spec=...  48.2 us
    ppermute x10, starting transfers between devices, exchange(): got.append(lax.ppermute(message, both, ends))  43 us
    ppermute x3, waiting for transfers between devices, on_device(): lax.ppermute(normed_one, both, back(far(o)))  35.4 us
    ppermute x3, starting transfers between devices, on_device(): lax.ppermute(pair_dx[i], both, far(o))  24.8 us
    unnamed x111, local copies, waits for them, and re-layouts  24.2 us
    pallas_call x1, Pallas kernels, feed_grads(): pl.pallas_call(feed_grads_kernel, grid=(steps,), in_specs=specs, out_spec...  21.7 us
  transfers between devices with their start and end apart: 41, of which 11 were waited for; matrix products, arithmetic and copies ran while one was open for 12% of the time, Pallas kernels for 38%

profile of v3, /device:TPU:0, one launch (start us, length us, event | category | flops | bytes accessed | tf_op | source)
XLA Modules:
  0.0 654.6 jit_solution(4762899018670002298)
XLA Ops:
  19.2 13.3 %collective-permute-start.1 = (bf16[768,1024]{1,0:T(8,128)(2,1)}, bf16[768,1024]{1,0:T(8,128)(2,1)}, u32[]{:S(2)}, u32[]{:S(2)}) collective-permute-start(bf16[768,1024]{1,0:T(8,128)(2,1)} %add_convert_fusion.3), channel_id=1, source_target_pairs={{0,0},{1,8},{2,2},{3,10},{4,4},{5,12},{6,6},{7,14},{8,1},{9,9},{10... | collective-permute-start | bytes 4718600 | tf_op jit(solution)/shard_map/ppermute | solution.py:746
  52.1 32.1 %collective-permute-done.2 = bf16[768,1024]{1,0:T(8,128)(2,1)} collective-permute-done((bf16[768,1024]{1,0:T(8,128)(2,1)}, bf16[768,1024]{1,0:T(8,128)(2,1)}, u32[]{:S(2)}, u32[]{:S(2)}) %collective-permute-start.2) | collective-permute-done | bytes 1572896 | tf_op jit(solution)/shard_map/ppermute | solution.py:746
  92.8 10.7 %psum.7 = f32[]{:T(128)} all-reduce(f32[]{:T(128)} %bitcast.6), channel_id=1, replica_groups=mesh['dp'=4,'mp'=8] {'dp'}, use_global_device_ids=true, to_apply=%region_5.6 | all-reduce | flops 1 | bytes 8 | tf_op jit(solution)/shard_map/psum | solution.py:750
  117.7 14.7 %shard_map.405.x_ref = bf16[3,2048,384]{2,1,0:T(8,128)(2,1)} custom-call(s32[54]{0:T(128)} %pad_add_fusion.1.table_ref, bf16[8,1056,384]{2,1,0:T(8,128)(2,1)} %bitcast.131, bf16[9,256,1024]{2,1,0:T(8,128)(2,1)} %bitcast.125, bf16[9,256,1024]{2,1,0:T(8,128)(2,1)} %bitcast.7.refs_1_), custom_call_target="tpu_custom_call" | custom-call | flops 4831838208 | bytes 14155776 | tf_op jit(solution)/shard_map/pallas_call | solution.py:85
  132.4 48.2 %shard_map.406 = (bf16[54,256,128]{2,1,0:T(8,128)(2,1)}, f32[3,2,2048]{2,1,0:T(2,128)}) custom-call(s32[24]{0:T(128)} %get-tuple-element.272.place_ref, bf16[3,2048,384]{2,1,0:T(8,128)(2,1)} %shard_map.405.x_ref), custom_call_target="tpu_custom_call" | custom-call | flops 25769803776 | bytes 7077888 | tf_op jit(solution)/shard_map/pallas_call | solution.py:217
  187.3 16.8 %collective-permute-start.8 = (bf16[3,3,256,128]{3,2,1,0:T(8,128)(2,1)S(1)}, bf16[3,3,256,128]{3,2,1,0:T(8,128)(2,1)S(1)}, u32[]{:S(2)}, u32[]{:S(2)}) collective-permute-start(bf16[3,3,256,128]{3,2,1,0:T(8,128)(2,1)S(1)} %bitcast.141), channel_id=1, source_target_pairs={{0,2},{2,4},{10,5},{12,7},{1,10},{3,12},{11,13},{13,15},{16,18},{1... | collective-permute-start | bytes 1769480 | tf_op jit(solution)/shard_map/ppermute | solution.py:638
  222.7 8.3 %shard_map.407 = (bf16[768,1024]{1,0:T(8,128)(2,1)}, f32[768,1024]{1,0:T(8,128)}, bf16[768,1024]{1,0:T(8,128)(2,1)}) custom-call(s32[24]{0:T(128)} %get-tuple-element.271.place_ref, bf16[54,256,128]{2,1,0:T(8,128)(2,1)} %bitcast.133, bf16[1024,1024]{1,0:T(8,128)(2,1)} %bitcast.121, f32[768,1024]{1,0:T(8,128)} %copy-done.1, f32[8,1024]{1,0:T(8,128)} %select_maximum_fusion.vec_ref), custom_call_target="tpu_custom_call" | custom-call | flops 1610612736 | bytes 15728640 | tf_op jit(solution)/shard_map/pallas_call | solution.py:453
  234.6 26.5 %shard_map.408 = (f32[768,1024]{1,0:T(8,128)}, f32[768,1024]{1,0:T(8,128)}, bf16[4,768,512]{2,1,0:T(8,128)(2,1)}, bf16[4,768,512]{2,1,0:T(8,128)(2,1)}, f32[4,1,512]{2,1,0:T(1,128)}) custom-call(bf16[768,1024]{1,0:T(8,128)(2,1)} %get-tuple-element.92.x_ref.refs_0_, bf16[768,1024]{1,0:T(8,128)(2,1)} %multiply_convert_fusion.g_ref.refs_1_, ...), custom_call_target="tpu_custom_call" | custom-call | flops 12884901888 | bytes 32636928 | tf_op jit(solution)/shard_map/pallas_call | solution.py:373
  262.0 14.4 %shard_map.409 = (bf16[384,1024]{1,0:T(8,128)(2,1)}, bf16[384,1024]{1,0:T(8,128)(2,1)}, bf16[4,384,512]{2,1,0:T(8,128)(2,1)}, bf16[4,384,512]{2,1,0:T(8,128)(2,1)}, f32[4,1,512]{2,1,0:T(1,128)}) custom-call(bf16[384,1024]{1,0:T(8,128)(2,1)} %copy-done.15, bf16[384,1024]{1,0:T(8,128)(2,1)} %get-tuple-element.249.g_ref.refs_5_, ...), custom_call_target="tpu_custom_call" | custom-call | flops 6442450944 | bytes 21626880 | tf_op jit(solution)/shard_map/pallas_call | solution.py:373
  278.8 15.2 %shard_map.410 = (bf16[384,1024]{1,0:T(8,128)(2,1)}, bf16[384,1024]{1,0:T(8,128)(2,1)}, bf16[4,384,512]{2,1,0:T(8,128)(2,1)}, bf16[4,384,512]{2,1,0:T(8,128)(2,1)}, f32[4,1,512]{2,1,0:T(1,128)}) custom-call(bf16[384,1024]{1,0:T(8,128)(2,1)} %copy-done.16, bf16[384,1024]{1,0:T(8,128)(2,1)} %get-tuple-element.248.g_ref.refs_9_, ...), custom_call_target="tpu_custom_call" | custom-call | flops 6442450944 | bytes 21626880 | tf_op jit(solution)/shard_map/pallas_call | solution.py:373
  295.8 18.7 %collective-permute-done.14 = bf16[384,1024]{1,0:T(8,128)(2,1)} collective-permute-done((bf16[384,1024]{1,0:T(8,128)(2,1)}, bf16[384,1024]{1,0:T(8,128)(2,1)}, u32[]{:S(2)}, u32[]{:S(2)}) %collective-permute-start.14) | collective-permute-done | bytes 786464 | tf_op jit(solution)/shard_map/ppermute | solution.py:787
  324.4 8.1 %shard_map.411 = bf16[18,768,128]{2,1,0:T(8,128)(2,1)} custom-call(s32[18]{0:T(128)} %and_select_fusion.5.shard_ref, bf16[768,1024]{1,0:T(8,128)(2,1)} %copy-done.9, bf16[1024,1024]{1,0:T(8,128)(2,1)} %bitcast.122), custom_call_target="tpu_custom_call" | custom-call | flops 1610612736 | bytes 6291456 | tf_op jit(solution)/shard_map/pallas_call | solution.py:489
  338.6 14.5 %collective-permute-start.18 = (bf16[3,3,256,128]{3,2,1,0:T(8,128)(2,1)}, bf16[3,3,256,128]{3,2,1,0:T(8,128)(2,1)}, u32[]{:S(2)}, u32[]{:S(2)}) collective-permute-start(bf16[3,3,256,128]{3,2,1,0:T(8,128)(2,1)} %bitcast.38), channel_id=1, source_target_pairs={{0,2},{2,4},{3,12},{5,14},{8,3},{10,5},{11,13},{13,15},{16,18},{18... | collective-permute-start | bytes 1769480 | tf_op jit(solution)/shard_map/ppermute | solution.py:638
  358.9 21.7 %shard_map.412 = bf16[8,2,288,1024]{3,2,1,0:T(8,128)(2,1)} custom-call(bf16[768,1024]{1,0:T(8,128)(2,1)} %get-tuple-element.92.x_ref.refs_0_, bf16[768,1024]{1,0:T(8,128)(2,1)} %multiply_convert_fusion.g_ref.refs_1_, bf16[4,768,512]{2,1,0:T(8,128)(2,1)} %get-tuple-element.110.refs_2_, bf16[4,768,512]{2,1,0:T(8,128)(2,1)} %get-tuple-element.111.refs_3_, ...), custom_call_target="tpu_custom_call" | custom-call | flops 12884901888 | bytes 20971520 | tf_op jit(solution)/shard_map/pallas_call | solution.py:426
  392.3 79.2 %shard_map.413 = (bf16[3,2048,384]{2,1,0:T(8,128)(2,1)}, f32[3,1,384]{2,1,0:T(1,128)}) custom-call(s32[24]{0:T(128)} %get-tuple-element.272.place_ref, bf16[3,2048,384]{2,1,0:T(8,128)(2,1)} %shard_map.405.x_ref, bf16[54,256,128]{2,1,0:T(8,128)(2,1)} %get-tuple-element.89.ctx_ref, bf16[54,256,128]{2,1,0:T(8,128)(2,1)} %bitcast.149, ...), custom_call_target="tpu_custom_call" | custom-call | flops 64424509440 | bytes 11796480 | tf_op jit(solution)/shard_map/pallas_call | solution.py:289
  471.5 16.5 %shard_map.414 = (bf16[9,256,1024]{2,1,0:T(8,128)(2,1)}, bf16[9,256,1024]{2,1,0:T(8,128)(2,1)}) custom-call(s32[54]{0:T(128)} %pad_add_fusion.1.table_ref, bf16[8,1056,384]{2,1,0:T(8,128)(2,1)} %bitcast.132, bf16[3,2048,384]{2,1,0:T(8,128)(2,1)} %get-tuple-element.128.g_ref), custom_call_target="tpu_custom_call" | custom-call | flops 4831838208 | bytes 14155776 | tf_op jit(solution)/shard_map/pallas_call | solution.py:168
  488.0 8.1 %collective-permute-done.22 = bf16[9,256,1024]{2,1,0:T(8,128)(2,1)S(1)} collective-permute-done((bf16[9,256,1024]{2,1,0:T(8,128)(2,1)}, bf16[9,256,1024]{2,1,0:T(8,128)(2,1)S(1)}, u32[]{:S(2)}, u32[]{:S(2)}) %collective-permute-start.22) | collective-permute-done | bytes 4718624 | tf_op jit(solution)/shard_map/ppermute | solution.py:828
  501.6 10.2 %collective-permute-start.25 = (bf16[768,1024]{1,0:T(8,128)(2,1)}, bf16[768,1024]{1,0:T(8,128)(2,1)}, u32[]{:S(2)}, u32[]{:S(2)}) collective-permute-start(bf16[768,1024]{1,0:T(8,128)(2,1)} %bitcast.47), channel_id=1, source_target_pairs={{0,2},{2,4},{10,5},{4,6},{12,7},{1,10},{3,12},{11,13},{5,14},{13,1... | collective-permute-start | bytes 4718600 | tf_op jit(solution)/shard_map/ppermute | solution.py:832
  513.1 13.3 %collective-permute-start.24 = (bf16[768,1024]{1,0:T(8,128)(2,1)}, bf16[768,1024]{1,0:T(8,128)(2,1)}, u32[]{:S(2)}, u32[]{:S(2)}) collective-permute-start(bf16[768,1024]{1,0:T(8,128)(2,1)} %bitcast.46), channel_id=1, source_target_pairs={{0,0},{8,1},{2,2},{10,3},{4,4},{12,5},{6,6},{14,7},{1,8},{9,9},{3,... | collective-permute-start | bytes 4718600 | tf_op jit(solution)/shard_map/ppermute | solution.py:832
  527.0 12.7 %shard_map.415 = bf16[3,384,1024]{2,1,0:T(8,128)(2,1)} custom-call(s32[54]{0:T(128)} %pad_add_fusion.1.table_ref, bf16[3,2048,384]{2,1,0:T(8,128)(2,1)} %get-tuple-element.128.g_ref, bf16[9,256,1024]{2,1,0:T(8,128)(2,1)} %bitcast.126, bf16[9,256,1024]{2,1,0:T(8,128)(2,1)} %bitcast.7.refs_1_), custom_call_target="tpu_custom_call" | custom-call | flops 4831838208 | bytes 11796480 | tf_op jit(solution)/shard_map/pallas_call | solution.py:111
  542.9 7.5 %collective-permute-start.29 = (bf16[384,1024]{1,0:T(8,128)(2,1)}, bf16[384,1024]{1,0:T(8,128)(2,1)}, u32[]{:S(2)}, u32[]{:S(2)}) collective-permute-start(bf16[384,1024]{1,0:T(8,128)(2,1)} %get-tuple-element.245), channel_id=1, source_target_pairs={{0,2},{8,5},{2,0},{10,3},{4,6},{12,1},{6,4},{14,7},{1,10},{9,13},{... | collective-permute-start | bytes 2359304 | tf_op jit(solution)/shard_map/ppermute | solution.py:837
  553.2 7.7 %collective-permute-start.27 = (bf16[384,1024]{1,0:T(8,128)(2,1)}, bf16[384,1024]{1,0:T(8,128)(2,1)}, u32[]{:S(2)}, u32[]{:S(2)}) collective-permute-start(bf16[384,1024]{1,0:T(8,128)(2,1)} %get-tuple-element.247), channel_id=1, source_target_pairs={{0,0},{8,3},{2,6},{10,1},{4,4},{12,7},{6,2},{14,5},{1,8},{9,11},{3... | collective-permute-start | bytes 2359304 | tf_op jit(solution)/shard_map/ppermute | solution.py:837
  570.8 11.8 %collective-permute-done.29 = bf16[384,1024]{1,0:T(8,128)(2,1)} collective-permute-done((bf16[384,1024]{1,0:T(8,128)(2,1)}, bf16[384,1024]{1,0:T(8,128)(2,1)}, u32[]{:S(2)}, u32[]{:S(2)}) %collective-permute-start.29) | collective-permute-done | bytes 786464 | tf_op jit(solution)/shard_map/ppermute | solution.py:837
  621.5 14.0 %collective-permute-done.35 = bf16[384,1024]{1,0:T(8,128)(2,1)S(1)} collective-permute-done((bf16[384,1024]{1,0:T(8,128)(2,1)S(1)}, bf16[384,1024]{1,0:T(8,128)(2,1)S(1)}, u32[]{:S(2)}, u32[]{:S(2)}) %collective-permute-start.35) | collective-permute-done | bytes 786464 | tf_op jit(solution)/shard_map/ppermute | solution.py:879
  (299 shorter events, 187.0 us)
Async XLA Ops:
  7.2 110.5 %all-gather.4.cloned.1.call-start = ((), (), s32[]{:S(2)}) async-start(), calls=%async_computation.1 | async-start | bytes 6893568 | tf_op jit(solution)/shard_map/all_gather | solution.py:726
  10.4 205.7 %all-gather.6.cloned.1.call-start = ((), (), s32[]{:S(2)}) async-start(), calls=%async_computation.2 | async-start | bytes 11280384 | tf_op jit(solution)/shard_map/all_gather | solution.py:751
  17.8 66.5 %collective-permute-start.2 = (bf16[768,1024]{1,0:T(8,128)(2,1)}, bf16[768,1024]{1,0:T(8,128)(2,1)}, u32[]{:S(2)}, u32[]{:S(2)}) collective-permute-start(bf16[768,1024]{1,0:T(8,128)(2,1)} %add_convert_fusion.3), channel_id=1, source_target_pairs={{2,0},{4,2},{5,10},{6,4},{7,12},{10,1},{12,3},{13,11},{14,5},{15,1... | collective-permute-start | bytes 4718600 | tf_op jit(solution)/shard_map/ppermute | solution.py:746
  19.2 65.0 %collective-permute-start.1 = (bf16[768,1024]{1,0:T(8,128)(2,1)}, bf16[768,1024]{1,0:T(8,128)(2,1)}, u32[]{:S(2)}, u32[]{:S(2)}) collective-permute-start(bf16[768,1024]{1,0:T(8,128)(2,1)} %add_convert_fusion.3), channel_id=1, source_target_pairs={{0,0},{1,8},{2,2},{3,10},{4,4},{5,12},{6,6},{7,14},{8,1},{9,9},{10... | collective-permute-start | bytes 4718600 | tf_op jit(solution)/shard_map/ppermute | solution.py:746
  32.5 55.1 %collective-permute-start = (bf16[768,1024]{1,0:T(8,128)(2,1)}, bf16[768,1024]{1,0:T(8,128)(2,1)}, u32[]{:S(2)}, u32[]{:S(2)}) collective-permute-start(bf16[768,1024]{1,0:T(8,128)(2,1)} %add_convert_fusion.3), channel_id=1, source_target_pairs={{0,2},{1,10},{2,4},{3,12},{5,14},{8,3},{9,11},{10,5},{11,13},{13,1... | collective-permute-start | bytes 4718600 | tf_op jit(solution)/shard_map/ppermute | solution.py:746
  92.7 476.8 %reduce-scatter.2.cloned.1.call-start = ((), (), s32[]{:S(2)}) async-start(), calls=%async_computation.3 | async-start | bytes 10027008 | tf_op jit(solution)/shard_map/reduce_scatter | solution.py:818
  117.0 68.9 %collective-permute-start.12 = (bf16[768,1024]{1,0:T(8,128)(2,1)S(1)}, bf16[768,1024]{1,0:T(8,128)(2,1)S(1)}, u32[]{:S(2)}, u32[]{:S(2)}) collective-permute-start(bf16[768,1024]{1,0:T(8,128)(2,1)S(1)} %copy-done.10), channel_id=1, source_target_pairs={{0,16},{8,24},{16,0},{24,8},{1,17},{9,25},{17,1},{25,9},{2,18},{10... | collective-permute-start | bytes 4718600 | tf_op jit(solution)/shard_map/ppermute | solution.py:753
  187.3 28.6 %collective-permute-start.8 = (bf16[3,3,256,128]{3,2,1,0:T(8,128)(2,1)S(1)}, bf16[3,3,256,128]{3,2,1,0:T(8,128)(2,1)S(1)}, u32[]{:S(2)}, u32[]{:S(2)}) collective-permute-start(bf16[3,3,256,128]{3,2,1,0:T(8,128)(2,1)S(1)} %bitcast.141), channel_id=1, source_target_pairs={{0,2},{2,4},{10,5},{12,7},{1,10},{3,12},{11,13},{13,15},{16,18},{1... | collective-permute-start | bytes 1769480 | tf_op jit(solution)/shard_map/ppermute | solution.py:638
  232.5 28.6 %collective-permute-start.11 = (bf16[384,1024]{1,0:T(8,128)(2,1)S(1)}, bf16[384,1024]{1,0:T(8,128)(2,1)S(1)}, u32[]{:S(2)}, u32[]{:S(2)}) collective-permute-start(bf16[384,1024]{1,0:T(8,128)(2,1)S(1)} %get-tuple-element.250), channel_id=1, source_target_pairs={{0,16},{8,24},{16,0},{24,8},{1,17},{9,25},{17,1},{25,9},{2,18},{10... | collective-permute-start | bytes 2359304 | tf_op jit(solution)/shard_map/ppermute | solution.py:774
  234.0 43.9 %collective-permute-start.10 = (bf16[384,1024]{1,0:T(8,128)(2,1)S(1)}, bf16[384,1024]{1,0:T(8,128)(2,1)S(1)}, u32[]{:S(2)}, u32[]{:S(2)}) collective-permute-start(bf16[384,1024]{1,0:T(8,128)(2,1)S(1)} %get-tuple-element.251), channel_id=1, source_target_pairs={{0,16},{8,24},{16,0},{24,8},{1,17},{9,25},{17,1},{25,9},{2,18},{10... | collective-permute-start | bytes 2359304 | tf_op jit(solution)/shard_map/ppermute | solution.py:774
  276.4 38.1 %collective-permute-start.13 = (bf16[384,1024]{1,0:T(8,128)(2,1)}, bf16[384,1024]{1,0:T(8,128)(2,1)}, u32[]{:S(2)}, u32[]{:S(2)}) collective-permute-start(bf16[384,1024]{1,0:T(8,128)(2,1)} %get-tuple-element.97), channel_id=1, source_target_pairs={{0,16},{8,24},{16,0},{24,8},{1,17},{9,25},{17,1},{25,9},{2,18},{10... | collective-permute-start | bytes 2359304 | tf_op jit(solution)/shard_map/ppermute | solution.py:787
  337.3 49.2 %collective-permute-start.19 = (bf16[3,3,256,128]{3,2,1,0:T(8,128)(2,1)S(1)}, bf16[3,3,256,128]{3,2,1,0:T(8,128)(2,1)}, u32[]{:S(2)}, u32[]{:S(2)}) collective-permute-start(bf16[3,3,256,128]{3,2,1,0:T(8,128)(2,1)S(1)} %bitcast.140), channel_id=1, source_target_pairs={{2,0},{4,2},{5,10},{7,12},{10,1},{12,3},{13,11},{15,13},{18,16},{2... | collective-permute-start | bytes 1769480 | tf_op jit(solution)/shard_map/ppermute | solution.py:638
  338.6 46.7 %collective-permute-start.18 = (bf16[3,3,256,128]{3,2,1,0:T(8,128)(2,1)}, bf16[3,3,256,128]{3,2,1,0:T(8,128)(2,1)}, u32[]{:S(2)}, u32[]{:S(2)}) collective-permute-start(bf16[3,3,256,128]{3,2,1,0:T(8,128)(2,1)} %bitcast.38), channel_id=1, source_target_pairs={{0,2},{2,4},{3,12},{5,14},{8,3},{10,5},{11,13},{13,15},{16,18},{18... | collective-permute-start | bytes 1769480 | tf_op jit(solution)/shard_map/ppermute | solution.py:638
  353.1 31.1 %collective-permute-start.17 = (bf16[3,3,256,128]{3,2,1,0:T(8,128)(2,1)}, bf16[3,3,256,128]{3,2,1,0:T(8,128)(2,1)}, u32[]{:S(2)}, u32[]{:S(2)}) collective-permute-start(bf16[3,3,256,128]{3,2,1,0:T(8,128)(2,1)} %bitcast.36), channel_id=1, source_target_pairs={{1,0},{2,8},{3,2},{4,10},{5,4},{6,12},{7,6},{9,1},{10,9},{11,3},{1... | collective-permute-start | bytes 1769480 | tf_op jit(solution)/shard_map/ppermute | solution.py:638
  358.1 31.5 %collective-permute-start.36 = (bf16[8,1,2,32,1024]{4,3,2,0,1:T(8,128)(2,1)S(1)}, bf16[8,1,2,32,1024]{4,3,2,0,1:T(8,128)(2,1)}, u32[]{:S(2)}, u32[]{:S(2)}) collective-permute-start(bf16[8,1,2,32,1024]{4,3,2,0,1:T(8,128)(2,1)S(1)} %dynamic-slice_bitcast_fusion), channel_id=1, source_target_pairs={{0,16},{8,24},{16,0},{24,8},{1,17},{9,25},{17,1},{25,9},{2,18},{10... | collective-permute-start | bytes 3145736 | tf_op jit(solution)/shard_map/ppermute | solution.py:814
  381.7 89.8 %collective-permute-start.21 = (bf16[768,1024]{1,0:T(8,128)(2,1)}, bf16[768,1024]{1,0:T(8,128)(2,1)}, u32[]{:S(2)}, u32[]{:S(2)}) collective-permute-start(bf16[768,1024]{1,0:T(8,128)(2,1)} %pad_maximum_fusion.1), channel_id=1, source_target_pairs={{0,16},{8,24},{16,0},{24,8},{1,17},{9,25},{17,1},{25,9},{2,18},{10... | collective-permute-start | bytes 4718600 | tf_op jit(solution)/shard_map/ppermute | solution.py:791
  392.2 248.1 %all-gather.8.cloned.1.call-start = ((), (), s32[]{:S(2)}) async-start(), calls=%async_computation.4 | async-start | bytes 2949120 | tf_op jit(solution)/shard_map/all_gather | solution.py:891
  501.6 38.1 %collective-permute-start.25 = (bf16[768,1024]{1,0:T(8,128)(2,1)}, bf16[768,1024]{1,0:T(8,128)(2,1)}, u32[]{:S(2)}, u32[]{:S(2)}) collective-permute-start(bf16[768,1024]{1,0:T(8,128)(2,1)} %bitcast.47), channel_id=1, source_target_pairs={{0,2},{2,4},{10,5},{4,6},{12,7},{1,10},{3,12},{11,13},{5,14},{13,1... | collective-permute-start | bytes 4718600 | tf_op jit(solution)/shard_map/ppermute | solution.py:832
  511.8 49.1 %collective-permute-start.23 = (bf16[768,1024]{1,0:T(8,128)(2,1)}, bf16[768,1024]{1,0:T(8,128)(2,1)}, u32[]{:S(2)}, u32[]{:S(2)}) collective-permute-start(bf16[768,1024]{1,0:T(8,128)(2,1)} %bitcast.45), channel_id=1, source_target_pairs={{2,0},{10,1},{4,2},{12,3},{14,5},{3,8},{11,9},{5,10},{13,11},{15,1... | collective-permute-start | bytes 4718600 | tf_op jit(solution)/shard_map/ppermute | solution.py:832
  513.1 47.8 %collective-permute-start.24 = (bf16[768,1024]{1,0:T(8,128)(2,1)}, bf16[768,1024]{1,0:T(8,128)(2,1)}, u32[]{:S(2)}, u32[]{:S(2)}) collective-permute-start(bf16[768,1024]{1,0:T(8,128)(2,1)} %bitcast.46), channel_id=1, source_target_pairs={{0,0},{8,1},{2,2},{10,3},{4,4},{12,5},{6,6},{14,7},{1,8},{9,9},{3,... | collective-permute-start | bytes 4718600 | tf_op jit(solution)/shard_map/ppermute | solution.py:832
  542.9 39.7 %collective-permute-start.29 = (bf16[384,1024]{1,0:T(8,128)(2,1)}, bf16[384,1024]{1,0:T(8,128)(2,1)}, u32[]{:S(2)}, u32[]{:S(2)}) collective-permute-start(bf16[384,1024]{1,0:T(8,128)(2,1)} %get-tuple-element.245), channel_id=1, source_target_pairs={{0,2},{8,5},{2,0},{10,3},{4,6},{12,1},{6,4},{14,7},{1,10},{9,13},{... | collective-permute-start | bytes 2359304 | tf_op jit(solution)/shard_map/ppermute | solution.py:837
  550.5 32.1 %collective-permute-start.28 = (bf16[384,1024]{1,0:T(8,128)(2,1)}, bf16[384,1024]{1,0:T(8,128)(2,1)}, u32[]{:S(2)}, u32[]{:S(2)}) collective-permute-start(bf16[384,1024]{1,0:T(8,128)(2,1)} %get-tuple-element.246), channel_id=1, source_target_pairs={{0,1},{8,4},{2,7},{10,2},{4,5},{12,0},{6,3},{14,6},{1,9},{9,12},{3... | collective-permute-start | bytes 2359304 | tf_op jit(solution)/shard_map/ppermute | solution.py:837
  553.2 29.4 %collective-permute-start.27 = (bf16[384,1024]{1,0:T(8,128)(2,1)}, bf16[384,1024]{1,0:T(8,128)(2,1)}, u32[]{:S(2)}, u32[]{:S(2)}) collective-permute-start(bf16[384,1024]{1,0:T(8,128)(2,1)} %get-tuple-element.247), channel_id=1, source_target_pairs={{0,0},{8,3},{2,6},{10,1},{4,4},{12,7},{6,2},{14,5},{1,8},{9,11},{3... | collective-permute-start | bytes 2359304 | tf_op jit(solution)/shard_map/ppermute | solution.py:837
  585.5 30.0 %collective-permute-start.34 = (bf16[384,1024]{1,0:T(8,128)(2,1)}, bf16[384,1024]{1,0:T(8,128)(2,1)}, u32[]{:S(2)}, u32[]{:S(2)}) collective-permute-start(bf16[384,1024]{1,0:T(8,128)(2,1)} %add_convert_fusion.6), channel_id=1, source_target_pairs={{0,8},{8,0},{16,24},{24,16},{1,9},{9,1},{17,25},{25,17},{2,10},{10... | collective-permute-start | bytes 2359304 | tf_op jit(solution)/shard_map/ppermute | solution.py:879
  (60 other events, 954.3 us)
Sparse Core Ops, SparseCore 0:
  10.8 99.1 all-gather.3
  112.8 87.6 all-gather.5
  392.3 117.4 reduce-scatter.1
  569.6 49.3 all-gather.7

commit v4 on v3

--- a/solution.py
+++ b/solution.py
@@ -197,12 +197,14 @@
 
     rows = pl.ds(pl.multiple_of(step * block, block), block)
     here = x_ref[0, rows, :]
+    scores = []
     for h in range(heads):
         c = h * 3 * HEAD_DIM
         query = here[:, c : c + HEAD_DIM] * jnp.asarray(HEAD_DIM**-0.5, BF16)
-        scores = mm(query, keys_s[h])
-        row_max = jnp.max(scores, 1, keepdims=True)
-        probs = jnp.exp(scores - row_max).astype(BF16)
+        scores.append(mm(query, keys_s[h]))
+    for h in range(heads):
+        row_max = jnp.max(scores[h], 1, keepdims=True)
+        probs = jnp.exp(scores[h] - row_max).astype(BF16)
         summed = mm(probs, values_s[h])
         total = summed[:, HEAD_DIM : HEAD_DIM + 1]
         ctx_ref[0, :, h * HEAD_DIM : (h + 1) * HEAD_DIM] = (summed[:, :HEAD_DIM] / total).astype(BF16)
@@ -562,7 +564,7 @@
     tile = widen_weight.shape[1] // 2
     parts = width // tile
     count = copies // 2
-    some = 2
+    some = 4
     dp_at = lax.axis_index("dp")
     mp_at = lax.axis_index("mp")
     both = ("dp", "mp")
@@ -697,6 +699,23 @@
             (g * shards + (slots * k + j) % shards, attention_device(g, k)) for g in groups for k in spots
         ]
 
+    def exact_rows(vector, pad):
+        high = vector.astype(BF16)
+        left = vector - high.astype(F32)
+        middle = left.astype(BF16)
+        low = (left - middle.astype(F32)).astype(BF16)
+        return jnp.pad(jnp.stack([high, middle, low]), ((0, pad - 3), (0, 0)))
+
+    bias_heads = heads_bias.reshape(heads_here, 2, HEAD_DIM)
+    full_bias = jnp.stack(
+        [bias_heads[:, 0], jnp.zeros_like(bias_heads[:, 0]), bias_heads[:, 1]], 1
+    ).reshape(-1)
+    heads_rows = jnp.concatenate([heads_weight, exact_rows(full_bias, 16 * count)], 0)
+    heads_piece = share_of(heads_rows, piece_at, count)
+    heads_piece, tokens = lax.optimization_barrier((heads_piece, tokens))
+    heads_all = lax.all_gather(heads_piece, BOTH, axis=0, tiled=True, axis_index_groups=plane)
+    heads_all = heads_all.reshape(shards, -1, cols)
+
     row_ids = mp_at * rows_here + jnp.arange(rows_here, dtype=jnp.int32)
     slot_ids = jnp.arange(slots, dtype=jnp.int32)
     slot_table = ((row_ids // length)[:, None] == slot_ids[None, :]).astype(F32)
@@ -710,22 +729,6 @@
     start_state = tokens + lead_scaled[:, None] * lead_weight + lead_shift
     first_normal, first_scale = norm_parts(start_state)
     normed_one = (first_normal * norm_one_gain + norm_one_shift).astype(BF16)
-
-    def exact_rows(vector, pad):
-        high = vector.astype(BF16)
-        left = vector - high.astype(F32)
-        middle = left.astype(BF16)
-        low = (left - middle.astype(F32)).astype(BF16)
-        return jnp.pad(jnp.stack([high, middle, low]), ((0, pad - 3), (0, 0)))
-
-    bias_heads = heads_bias.reshape(heads_here, 2, HEAD_DIM)
-    full_bias = jnp.stack(
-        [bias_heads[:, 0], jnp.zeros_like(bias_heads[:, 0]), bias_heads[:, 1]], 1
-    ).reshape(-1)
-    heads_rows = jnp.concatenate([heads_weight, exact_rows(full_bias, 16 * count)], 0)
-    heads_all = lax.all_gather(
-        share_of(heads_rows, piece_at, count), BOTH, axis=0, tiled=True, axis_index_groups=plane
-    ).reshape(shards, -1, cols)
 
     def fold(part):
         return jnp.concatenate(jnp.split(part, parts, 1), 0)
@@ -786,7 +789,8 @@
         their_fed.append(part_fed)
         their_dx.append(lax.ppermute(part_dx, "dp", half_swap))
         fed = lax.optimization_barrier((fed, part_dx))[0]
-    their_dx[-1], *their_fed = lax.optimization_barrier((their_dx[-1], *their_fed))
+    grads_one = feed_grads(feed_parts, count, some, merge_weight.shape[0] // copies)
+    their_dx[-1], grads_one, *their_fed = lax.optimization_barrier((their_dx[-1], grads_one, *their_fed))
     grad_norm_two = grad_norm_two + jnp.concatenate(their_dx).astype(F32)
     their_fed = lax.ppermute(jnp.concatenate(their_fed), "dp", half_swap)
     widen_bias_grad = widen_bias_grad.reshape(shards, 1, tile)
@@ -801,11 +805,6 @@
     merge_bias_grad = jnp.sum(grad_mid_low.astype(F32), 0)
     grad_context = merge_back(grad_mid_low, merge_all, wanted, wide)
     grad_context = exchange(grad_context.reshape(-1, *message), False)
-    first = feed_parts[0][:2]
-    grad_context[0], *hold = lax.optimization_barrier((grad_context[0], *feed_parts[0][2:]))
-    feed_parts[0] = first + tuple(hold)
-    grads_one = feed_grads(feed_parts, count, some, merge_weight.shape[0] // copies)
-    grad_context[1], grads_one = lax.optimization_barrier((grad_context[1], grads_one))
     grad_context = together(grad_context, message)
     merge_weight_grad = mm(context_rows, grad_mid_low, TN).astype(BF16)
     merge_weight_grad = merge_weight_grad.reshape(shards, copies // 4, 2, 2, -1, width)
@@ -823,18 +822,24 @@
     )
     grad_packed, their_fed = lax.optimization_barrier((grad_packed, their_fed))
     activations = middle + fed + their_fed.astype(F32) + narrow_bias
+    unit_grads = weight_back(pieces, grad_packed, table)
+    heads_parts = [lax.ppermute(unit_grads[j], both, back(weight_pairs(j))) for j in range(slots)]
+    grad_packed, unit_grads = lax.optimization_barrier((grad_packed, unit_grads))
     own_dx, other_dx = rows_back(grad_packed, heads_all, table, block, 2, len(steps) * slots, width)
 
-    other_dx = lax.ppermute(other_dx, "dp", core_swap).reshape(-1, rows_here, width)
+    other_dx = lax.ppermute(other_dx, "dp", core_swap)
+    other_dx, *heads_parts = lax.optimization_barrier((other_dx, *heads_parts))
+    other_dx = other_dx.reshape(-1, rows_here, width)
     own_dx = own_dx.reshape(-1, rows_here, width)
     pair_dx = [(own_dx[i].astype(F32) + other_dx[i].astype(F32)).astype(BF16) for i in range(len(steps))]
-    grad_packed, *pair_dx = lax.optimization_barrier((grad_packed, *pair_dx))
     grad_norm_one = [lax.ppermute(pair_dx[i], both, far(o)) for i, o in enumerate(steps)]
 
-    unit_grads = weight_back(pieces, grad_packed, table)
-    grad_norm_one[-1], unit_grads = lax.optimization_barrier((grad_norm_one[-1], unit_grads))
+    heads_total = sum(part.astype(F32) for part in heads_parts).astype(BF16)
+    for bit in range((copies - 1).bit_length()):
+        over = lax.ppermute(heads_total, "dp", [(g, g ^ 1 << bit) for g in groups])
+        heads_total = (heads_total.astype(F32) + over.astype(F32)).astype(BF16)
+    grad_norm_one[-1], heads_total = lax.optimization_barrier((grad_norm_one[-1], heads_total))
     grad_norm_one = sum(part.astype(F32) for part in grad_norm_one)
-    heads_parts = [lax.ppermute(unit_grads[j], both, back(weight_pairs(j))) for j in range(slots)]
     heads_bias_grad = jnp.sum(
         jnp.where(
             (unit_ids % shards)[:, None, None] == jnp.arange(shards, dtype=jnp.int32)[None, :, None],
@@ -868,17 +873,9 @@
         for axis, size in (("dp", copies), ("mp", shards))
         for bit in range((size - 1).bit_length())
     ]
-    heads_total = None
-    for at, (axis, pairs) in enumerate(hops):
+    for axis, pairs in hops:
         vectors += lax.ppermute(vectors, axis, pairs)
-        if at == 0:
-            vectors, *heads_parts = lax.optimization_barrier((vectors, *heads_parts))
-            heads_total = sum(part.astype(F32) for part in heads_parts).astype(BF16)
-        elif at <= (copies - 1).bit_length():
-            axis, pairs = hops[at - 1]
-            over = lax.ppermute(heads_total, axis, pairs)
-            heads_total = (heads_total.astype(F32) + over.astype(F32)).astype(BF16)
-    vectors, heads_total = lax.optimization_barrier((vectors / item_total, heads_total))
+    vectors /= item_total
     heads_total = heads_total.astype(F32)
     shared = vectors[: 8 * width].reshape(8, width)
     place = lax.axis_index("mp")

time: 666 us -> 655 us (0.983)
  local copies, waits for them, and re-layouts: 51.8 us -> 41.6 us
  Pallas kernels: 265 us -> 255 us
  starting transfers between devices: 135 us -> 142 us
  waiting for transfers between devices: 103 us -> 110 us
    ppermute x10, waiting for transfers between devices: 6.99 us -> 25.8 us  [exchange(): got.append(lax.ppermute(message, both, ends))]
    ppermute x2, waiting for transfers between devices: 18.7 us -> 0.01 us  [on_device(): their_dx.append(lax.ppermute(part_dx, 'dp', half_swap))]
    ppermute x3, waiting for transfers between devices: 0.01 us -> 9.46 us  [on_device(): lax.ppermute(pair_dx[i], both, far(o))]
    ppermute x5, starting transfers between devices: 13.5 us -> 22.4 us  [on_device(): vectors += lax.ppermute(vectors, axis, pairs)]
    ppermute x10, starting transfers between devices: 43 us -> 51.6 us  [exchange(): got.append(lax.ppermute(message, both, ends))]
    ppermute x3, waiting for transfers between devices: 22.1 us -> 13.7 us  [the longest x2 13.7 us: on_device(): over = lax.ppermute(heads_total, 'dp', [(g, g ^ 1 << bit) for g in groups])]
    ppermute x3, starting transfers between devices: 24.8 us -> 17.4 us  [on_device(): lax.ppermute(pair_dx[i], both, far(o))]
    unnamed x111 -> x115, local copies, waits for them, and re-layouts: 24.2 us -> 17.1 us
  transfers between devices with their start and end apart: 41 -> 41, of which waited for: 11 -> 13; matrix products, arithmetic and copies ran while one was open for 12% -> 11% of each run, Pallas kernels for 38% -> 37%
where the time goes in v4:
time: 655 us; the launch traced here: 645 us
  Pallas kernels  255 us (39%)
  starting transfers between devices  142 us (22%)
  waiting for transfers between devices  110 us (17%)
  other arithmetic  59.4 us (9%)
  local copies, waits for them, and re-layouts  41.6 us (6%)
  between operations  23.6 us (4%)
  blocking collectives  11 us (2%)
    pallas_call x1, Pallas kernels, attend_back(): pl.pallas_call(functools.partial(attend_back_kernel, heads, block), grid_...  79.6 us
    ppermute x10, starting transfers between devices, exchange(): got.append(lax.ppermute(message, both, ends))  51.6 us
    pallas_call x3, Pallas kernels, feed(): pl.pallas_call(functools.partial(feed_kernel, parts), grid=(steps,), in_s...  50 us
    pallas_call x1, Pallas kernels, attend(): pl.pallas_call(functools.partial(attend_kernel, heads, block), grid_spec=...  41.6 us
    ppermute x3, waiting for transfers between devices, on_device(): lax.ppermute(normed_one, both, back(far(o)))  33.6 us
    ppermute x10, waiting for transfers between devices, exchange(): got.append(lax.ppermute(message, both, ends))  25.8 us
    pallas_call x1, Pallas kernels, feed_grads(): pl.pallas_call(feed_grads_kernel, grid=(steps,), in_specs=specs, out_spec...  23.3 us
    ppermute x5, starting transfers between devices, on_device(): vectors += lax.ppermute(vectors, axis, pairs)  22.4 us
  transfers between devices with their start and end apart: 41, of which 13 were waited for; matrix products, arithmetic and copies ran while one was open for 11% of the time, Pallas kernels for 37%

profile of v4, /device:TPU:0, one launch (start us, length us, event | category | flops | bytes accessed | tf_op | source)
XLA Modules:
  0.0 644.5 jit_solution(3344222317039219837)
XLA Ops:
  24.0 13.3 %collective-permute-start.1 = (bf16[768,1024]{1,0:T(8,128)(2,1)}, bf16[768,1024]{1,0:T(8,128)(2,1)}, u32[]{:S(2)}, u32[]{:S(2)}) collective-permute-start(bf16[768,1024]{1,0:T(8,128)(2,1)} %add_convert_fusion.3), channel_id=1, source_target_pairs={{0,0},{1,8},{2,2},{3,10},{4,4},{5,12},{6,6},{7,14},{8,1},{9,9},{10... | collective-permute-start | bytes 4718600 | tf_op jit(solution)/shard_map/ppermute | solution.py:749
  51.5 32.0 %collective-permute-done = bf16[768,1024]{1,0:T(8,128)(2,1)} collective-permute-done((bf16[768,1024]{1,0:T(8,128)(2,1)}, bf16[768,1024]{1,0:T(8,128)(2,1)}, u32[]{:S(2)}, u32[]{:S(2)}) %collective-permute-start) | collective-permute-done | bytes 1572896 | tf_op jit(solution)/shard_map/ppermute | solution.py:749
  90.4 11.0 %psum.7 = f32[]{:T(128)} all-reduce(f32[]{:T(128)} %bitcast.6), channel_id=1, replica_groups=mesh['dp'=4,'mp'=8] {'dp'}, use_global_device_ids=true, to_apply=%region_5.6 | all-reduce | flops 1 | bytes 8 | tf_op jit(solution)/shard_map/psum | solution.py:753
  115.8 14.6 %shard_map.405.x_ref = bf16[3,2048,384]{2,1,0:T(8,128)(2,1)} custom-call(s32[54]{0:T(128)} %pad_add_fusion.1.table_ref, bf16[8,1056,384]{2,1,0:T(8,128)(2,1)} %bitcast.130, bf16[9,256,1024]{2,1,0:T(8,128)(2,1)} %bitcast.125, bf16[9,256,1024]{2,1,0:T(8,128)(2,1)} %bitcast.7.refs_1_), custom_call_target="tpu_custom_call" | custom-call | flops 4831838208 | bytes 14155776 | tf_op jit(solution)/shard_map/pallas_call | solution.py:85
  130.5 41.6 %shard_map.406 = (bf16[54,256,128]{2,1,0:T(8,128)(2,1)}, f32[3,2,2048]{2,1,0:T(2,128)}) custom-call(s32[24]{0:T(128)} %get-tuple-element.258.place_ref, bf16[3,2048,384]{2,1,0:T(8,128)(2,1)} %shard_map.405.x_ref), custom_call_target="tpu_custom_call" | custom-call | flops 25769803776 | bytes 7077888 | tf_op jit(solution)/shard_map/pallas_call | solution.py:219
  183.9 20.4 %collective-permute-start.8 = (bf16[3,3,256,128]{3,2,1,0:T(8,128)(2,1)S(1)}, bf16[3,3,256,128]{3,2,1,0:T(8,128)(2,1)S(1)}, u32[]{:S(2)}, u32[]{:S(2)}) collective-permute-start(bf16[3,3,256,128]{3,2,1,0:T(8,128)(2,1)S(1)} %bitcast.141), channel_id=1, source_target_pairs={{0,2},{2,4},{10,5},{12,7},{1,10},{3,12},{11,13},{13,15},{16,18},{1... | collective-permute-start | bytes 1769480 | tf_op jit(solution)/shard_map/ppermute | solution.py:640
  218.2 8.3 %shard_map.407 = (bf16[768,1024]{1,0:T(8,128)(2,1)}, f32[768,1024]{1,0:T(8,128)}, bf16[768,1024]{1,0:T(8,128)(2,1)}) custom-call(s32[24]{0:T(128)} %get-tuple-element.257.place_ref, bf16[54,256,128]{2,1,0:T(8,128)(2,1)} %bitcast.132, bf16[1024,1024]{1,0:T(8,128)(2,1)} %bitcast.121, f32[768,1024]{1,0:T(8,128)} %copy-done.1, f32[8,1024]{1,0:T(8,128)} %select_maximum_fusion.vec_ref), custom_call_target="tpu_custom_call" | custom-call | flops 1610612736 | bytes 15728640 | tf_op jit(solution)/shard_map/pallas_call | solution.py:455
  230.5 23.6 %shard_map.408 = (f32[768,1024]{1,0:T(8,128)}, f32[768,1024]{1,0:T(8,128)}, bf16[2,768,1024]{2,1,0:T(8,128)(2,1)}, bf16[2,768,1024]{2,1,0:T(8,128)(2,1)}, f32[2,1,1024]{2,1,0:T(1,128)}) custom-call(bf16[768,1024]{1,0:T(8,128)(2,1)} %get-tuple-element.87.x_ref.refs_0_, bf16[768,1024]{1,0:T(8,128)(2,1)} %multiply_convert_fusion.g_ref.refs_1_, ...), custom_call_target="tpu_custom_call" | custom-call | flops 12884901888 | bytes 32636928 | tf_op jit(solution)/shard_map/pallas_call | solution.py:375
  255.7 13.3 %shard_map.409 = (bf16[384,1024]{1,0:T(8,128)(2,1)}, bf16[384,1024]{1,0:T(8,128)(2,1)}, bf16[2,384,1024]{2,1,0:T(8,128)(2,1)}, bf16[2,384,1024]{2,1,0:T(8,128)(2,1)}, f32[2,1,1024]{2,1,0:T(1,128)}) custom-call(bf16[384,1024]{1,0:T(8,128)(2,1)} %collective-permute-done.11.x_ref.refs_4_, bf16[384,1024]{1,0:T(8,128)(2,1)} %get-tuple-element.235.g_ref.refs_5_, ...), custom_call_target="tpu_custom_call" | custom-call | flops 6442450944 | bytes 21626880 | tf_op jit(solution)/shard_map/pallas_call | solution.py:375
  274.7 13.1 %shard_map.410 = (bf16[384,1024]{1,0:T(8,128)(2,1)}, bf16[384,1024]{1,0:T(8,128)(2,1)}, bf16[2,384,1024]{2,1,0:T(8,128)(2,1)}, bf16[2,384,1024]{2,1,0:T(8,128)(2,1)}, f32[2,1,1024]{2,1,0:T(1,128)}) custom-call(bf16[384,1024]{1,0:T(8,128)(2,1)} %collective-permute-done.10.x_ref.refs_8_, bf16[384,1024]{1,0:T(8,128)(2,1)} %get-tuple-element.234.g_ref.refs_9_, ...), custom_call_target="tpu_custom_call" | custom-call | flops 6442450944 | bytes 21626880 | tf_op jit(solution)/shard_map/pallas_call | solution.py:375
  289.0 23.3 %shard_map.411 = bf16[8,2,288,1024]{3,2,1,0:T(8,128)(2,1)} custom-call(bf16[768,1024]{1,0:T(8,128)(2,1)} %get-tuple-element.87.x_ref.refs_0_, bf16[768,1024]{1,0:T(8,128)(2,1)} %multiply_convert_fusion.g_ref.refs_1_, bf16[2,768,1024]{2,1,0:T(8,128)(2,1)} %get-tuple-element.99.refs_2_, bf16[2,768,1024]{2,1,0:T(8,128)(2,1)} %get-tuple-element.100.refs_3_, ...), custom_call_target="tpu_custom_call" | custom-call | flops 12884901888 | bytes 20971520 | tf_op jit(solution)/shard_map/pallas_call | solution.py:428
  321.5 8.1 %shard_map.412 = bf16[18,768,128]{2,1,0:T(8,128)(2,1)} custom-call(s32[18]{0:T(128)} %and_select_fusion.5.shard_ref, bf16[768,1024]{1,0:T(8,128)(2,1)} %copy-done.8, bf16[1024,1024]{1,0:T(8,128)(2,1)} %bitcast.122), custom_call_target="tpu_custom_call" | custom-call | flops 1610612736 | bytes 6291456 | tf_op jit(solution)/shard_map/pallas_call | solution.py:491
  338.6 18.8 %collective-permute-start.18 = (bf16[3,3,256,128]{3,2,1,0:T(8,128)(2,1)S(1)}, bf16[3,3,256,128]{3,2,1,0:T(8,128)(2,1)S(1)}, u32[]{:S(2)}, u32[]{:S(2)}) collective-permute-start(bf16[3,3,256,128]{3,2,1,0:T(8,128)(2,1)S(1)} %bitcast.140), channel_id=1, source_target_pairs={{0,2},{2,4},{3,12},{5,14},{8,3},{10,5},{11,13},{13,15},{16,18},{18... | collective-permute-start | bytes 1769480 | tf_op jit(solution)/shard_map/ppermute | solution.py:640
  358.9 11.3 %collective-permute-done.18 = bf16[3,3,256,128]{3,2,1,0:T(8,128)(2,1)S(1)} collective-permute-done((bf16[3,3,256,128]{3,2,1,0:T(8,128)(2,1)S(1)}, bf16[3,3,256,128]{3,2,1,0:T(8,128)(2,1)S(1)}, u32[]{:S(2)}, u32[]{:S(2)}) %collective-permute-start.18) | collective-permute-done | bytes 589856 | tf_op jit(solution)/shard_map/ppermute | solution.py:640
  370.2 8.0 %collective-permute-done.19 = bf16[3,3,256,128]{3,2,1,0:T(8,128)(2,1)S(1)} collective-permute-done((bf16[3,3,256,128]{3,2,1,0:T(8,128)(2,1)S(1)}, bf16[3,3,256,128]{3,2,1,0:T(8,128)(2,1)S(1)}, u32[]{:S(2)}, u32[]{:S(2)}) %collective-permute-start.19) | collective-permute-done | bytes 589856 | tf_op jit(solution)/shard_map/ppermute | solution.py:640
  381.6 79.6 %shard_map.413 = (bf16[3,2048,384]{2,1,0:T(8,128)(2,1)}, f32[3,1,384]{2,1,0:T(1,128)}) custom-call(s32[24]{0:T(128)} %get-tuple-element.258.place_ref, bf16[3,2048,384]{2,1,0:T(8,128)(2,1)} %shard_map.405.x_ref, bf16[54,256,128]{2,1,0:T(8,128)(2,1)} %get-tuple-element.84.ctx_ref, bf16[54,256,128]{2,1,0:T(8,128)(2,1)} %bitcast.151, ...), custom_call_target="tpu_custom_call" | custom-call | flops 64424509440 | bytes 11796480 | tf_op jit(solution)/shard_map/pallas_call | solution.py:291
  461.3 12.6 %shard_map.414 = bf16[3,384,1024]{2,1,0:T(8,128)(2,1)} custom-call(s32[54]{0:T(128)} %pad_add_fusion.1.table_ref, bf16[3,2048,384]{2,1,0:T(8,128)(2,1)} %get-tuple-element.114.g_ref, bf16[9,256,1024]{2,1,0:T(8,128)(2,1)} %bitcast.126, bf16[9,256,1024]{2,1,0:T(8,128)(2,1)} %bitcast.7.refs_1_), custom_call_target="tpu_custom_call" | custom-call | flops 4831838208 | bytes 11796480 | tf_op jit(solution)/shard_map/pallas_call | solution.py:111
  473.9 16.7 %shard_map.415 = (bf16[9,256,1024]{2,1,0:T(8,128)(2,1)}, bf16[9,256,1024]{2,1,0:T(8,128)(2,1)}) custom-call(s32[54]{0:T(128)} %pad_add_fusion.1.table_ref, bf16[8,1056,384]{2,1,0:T(8,128)(2,1)} %bitcast.131, bf16[3,2048,384]{2,1,0:T(8,128)(2,1)} %get-tuple-element.114.g_ref), custom_call_target="tpu_custom_call" | custom-call | flops 4831838208 | bytes 14155776 | tf_op jit(solution)/shard_map/pallas_call | solution.py:168
  495.0 9.5 %collective-permute-start.25 = (bf16[384,1024]{1,0:T(8,128)(2,1)S(1)}, bf16[384,1024]{1,0:T(8,128)(2,1)S(1)}, u32[]{:S(2)}, u32[]{:S(2)}) collective-permute-start(bf16[384,1024]{1,0:T(8,128)(2,1)S(1)} %get-tuple-element.231), channel_id=1, source_target_pairs={{0,2},{8,5},{2,0},{10,3},{4,6},{12,1},{6,4},{14,7},{1,10},{9,13},{... | collective-permute-start | bytes 2359304 | tf_op jit(solution)/shard_map/ppermute | solution.py:826
  504.4 17.6 %collective-permute-done.24 = bf16[384,1024]{1,0:T(8,128)(2,1)S(1)} collective-permute-done((bf16[384,1024]{1,0:T(8,128)(2,1)S(1)}, bf16[384,1024]{1,0:T(8,128)(2,1)S(1)}, u32[]{:S(2)}, u32[]{:S(2)}) %collective-permute-start.24) | collective-permute-done | bytes 786464 | tf_op jit(solution)/shard_map/ppermute | solution.py:826
  538.5 13.6 %collective-permute-start.27 = (bf16[768,1024]{1,0:T(8,128)(2,1)}, bf16[768,1024]{1,0:T(8,128)(2,1)}, u32[]{:S(2)}, u32[]{:S(2)}) collective-permute-start(bf16[768,1024]{1,0:T(8,128)(2,1)} %bitcast.49), channel_id=1, source_target_pairs={{0,0},{8,1},{2,2},{10,3},{4,4},{12,5},{6,6},{14,7},{1,8},{9,9},{3,... | collective-permute-start | bytes 4718600 | tf_op jit(solution)/shard_map/ppermute | solution.py:835
  555.2 13.7 %collective-permute-done.30 = bf16[384,1024]{1,0:T(8,128)(2,1)} collective-permute-done((bf16[384,1024]{1,0:T(8,128)(2,1)}, bf16[384,1024]{1,0:T(8,128)(2,1)}, u32[]{:S(2)}, u32[]{:S(2)}) %collective-permute-start.30) | collective-permute-done | bytes 786464 | tf_op jit(solution)/shard_map/ppermute | solution.py:839
  571.5 9.5 %collective-permute-done.26 = bf16[768,1024]{1,0:T(8,128)(2,1)} collective-permute-done((bf16[768,1024]{1,0:T(8,128)(2,1)}, bf16[768,1024]{1,0:T(8,128)(2,1)}, u32[]{:S(2)}, u32[]{:S(2)}) %collective-permute-start.26) | collective-permute-done | bytes 1572896 | tf_op jit(solution)/shard_map/ppermute | solution.py:835
  605.4 13.7 %collective-permute-start.34 = (f32[15360]{0:T(1024)S(1)}, f32[15360]{0:T(1024)S(1)}, u32[]{:S(2)}, u32[]{:S(2)}) collective-permute-start(f32[15360]{0:T(1024)S(1)} %add.610), channel_id=1, source_target_pairs={{0,2},{1,3},{2,0},{3,1},{4,6},{5,7},{6,4},{7,5},{8,10},{9,11},{10,... | collective-permute-start | bytes 184328 | tf_op jit(solution)/shard_map/ppermute | solution.py:877
  (303 shorter events, 173.9 us)
Async XLA Ops:
  7.2 108.6 %all-gather.4.cloned.1.call-start = ((), (), s32[]{:S(2)}) async-start(), calls=%async_computation.1 | async-start | bytes 6893568 | tf_op jit(solution)/shard_map/all_gather | solution.py:716
  10.4 201.1 %all-gather.6.cloned.1.call-start = ((), (), s32[]{:S(2)}) async-start(), calls=%async_computation.2 | async-start | bytes 11280384 | tf_op jit(solution)/shard_map/all_gather | solution.py:754
  17.8 65.7 %collective-permute-start = (bf16[768,1024]{1,0:T(8,128)(2,1)}, bf16[768,1024]{1,0:T(8,128)(2,1)}, u32[]{:S(2)}, u32[]{:S(2)}) collective-permute-start(bf16[768,1024]{1,0:T(8,128)(2,1)} %add_convert_fusion.3), channel_id=1, source_target_pairs={{0,2},{1,10},{2,4},{3,12},{5,14},{8,3},{9,11},{10,5},{11,13},{13,1... | collective-permute-start | bytes 4718600 | tf_op jit(solution)/shard_map/ppermute | solution.py:749
  24.0 59.5 %collective-permute-start.1 = (bf16[768,1024]{1,0:T(8,128)(2,1)}, bf16[768,1024]{1,0:T(8,128)(2,1)}, u32[]{:S(2)}, u32[]{:S(2)}) collective-permute-start(bf16[768,1024]{1,0:T(8,128)(2,1)} %add_convert_fusion.3), channel_id=1, source_target_pairs={{0,0},{1,8},{2,2},{3,10},{4,4},{5,12},{6,6},{7,14},{8,1},{9,9},{10... | collective-permute-start | bytes 4718600 | tf_op jit(solution)/shard_map/ppermute | solution.py:749
  37.3 47.9 %collective-permute-start.2 = (bf16[768,1024]{1,0:T(8,128)(2,1)}, bf16[768,1024]{1,0:T(8,128)(2,1)}, u32[]{:S(2)}, u32[]{:S(2)}) collective-permute-start(bf16[768,1024]{1,0:T(8,128)(2,1)} %add_convert_fusion.3), channel_id=1, source_target_pairs={{2,0},{4,2},{5,10},{6,4},{7,12},{10,1},{12,3},{13,11},{14,5},{15,1... | collective-permute-start | bytes 4718600 | tf_op jit(solution)/shard_map/ppermute | solution.py:749
  90.3 494.4 %reduce-scatter.2.cloned.1.call-start = ((), (), s32[]{:S(2)}) async-start(), calls=%async_computation.3 | async-start | bytes 10027008 | tf_op jit(solution)/shard_map/reduce_scatter | solution.py:817
  115.4 61.7 %collective-permute-start.12 = (bf16[768,1024]{1,0:T(8,128)(2,1)S(1)}, bf16[768,1024]{1,0:T(8,128)(2,1)S(1)}, u32[]{:S(2)}, u32[]{:S(2)}) collective-permute-start(bf16[768,1024]{1,0:T(8,128)(2,1)S(1)} %copy-done.9), channel_id=1, source_target_pairs={{0,16},{8,24},{16,0},{24,8},{1,17},{9,25},{17,1},{25,9},{2,18},{10... | collective-permute-start | bytes 4718600 | tf_op jit(solution)/shard_map/ppermute | solution.py:756
  174.4 30.0 %collective-permute-start.4 = (bf16[3,3,256,128]{3,2,1,0:T(8,128)(2,1)S(1)}, bf16[3,3,256,128]{3,2,1,0:T(8,128)(2,1)S(1)}, u32[]{:S(2)}, u32[]{:S(2)}) collective-permute-start(bf16[3,3,256,128]{3,2,1,0:T(8,128)(2,1)S(1)} %bitcast.148), channel_id=1, source_target_pairs={{0,0},{8,1},{2,2},{10,3},{4,4},{12,5},{6,6},{14,7},{1,8},{9,9},{3,... | collective-permute-start | bytes 1769480 | tf_op jit(solution)/shard_map/ppermute | solution.py:640
  175.1 29.4 %collective-permute-start.5 = (bf16[3,3,256,128]{3,2,1,0:T(8,128)(2,1)S(1)}, bf16[3,3,256,128]{3,2,1,0:T(8,128)(2,1)S(1)}, u32[]{:S(2)}, u32[]{:S(2)}) collective-permute-start(bf16[3,3,256,128]{3,2,1,0:T(8,128)(2,1)S(1)} %bitcast.146), channel_id=1, source_target_pairs={{8,0},{2,1},{10,2},{4,3},{12,4},{6,5},{14,6},{9,8},{3,9},{11,10},{... | collective-permute-start | bytes 1769480 | tf_op jit(solution)/shard_map/ppermute | solution.py:640
  182.6 27.3 %collective-permute-start.7 = (bf16[3,3,256,128]{3,2,1,0:T(8,128)(2,1)S(1)}, bf16[3,3,256,128]{3,2,1,0:T(8,128)(2,1)S(1)}, u32[]{:S(2)}, u32[]{:S(2)}) collective-permute-start(bf16[3,3,256,128]{3,2,1,0:T(8,128)(2,1)S(1)} %bitcast.143), channel_id=1, source_target_pairs={{2,0},{4,2},{12,3},{14,5},{3,8},{5,10},{13,11},{15,13},{18,16},{20... | collective-permute-start | bytes 1769480 | tf_op jit(solution)/shard_map/ppermute | solution.py:640
  183.9 27.4 %collective-permute-start.8 = (bf16[3,3,256,128]{3,2,1,0:T(8,128)(2,1)S(1)}, bf16[3,3,256,128]{3,2,1,0:T(8,128)(2,1)S(1)}, u32[]{:S(2)}, u32[]{:S(2)}) collective-permute-start(bf16[3,3,256,128]{3,2,1,0:T(8,128)(2,1)S(1)} %bitcast.141), channel_id=1, source_target_pairs={{0,2},{2,4},{10,5},{12,7},{1,10},{3,12},{11,13},{13,15},{16,18},{1... | collective-permute-start | bytes 1769480 | tf_op jit(solution)/shard_map/ppermute | solution.py:640
  229.1 26.6 %collective-permute-start.11 = (bf16[384,1024]{1,0:T(8,128)(2,1)}, bf16[384,1024]{1,0:T(8,128)(2,1)}, u32[]{:S(2)}, u32[]{:S(2)}) collective-permute-start(bf16[384,1024]{1,0:T(8,128)(2,1)} %get-tuple-element.236), channel_id=1, source_target_pairs={{0,16},{8,24},{16,0},{24,8},{1,17},{9,25},{17,1},{25,9},{2,18},{10... | collective-permute-start | bytes 2359304 | tf_op jit(solution)/shard_map/ppermute | solution.py:777
  269.1 43.2 %collective-permute-start.13 = (bf16[384,1024]{1,0:T(8,128)(2,1)}, bf16[384,1024]{1,0:T(8,128)(2,1)S(1)}, u32[]{:S(2)}, u32[]{:S(2)}) collective-permute-start(bf16[384,1024]{1,0:T(8,128)(2,1)} %get-tuple-element.92), channel_id=1, source_target_pairs={{0,16},{8,24},{16,0},{24,8},{1,17},{9,25},{17,1},{25,9},{2,18},{10... | collective-permute-start | bytes 2359304 | tf_op jit(solution)/shard_map/ppermute | solution.py:790
  332.8 47.3 %collective-permute-start.36 = (bf16[8,1,2,32,1024]{4,3,2,0,1:T(8,128)(2,1)S(1)}, bf16[8,1,2,32,1024]{4,3,2,0,1:T(8,128)(2,1)S(1)}, u32[]{:S(2)}, u32[]{:S(2)}) collective-permute-start(bf16[8,1,2,32,1024]{4,3,2,0,1:T(8,128)(2,1)S(1)} %dynamic-slice_bitcast_fusion), channel_id=1, source_target_pairs={{0,16},{8,24},{16,0},{24,8},{1,17},{9,25},{17,1},{25,9},{2,18},{10... | collective-permute-start | bytes 3145736 | tf_op jit(solution)/shard_map/ppermute | solution.py:813
  336.3 125.0 %collective-permute-start.21 = (bf16[768,1024]{1,0:T(8,128)(2,1)S(1)}, bf16[768,1024]{1,0:T(8,128)(2,1)S(1)}, u32[]{:S(2)}, u32[]{:S(2)}) collective-permute-start(bf16[768,1024]{1,0:T(8,128)(2,1)S(1)} %pad_maximum_fusion.1), channel_id=1, source_target_pairs={{0,16},{8,24},{16,0},{24,8},{1,17},{9,25},{17,1},{25,9},{2,18},{10... | collective-permute-start | bytes 4718600 | tf_op jit(solution)/shard_map/ppermute | solution.py:795
  338.6 31.6 %collective-permute-start.18 = (bf16[3,3,256,128]{3,2,1,0:T(8,128)(2,1)S(1)}, bf16[3,3,256,128]{3,2,1,0:T(8,128)(2,1)S(1)}, u32[]{:S(2)}, u32[]{:S(2)}) collective-permute-start(bf16[3,3,256,128]{3,2,1,0:T(8,128)(2,1)S(1)} %bitcast.140), channel_id=1, source_target_pairs={{0,2},{2,4},{3,12},{5,14},{8,3},{10,5},{11,13},{13,15},{16,18},{18... | collective-permute-start | bytes 1769480 | tf_op jit(solution)/shard_map/ppermute | solution.py:640
  381.6 248.8 %all-gather.8.cloned.1.call-start = ((), (), s32[]{:S(2)}) async-start(), calls=%async_computation.4 | async-start | bytes 2949120 | tf_op jit(solution)/shard_map/all_gather | solution.py:888
  490.6 32.6 %collective-permute-start.22 = (bf16[9,256,1024]{2,1,0:T(8,128)(2,1)}, bf16[9,256,1024]{2,1,0:T(8,128)(2,1)S(1)}, u32[]{:S(2)}, u32[]{:S(2)}) collective-permute-start(bf16[9,256,1024]{2,1,0:T(8,128)(2,1)} %get-tuple-element.116), channel_id=1, source_target_pairs={{0,8},{8,0},{16,24},{24,16},{1,9},{9,1},{17,25},{25,17},{2,10},{10... | collective-permute-start | bytes 14155784 | tf_op jit(solution)/shard_map/ppermute | solution.py:830
  491.7 30.4 %collective-permute-start.24 = (bf16[384,1024]{1,0:T(8,128)(2,1)S(1)}, bf16[384,1024]{1,0:T(8,128)(2,1)S(1)}, u32[]{:S(2)}, u32[]{:S(2)}) collective-permute-start(bf16[384,1024]{1,0:T(8,128)(2,1)S(1)} %get-tuple-element.232), channel_id=1, source_target_pairs={{0,1},{8,4},{2,7},{10,2},{4,5},{12,0},{6,3},{14,6},{1,9},{9,12},{3... | collective-permute-start | bytes 2359304 | tf_op jit(solution)/shard_map/ppermute | solution.py:826
  495.0 28.3 %collective-permute-start.25 = (bf16[384,1024]{1,0:T(8,128)(2,1)S(1)}, bf16[384,1024]{1,0:T(8,128)(2,1)S(1)}, u32[]{:S(2)}, u32[]{:S(2)}) collective-permute-start(bf16[384,1024]{1,0:T(8,128)(2,1)S(1)} %get-tuple-element.231), channel_id=1, source_target_pairs={{0,2},{8,5},{2,0},{10,3},{4,6},{12,1},{6,4},{14,7},{1,10},{9,13},{... | collective-permute-start | bytes 2359304 | tf_op jit(solution)/shard_map/ppermute | solution.py:826
  523.7 28.4 %collective-permute-start.29 = (bf16[384,1024]{1,0:T(8,128)(2,1)S(1)}, bf16[384,1024]{1,0:T(8,128)(2,1)S(1)}, u32[]{:S(2)}, u32[]{:S(2)}) collective-permute-start(bf16[384,1024]{1,0:T(8,128)(2,1)S(1)} %add_convert_fusion.6), channel_id=1, source_target_pairs={{0,8},{8,0},{16,24},{24,16},{1,9},{9,1},{17,25},{25,17},{2,10},{10... | collective-permute-start | bytes 2359304 | tf_op jit(solution)/shard_map/ppermute | solution.py:839
  534.6 36.9 %collective-permute-start.28 = (bf16[768,1024]{1,0:T(8,128)(2,1)}, bf16[768,1024]{1,0:T(8,128)(2,1)}, u32[]{:S(2)}, u32[]{:S(2)}) collective-permute-start(bf16[768,1024]{1,0:T(8,128)(2,1)} %bitcast.50), channel_id=1, source_target_pairs={{0,2},{2,4},{10,5},{4,6},{12,7},{1,10},{3,12},{11,13},{5,14},{13,1... | collective-permute-start | bytes 4718600 | tf_op jit(solution)/shard_map/ppermute | solution.py:835
  537.2 43.8 %collective-permute-start.26 = (bf16[768,1024]{1,0:T(8,128)(2,1)}, bf16[768,1024]{1,0:T(8,128)(2,1)}, u32[]{:S(2)}, u32[]{:S(2)}) collective-permute-start(bf16[768,1024]{1,0:T(8,128)(2,1)} %bitcast.48), channel_id=1, source_target_pairs={{2,0},{10,1},{4,2},{12,3},{14,5},{3,8},{11,9},{5,10},{13,11},{15,1... | collective-permute-start | bytes 4718600 | tf_op jit(solution)/shard_map/ppermute | solution.py:835
  538.5 42.4 %collective-permute-start.27 = (bf16[768,1024]{1,0:T(8,128)(2,1)}, bf16[768,1024]{1,0:T(8,128)(2,1)}, u32[]{:S(2)}, u32[]{:S(2)}) collective-permute-start(bf16[768,1024]{1,0:T(8,128)(2,1)} %bitcast.49), channel_id=1, source_target_pairs={{0,0},{8,1},{2,2},{10,3},{4,4},{12,5},{6,6},{14,7},{1,8},{9,9},{3,... | collective-permute-start | bytes 4718600 | tf_op jit(solution)/shard_map/ppermute | solution.py:835
  (62 other events, 1006.6 us)
Sparse Core Ops, SparseCore 0:
  10.8 98.8 all-gather.3
  112.5 89.9 all-gather.5
  381.7 118.2 reduce-scatter.1
  584.8 37.8 all-gather.7

commit v5 on v4

--- a/solution.py
+++ b/solution.py
@@ -870,7 +870,7 @@
     )
     hops = [
         (axis, [(i, i ^ 1 << bit) for i in range(size)])
-        for axis, size in (("dp", copies), ("mp", shards))
+        for axis, size in (("mp", shards), ("dp", copies))
         for bit in range((size - 1).bit_length())
     ]
     for axis, pairs in hops:

time: 655 us -> 656 us (level)
  transfers between devices with their start and end apart: 41 -> 41, of which waited for: 13 -> 14; matrix products, arithmetic and copies ran while one was open for 11% -> 11% of each run, Pallas kernels for 37% -> 37%
where the time goes in v5:
time: 656 us; the launch traced here: 645 us
  Pallas kernels  255 us (39%)
  starting transfers between devices  141 us (21%)
  waiting for transfers between devices  112 us (17%)
  other arithmetic  59.4 us (9%)
  local copies, waits for them, and re-layouts  41.6 us (6%)
  between operations  23.6 us (4%)
  blocking collectives  11 us (2%)
    pallas_call x1, Pallas kernels, attend_back(): pl.pallas_call(functools.partial(attend_back_kernel, heads, block), grid_...  79.6 us
    ppermute x10, starting transfers between devices, exchange(): got.append(lax.ppermute(message, both, ends))  51.6 us
    pallas_call x3, Pallas kernels, feed(): pl.pallas_call(functools.partial(feed_kernel, parts), grid=(steps,), in_s...  50 us
    pallas_call x1, Pallas kernels, attend(): pl.pallas_call(functools.partial(attend_kernel, heads, block), grid_spec=...  41.6 us
    ppermute x3, waiting for transfers between devices, on_device(): lax.ppermute(normed_one, both, back(far(o)))  33.6 us
    ppermute x10, waiting for transfers between devices, exchange(): got.append(lax.ppermute(message, both, ends))  25.8 us
    pallas_call x1, Pallas kernels, feed_grads(): pl.pallas_call(feed_grads_kernel, grid=(steps,), in_specs=specs, out_spec...  23.3 us
    ppermute x3, starting transfers between devices, on_device(): lax.ppermute(normed_one, both, back(far(o)))  20.8 us
  transfers between devices with their start and end apart: 41, of which 14 were waited for; matrix products, arithmetic and copies ran while one was open for 11% of the time, Pallas kernels for 37%

profile of v5, /device:TPU:0, one launch (start us, length us, event | category | flops | bytes accessed | tf_op | source)
XLA Modules:
  0.0 644.8 jit_solution(1417359796696889310)
XLA Ops:
  24.0 13.3 %collective-permute-start.1 = (bf16[768,1024]{1,0:T(8,128)(2,1)}, bf16[768,1024]{1,0:T(8,128)(2,1)}, u32[]{:S(2)}, u32[]{:S(2)}) collective-permute-start(bf16[768,1024]{1,0:T(8,128)(2,1)} %add_convert_fusion.3), channel_id=1, source_target_pairs={{0,0},{1,8},{2,2},{3,10},{4,4},{5,12},{6,6},{7,14},{8,1},{9,9},{10... | collective-permute-start | bytes 4718600 | tf_op jit(solution)/shard_map/ppermute | solution.py:749
  51.5 32.0 %collective-permute-done = bf16[768,1024]{1,0:T(8,128)(2,1)} collective-permute-done((bf16[768,1024]{1,0:T(8,128)(2,1)}, bf16[768,1024]{1,0:T(8,128)(2,1)}, u32[]{:S(2)}, u32[]{:S(2)}) %collective-permute-start) | collective-permute-done | bytes 1572896 | tf_op jit(solution)/shard_map/ppermute | solution.py:749
  90.4 11.0 %psum.7 = f32[]{:T(128)} all-reduce(f32[]{:T(128)} %bitcast.6), channel_id=1, replica_groups=mesh['dp'=4,'mp'=8] {'dp'}, use_global_device_ids=true, to_apply=%region_5.6 | all-reduce | flops 1 | bytes 8 | tf_op jit(solution)/shard_map/psum | solution.py:753
  115.8 14.6 %shard_map.405.x_ref = bf16[3,2048,384]{2,1,0:T(8,128)(2,1)} custom-call(s32[54]{0:T(128)} %pad_add_fusion.1.table_ref, bf16[8,1056,384]{2,1,0:T(8,128)(2,1)} %bitcast.130, bf16[9,256,1024]{2,1,0:T(8,128)(2,1)} %bitcast.125, bf16[9,256,1024]{2,1,0:T(8,128)(2,1)} %bitcast.7.refs_1_), custom_call_target="tpu_custom_call" | custom-call | flops 4831838208 | bytes 14155776 | tf_op jit(solution)/shard_map/pallas_call | solution.py:85
  130.5 41.6 %shard_map.406 = (bf16[54,256,128]{2,1,0:T(8,128)(2,1)}, f32[3,2,2048]{2,1,0:T(2,128)}) custom-call(s32[24]{0:T(128)} %get-tuple-element.258.place_ref, bf16[3,2048,384]{2,1,0:T(8,128)(2,1)} %shard_map.405.x_ref), custom_call_target="tpu_custom_call" | custom-call | flops 25769803776 | bytes 7077888 | tf_op jit(solution)/shard_map/pallas_call | solution.py:219
  183.9 20.4 %collective-permute-start.8 = (bf16[3,3,256,128]{3,2,1,0:T(8,128)(2,1)S(1)}, bf16[3,3,256,128]{3,2,1,0:T(8,128)(2,1)S(1)}, u32[]{:S(2)}, u32[]{:S(2)}) collective-permute-start(bf16[3,3,256,128]{3,2,1,0:T(8,128)(2,1)S(1)} %bitcast.141), channel_id=1, source_target_pairs={{0,2},{2,4},{10,5},{12,7},{1,10},{3,12},{11,13},{13,15},{16,18},{1... | collective-permute-start | bytes 1769480 | tf_op jit(solution)/shard_map/ppermute | solution.py:640
  218.2 8.3 %shard_map.407 = (bf16[768,1024]{1,0:T(8,128)(2,1)}, f32[768,1024]{1,0:T(8,128)}, bf16[768,1024]{1,0:T(8,128)(2,1)}) custom-call(s32[24]{0:T(128)} %get-tuple-element.257.place_ref, bf16[54,256,128]{2,1,0:T(8,128)(2,1)} %bitcast.132, bf16[1024,1024]{1,0:T(8,128)(2,1)} %bitcast.121, f32[768,1024]{1,0:T(8,128)} %copy-done.1, f32[8,1024]{1,0:T(8,128)} %select_maximum_fusion.vec_ref), custom_call_target="tpu_custom_call" | custom-call | flops 1610612736 | bytes 15728640 | tf_op jit(solution)/shard_map/pallas_call | solution.py:455
  230.5 23.6 %shard_map.408 = (f32[768,1024]{1,0:T(8,128)}, f32[768,1024]{1,0:T(8,128)}, bf16[2,768,1024]{2,1,0:T(8,128)(2,1)}, bf16[2,768,1024]{2,1,0:T(8,128)(2,1)}, f32[2,1,1024]{2,1,0:T(1,128)}) custom-call(bf16[768,1024]{1,0:T(8,128)(2,1)} %get-tuple-element.87.x_ref.refs_0_, bf16[768,1024]{1,0:T(8,128)(2,1)} %multiply_convert_fusion.g_ref.refs_1_, ...), custom_call_target="tpu_custom_call" | custom-call | flops 12884901888 | bytes 32636928 | tf_op jit(solution)/shard_map/pallas_call | solution.py:375
  255.7 13.3 %shard_map.409 = (bf16[384,1024]{1,0:T(8,128)(2,1)}, bf16[384,1024]{1,0:T(8,128)(2,1)}, bf16[2,384,1024]{2,1,0:T(8,128)(2,1)}, bf16[2,384,1024]{2,1,0:T(8,128)(2,1)}, f32[2,1,1024]{2,1,0:T(1,128)}) custom-call(bf16[384,1024]{1,0:T(8,128)(2,1)} %collective-permute-done.11.x_ref.refs_4_, bf16[384,1024]{1,0:T(8,128)(2,1)} %get-tuple-element.235.g_ref.refs_5_, ...), custom_call_target="tpu_custom_call" | custom-call | flops 6442450944 | bytes 21626880 | tf_op jit(solution)/shard_map/pallas_call | solution.py:375
  274.7 13.1 %shard_map.410 = (bf16[384,1024]{1,0:T(8,128)(2,1)}, bf16[384,1024]{1,0:T(8,128)(2,1)}, bf16[2,384,1024]{2,1,0:T(8,128)(2,1)}, bf16[2,384,1024]{2,1,0:T(8,128)(2,1)}, f32[2,1,1024]{2,1,0:T(1,128)}) custom-call(bf16[384,1024]{1,0:T(8,128)(2,1)} %collective-permute-done.10.x_ref.refs_8_, bf16[384,1024]{1,0:T(8,128)(2,1)} %get-tuple-element.234.g_ref.refs_9_, ...), custom_call_target="tpu_custom_call" | custom-call | flops 6442450944 | bytes 21626880 | tf_op jit(solution)/shard_map/pallas_call | solution.py:375
  289.0 23.3 %shard_map.411 = bf16[8,2,288,1024]{3,2,1,0:T(8,128)(2,1)} custom-call(bf16[768,1024]{1,0:T(8,128)(2,1)} %get-tuple-element.87.x_ref.refs_0_, bf16[768,1024]{1,0:T(8,128)(2,1)} %multiply_convert_fusion.g_ref.refs_1_, bf16[2,768,1024]{2,1,0:T(8,128)(2,1)} %get-tuple-element.99.refs_2_, bf16[2,768,1024]{2,1,0:T(8,128)(2,1)} %get-tuple-element.100.refs_3_, ...), custom_call_target="tpu_custom_call" | custom-call | flops 12884901888 | bytes 20971520 | tf_op jit(solution)/shard_map/pallas_call | solution.py:428
  321.5 8.1 %shard_map.412 = bf16[18,768,128]{2,1,0:T(8,128)(2,1)} custom-call(s32[18]{0:T(128)} %and_select_fusion.5.shard_ref, bf16[768,1024]{1,0:T(8,128)(2,1)} %copy-done.8, bf16[1024,1024]{1,0:T(8,128)(2,1)} %bitcast.122), custom_call_target="tpu_custom_call" | custom-call | flops 1610612736 | bytes 6291456 | tf_op jit(solution)/shard_map/pallas_call | solution.py:491
  338.6 18.8 %collective-permute-start.18 = (bf16[3,3,256,128]{3,2,1,0:T(8,128)(2,1)S(1)}, bf16[3,3,256,128]{3,2,1,0:T(8,128)(2,1)S(1)}, u32[]{:S(2)}, u32[]{:S(2)}) collective-permute-start(bf16[3,3,256,128]{3,2,1,0:T(8,128)(2,1)S(1)} %bitcast.140), channel_id=1, source_target_pairs={{0,2},{2,4},{3,12},{5,14},{8,3},{10,5},{11,13},{13,15},{16,18},{18... | collective-permute-start | bytes 1769480 | tf_op jit(solution)/shard_map/ppermute | solution.py:640
  358.9 11.3 %collective-permute-done.18 = bf16[3,3,256,128]{3,2,1,0:T(8,128)(2,1)S(1)} collective-permute-done((bf16[3,3,256,128]{3,2,1,0:T(8,128)(2,1)S(1)}, bf16[3,3,256,128]{3,2,1,0:T(8,128)(2,1)S(1)}, u32[]{:S(2)}, u32[]{:S(2)}) %collective-permute-start.18) | collective-permute-done | bytes 589856 | tf_op jit(solution)/shard_map/ppermute | solution.py:640
  370.2 8.0 %collective-permute-done.19 = bf16[3,3,256,128]{3,2,1,0:T(8,128)(2,1)S(1)} collective-permute-done((bf16[3,3,256,128]{3,2,1,0:T(8,128)(2,1)S(1)}, bf16[3,3,256,128]{3,2,1,0:T(8,128)(2,1)S(1)}, u32[]{:S(2)}, u32[]{:S(2)}) %collective-permute-start.19) | collective-permute-done | bytes 589856 | tf_op jit(solution)/shard_map/ppermute | solution.py:640
  381.6 79.6 %shard_map.413 = (bf16[3,2048,384]{2,1,0:T(8,128)(2,1)}, f32[3,1,384]{2,1,0:T(1,128)}) custom-call(s32[24]{0:T(128)} %get-tuple-element.258.place_ref, bf16[3,2048,384]{2,1,0:T(8,128)(2,1)} %shard_map.405.x_ref, bf16[54,256,128]{2,1,0:T(8,128)(2,1)} %get-tuple-element.84.ctx_ref, bf16[54,256,128]{2,1,0:T(8,128)(2,1)} %bitcast.151, ...), custom_call_target="tpu_custom_call" | custom-call | flops 64424509440 | bytes 11796480 | tf_op jit(solution)/shard_map/pallas_call | solution.py:291
  461.3 12.6 %shard_map.414 = bf16[3,384,1024]{2,1,0:T(8,128)(2,1)} custom-call(s32[54]{0:T(128)} %pad_add_fusion.1.table_ref, bf16[3,2048,384]{2,1,0:T(8,128)(2,1)} %get-tuple-element.114.g_ref, bf16[9,256,1024]{2,1,0:T(8,128)(2,1)} %bitcast.126, bf16[9,256,1024]{2,1,0:T(8,128)(2,1)} %bitcast.7.refs_1_), custom_call_target="tpu_custom_call" | custom-call | flops 4831838208 | bytes 11796480 | tf_op jit(solution)/shard_map/pallas_call | solution.py:111
  473.9 16.7 %shard_map.415 = (bf16[9,256,1024]{2,1,0:T(8,128)(2,1)}, bf16[9,256,1024]{2,1,0:T(8,128)(2,1)}) custom-call(s32[54]{0:T(128)} %pad_add_fusion.1.table_ref, bf16[8,1056,384]{2,1,0:T(8,128)(2,1)} %bitcast.131, bf16[3,2048,384]{2,1,0:T(8,128)(2,1)} %get-tuple-element.114.g_ref), custom_call_target="tpu_custom_call" | custom-call | flops 4831838208 | bytes 14155776 | tf_op jit(solution)/shard_map/pallas_call | solution.py:168
  495.0 9.5 %collective-permute-start.25 = (bf16[384,1024]{1,0:T(8,128)(2,1)S(1)}, bf16[384,1024]{1,0:T(8,128)(2,1)S(1)}, u32[]{:S(2)}, u32[]{:S(2)}) collective-permute-start(bf16[384,1024]{1,0:T(8,128)(2,1)S(1)} %get-tuple-element.231), channel_id=1, source_target_pairs={{0,2},{8,5},{2,0},{10,3},{4,6},{12,1},{6,4},{14,7},{1,10},{9,13},{... | collective-permute-start | bytes 2359304 | tf_op jit(solution)/shard_map/ppermute | solution.py:826
  504.4 17.6 %collective-permute-done.24 = bf16[384,1024]{1,0:T(8,128)(2,1)S(1)} collective-permute-done((bf16[384,1024]{1,0:T(8,128)(2,1)S(1)}, bf16[384,1024]{1,0:T(8,128)(2,1)S(1)}, u32[]{:S(2)}, u32[]{:S(2)}) %collective-permute-start.24) | collective-permute-done | bytes 786464 | tf_op jit(solution)/shard_map/ppermute | solution.py:826
  538.5 13.6 %collective-permute-start.27 = (bf16[768,1024]{1,0:T(8,128)(2,1)}, bf16[768,1024]{1,0:T(8,128)(2,1)}, u32[]{:S(2)}, u32[]{:S(2)}) collective-permute-start(bf16[768,1024]{1,0:T(8,128)(2,1)} %bitcast.49), channel_id=1, source_target_pairs={{0,0},{8,1},{2,2},{10,3},{4,4},{12,5},{6,6},{14,7},{1,8},{9,9},{3,... | collective-permute-start | bytes 4718600 | tf_op jit(solution)/shard_map/ppermute | solution.py:835
  555.2 13.7 %collective-permute-done.30 = bf16[384,1024]{1,0:T(8,128)(2,1)} collective-permute-done((bf16[384,1024]{1,0:T(8,128)(2,1)}, bf16[384,1024]{1,0:T(8,128)(2,1)}, u32[]{:S(2)}, u32[]{:S(2)}) %collective-permute-start.30) | collective-permute-done | bytes 786464 | tf_op jit(solution)/shard_map/ppermute | solution.py:839
  571.5 9.5 %collective-permute-done.26 = bf16[768,1024]{1,0:T(8,128)(2,1)} collective-permute-done((bf16[768,1024]{1,0:T(8,128)(2,1)}, bf16[768,1024]{1,0:T(8,128)(2,1)}, u32[]{:S(2)}, u32[]{:S(2)}) %collective-permute-start.26) | collective-permute-done | bytes 1572896 | tf_op jit(solution)/shard_map/ppermute | solution.py:835
  596.3 11.7 %collective-permute-start.32 = (f32[15360]{0:T(1024)S(1)}, f32[15360]{0:T(1024)S(1)}, u32[]{:S(2)}, u32[]{:S(2)}) collective-permute-start(f32[15360]{0:T(1024)S(1)} %add.608), channel_id=1, source_target_pairs={{0,2},{1,3},{2,0},{3,1},{4,6},{5,7},{6,4},{7,5},{8,10},{9,11},{10,... | collective-permute-start | bytes 184328 | tf_op jit(solution)/shard_map/ppermute | solution.py:877
  (303 shorter events, 176.2 us)
Async XLA Ops:
  7.2 108.6 %all-gather.4.cloned.1.call-start = ((), (), s32[]{:S(2)}) async-start(), calls=%async_computation.1 | async-start | bytes 6893568 | tf_op jit(solution)/shard_map/all_gather | solution.py:716
  10.4 201.1 %all-gather.6.cloned.1.call-start = ((), (), s32[]{:S(2)}) async-start(), calls=%async_computation.2 | async-start | bytes 11280384 | tf_op jit(solution)/shard_map/all_gather | solution.py:754
  17.8 65.7 %collective-permute-start = (bf16[768,1024]{1,0:T(8,128)(2,1)}, bf16[768,1024]{1,0:T(8,128)(2,1)}, u32[]{:S(2)}, u32[]{:S(2)}) collective-permute-start(bf16[768,1024]{1,0:T(8,128)(2,1)} %add_convert_fusion.3), channel_id=1, source_target_pairs={{0,2},{1,10},{2,4},{3,12},{5,14},{8,3},{9,11},{10,5},{11,13},{13,1... | collective-permute-start | bytes 4718600 | tf_op jit(solution)/shard_map/ppermute | solution.py:749
  24.0 59.5 %collective-permute-start.1 = (bf16[768,1024]{1,0:T(8,128)(2,1)}, bf16[768,1024]{1,0:T(8,128)(2,1)}, u32[]{:S(2)}, u32[]{:S(2)}) collective-permute-start(bf16[768,1024]{1,0:T(8,128)(2,1)} %add_convert_fusion.3), channel_id=1, source_target_pairs={{0,0},{1,8},{2,2},{3,10},{4,4},{5,12},{6,6},{7,14},{8,1},{9,9},{10... | collective-permute-start | bytes 4718600 | tf_op jit(solution)/shard_map/ppermute | solution.py:749
  37.3 47.9 %collective-permute-start.2 = (bf16[768,1024]{1,0:T(8,128)(2,1)}, bf16[768,1024]{1,0:T(8,128)(2,1)}, u32[]{:S(2)}, u32[]{:S(2)}) collective-permute-start(bf16[768,1024]{1,0:T(8,128)(2,1)} %add_convert_fusion.3), channel_id=1, source_target_pairs={{2,0},{4,2},{5,10},{6,4},{7,12},{10,1},{12,3},{13,11},{14,5},{15,1... | collective-permute-start | bytes 4718600 | tf_op jit(solution)/shard_map/ppermute | solution.py:749
  90.3 494.4 %reduce-scatter.2.cloned.1.call-start = ((), (), s32[]{:S(2)}) async-start(), calls=%async_computation.3 | async-start | bytes 10027008 | tf_op jit(solution)/shard_map/reduce_scatter | solution.py:817
  115.4 61.7 %collective-permute-start.12 = (bf16[768,1024]{1,0:T(8,128)(2,1)S(1)}, bf16[768,1024]{1,0:T(8,128)(2,1)S(1)}, u32[]{:S(2)}, u32[]{:S(2)}) collective-permute-start(bf16[768,1024]{1,0:T(8,128)(2,1)S(1)} %copy-done.9), channel_id=1, source_target_pairs={{0,16},{8,24},{16,0},{24,8},{1,17},{9,25},{17,1},{25,9},{2,18},{10... | collective-permute-start | bytes 4718600 | tf_op jit(solution)/shard_map/ppermute | solution.py:756
  174.4 30.0 %collective-permute-start.4 = (bf16[3,3,256,128]{3,2,1,0:T(8,128)(2,1)S(1)}, bf16[3,3,256,128]{3,2,1,0:T(8,128)(2,1)S(1)}, u32[]{:S(2)}, u32[]{:S(2)}) collective-permute-start(bf16[3,3,256,128]{3,2,1,0:T(8,128)(2,1)S(1)} %bitcast.148), channel_id=1, source_target_pairs={{0,0},{8,1},{2,2},{10,3},{4,4},{12,5},{6,6},{14,7},{1,8},{9,9},{3,... | collective-permute-start | bytes 1769480 | tf_op jit(solution)/shard_map/ppermute | solution.py:640
  175.1 29.4 %collective-permute-start.5 = (bf16[3,3,256,128]{3,2,1,0:T(8,128)(2,1)S(1)}, bf16[3,3,256,128]{3,2,1,0:T(8,128)(2,1)S(1)}, u32[]{:S(2)}, u32[]{:S(2)}) collective-permute-start(bf16[3,3,256,128]{3,2,1,0:T(8,128)(2,1)S(1)} %bitcast.146), channel_id=1, source_target_pairs={{8,0},{2,1},{10,2},{4,3},{12,4},{6,5},{14,6},{9,8},{3,9},{11,10},{... | collective-permute-start | bytes 1769480 | tf_op jit(solution)/shard_map/ppermute | solution.py:640
  182.6 27.3 %collective-permute-start.7 = (bf16[3,3,256,128]{3,2,1,0:T(8,128)(2,1)S(1)}, bf16[3,3,256,128]{3,2,1,0:T(8,128)(2,1)S(1)}, u32[]{:S(2)}, u32[]{:S(2)}) collective-permute-start(bf16[3,3,256,128]{3,2,1,0:T(8,128)(2,1)S(1)} %bitcast.143), channel_id=1, source_target_pairs={{2,0},{4,2},{12,3},{14,5},{3,8},{5,10},{13,11},{15,13},{18,16},{20... | collective-permute-start | bytes 1769480 | tf_op jit(solution)/shard_map/ppermute | solution.py:640
  183.9 27.4 %collective-permute-start.8 = (bf16[3,3,256,128]{3,2,1,0:T(8,128)(2,1)S(1)}, bf16[3,3,256,128]{3,2,1,0:T(8,128)(2,1)S(1)}, u32[]{:S(2)}, u32[]{:S(2)}) collective-permute-start(bf16[3,3,256,128]{3,2,1,0:T(8,128)(2,1)S(1)} %bitcast.141), channel_id=1, source_target_pairs={{0,2},{2,4},{10,5},{12,7},{1,10},{3,12},{11,13},{13,15},{16,18},{1... | collective-permute-start | bytes 1769480 | tf_op jit(solution)/shard_map/ppermute | solution.py:640
  229.1 26.6 %collective-permute-start.11 = (bf16[384,1024]{1,0:T(8,128)(2,1)}, bf16[384,1024]{1,0:T(8,128)(2,1)}, u32[]{:S(2)}, u32[]{:S(2)}) collective-permute-start(bf16[384,1024]{1,0:T(8,128)(2,1)} %get-tuple-element.236), channel_id=1, source_target_pairs={{0,16},{8,24},{16,0},{24,8},{1,17},{9,25},{17,1},{25,9},{2,18},{10... | collective-permute-start | bytes 2359304 | tf_op jit(solution)/shard_map/ppermute | solution.py:777
  269.1 43.2 %collective-permute-start.13 = (bf16[384,1024]{1,0:T(8,128)(2,1)}, bf16[384,1024]{1,0:T(8,128)(2,1)S(1)}, u32[]{:S(2)}, u32[]{:S(2)}) collective-permute-start(bf16[384,1024]{1,0:T(8,128)(2,1)} %get-tuple-element.92), channel_id=1, source_target_pairs={{0,16},{8,24},{16,0},{24,8},{1,17},{9,25},{17,1},{25,9},{2,18},{10... | collective-permute-start | bytes 2359304 | tf_op jit(solution)/shard_map/ppermute | solution.py:790
  332.8 47.3 %collective-permute-start.36 = (bf16[8,1,2,32,1024]{4,3,2,0,1:T(8,128)(2,1)S(1)}, bf16[8,1,2,32,1024]{4,3,2,0,1:T(8,128)(2,1)S(1)}, u32[]{:S(2)}, u32[]{:S(2)}) collective-permute-start(bf16[8,1,2,32,1024]{4,3,2,0,1:T(8,128)(2,1)S(1)} %dynamic-slice_bitcast_fusion), channel_id=1, source_target_pairs={{0,16},{8,24},{16,0},{24,8},{1,17},{9,25},{17,1},{25,9},{2,18},{10... | collective-permute-start | bytes 3145736 | tf_op jit(solution)/shard_map/ppermute | solution.py:813
  336.3 125.0 %collective-permute-start.21 = (bf16[768,1024]{1,0:T(8,128)(2,1)S(1)}, bf16[768,1024]{1,0:T(8,128)(2,1)S(1)}, u32[]{:S(2)}, u32[]{:S(2)}) collective-permute-start(bf16[768,1024]{1,0:T(8,128)(2,1)S(1)} %pad_maximum_fusion.1), channel_id=1, source_target_pairs={{0,16},{8,24},{16,0},{24,8},{1,17},{9,25},{17,1},{25,9},{2,18},{10... | collective-permute-start | bytes 4718600 | tf_op jit(solution)/shard_map/ppermute | solution.py:795
  338.6 31.6 %collective-permute-start.18 = (bf16[3,3,256,128]{3,2,1,0:T(8,128)(2,1)S(1)}, bf16[3,3,256,128]{3,2,1,0:T(8,128)(2,1)S(1)}, u32[]{:S(2)}, u32[]{:S(2)}) collective-permute-start(bf16[3,3,256,128]{3,2,1,0:T(8,128)(2,1)S(1)} %bitcast.140), channel_id=1, source_target_pairs={{0,2},{2,4},{3,12},{5,14},{8,3},{10,5},{11,13},{13,15},{16,18},{18... | collective-permute-start | bytes 1769480 | tf_op jit(solution)/shard_map/ppermute | solution.py:640
  381.6 249.1 %all-gather.8.cloned.1.call-start = ((), (), s32[]{:S(2)}) async-start(), calls=%async_computation.4 | async-start | bytes 2949120 | tf_op jit(solution)/shard_map/all_gather | solution.py:888
  490.6 32.6 %collective-permute-start.22 = (bf16[9,256,1024]{2,1,0:T(8,128)(2,1)}, bf16[9,256,1024]{2,1,0:T(8,128)(2,1)S(1)}, u32[]{:S(2)}, u32[]{:S(2)}) collective-permute-start(bf16[9,256,1024]{2,1,0:T(8,128)(2,1)} %get-tuple-element.116), channel_id=1, source_target_pairs={{0,8},{8,0},{16,24},{24,16},{1,9},{9,1},{17,25},{25,17},{2,10},{10... | collective-permute-start | bytes 14155784 | tf_op jit(solution)/shard_map/ppermute | solution.py:830
  491.7 30.4 %collective-permute-start.24 = (bf16[384,1024]{1,0:T(8,128)(2,1)S(1)}, bf16[384,1024]{1,0:T(8,128)(2,1)S(1)}, u32[]{:S(2)}, u32[]{:S(2)}) collective-permute-start(bf16[384,1024]{1,0:T(8,128)(2,1)S(1)} %get-tuple-element.232), channel_id=1, source_target_pairs={{0,1},{8,4},{2,7},{10,2},{4,5},{12,0},{6,3},{14,6},{1,9},{9,12},{3... | collective-permute-start | bytes 2359304 | tf_op jit(solution)/shard_map/ppermute | solution.py:826
  495.0 28.3 %collective-permute-start.25 = (bf16[384,1024]{1,0:T(8,128)(2,1)S(1)}, bf16[384,1024]{1,0:T(8,128)(2,1)S(1)}, u32[]{:S(2)}, u32[]{:S(2)}) collective-permute-start(bf16[384,1024]{1,0:T(8,128)(2,1)S(1)} %get-tuple-element.231), channel_id=1, source_target_pairs={{0,2},{8,5},{2,0},{10,3},{4,6},{12,1},{6,4},{14,7},{1,10},{9,13},{... | collective-permute-start | bytes 2359304 | tf_op jit(solution)/shard_map/ppermute | solution.py:826
  523.7 28.4 %collective-permute-start.29 = (bf16[384,1024]{1,0:T(8,128)(2,1)S(1)}, bf16[384,1024]{1,0:T(8,128)(2,1)S(1)}, u32[]{:S(2)}, u32[]{:S(2)}) collective-permute-start(bf16[384,1024]{1,0:T(8,128)(2,1)S(1)} %add_convert_fusion.6), channel_id=1, source_target_pairs={{0,8},{8,0},{16,24},{24,16},{1,9},{9,1},{17,25},{25,17},{2,10},{10... | collective-permute-start | bytes 2359304 | tf_op jit(solution)/shard_map/ppermute | solution.py:839
  534.6 36.9 %collective-permute-start.28 = (bf16[768,1024]{1,0:T(8,128)(2,1)}, bf16[768,1024]{1,0:T(8,128)(2,1)}, u32[]{:S(2)}, u32[]{:S(2)}) collective-permute-start(bf16[768,1024]{1,0:T(8,128)(2,1)} %bitcast.50), channel_id=1, source_target_pairs={{0,2},{2,4},{10,5},{4,6},{12,7},{1,10},{3,12},{11,13},{5,14},{13,1... | collective-permute-start | bytes 4718600 | tf_op jit(solution)/shard_map/ppermute | solution.py:835
  537.2 43.8 %collective-permute-start.26 = (bf16[768,1024]{1,0:T(8,128)(2,1)}, bf16[768,1024]{1,0:T(8,128)(2,1)}, u32[]{:S(2)}, u32[]{:S(2)}) collective-permute-start(bf16[768,1024]{1,0:T(8,128)(2,1)} %bitcast.48), channel_id=1, source_target_pairs={{2,0},{10,1},{4,2},{12,3},{14,5},{3,8},{11,9},{5,10},{13,11},{15,1... | collective-permute-start | bytes 4718600 | tf_op jit(solution)/shard_map/ppermute | solution.py:835
  538.5 42.4 %collective-permute-start.27 = (bf16[768,1024]{1,0:T(8,128)(2,1)}, bf16[768,1024]{1,0:T(8,128)(2,1)}, u32[]{:S(2)}, u32[]{:S(2)}) collective-permute-start(bf16[768,1024]{1,0:T(8,128)(2,1)} %bitcast.49), channel_id=1, source_target_pairs={{0,0},{8,1},{2,2},{10,3},{4,4},{12,5},{6,6},{14,7},{1,8},{9,9},{3,... | collective-permute-start | bytes 4718600 | tf_op jit(solution)/shard_map/ppermute | solution.py:835
  (62 other events, 1009.1 us)
Sparse Core Ops, SparseCore 0:
  10.8 98.8 all-gather.3
  112.5 89.9 all-gather.5
  381.7 118.2 reduce-scatter.1
  584.8 37.8 all-gather.7
